TPU v7x, 128 devices: a whole 4x4x4 slice. The times are simulated.
128 devices in a mesh: span: 32 (over z, x, core), chan: 4 (over y).
Axes of the slice: x: 4, y: 4, z: 4, core: 2. Of those that a mesh axis runs over, the one named last changes fastest.
Arguments:
- noise: bfloat16 [3, 160, 2048, 512], P(None, 'chan', 'span'), may hold values from -6 to 6
- widths: int32 [512], replicated, may hold values from 0 to 3
- rms_profile: float32 [3, 512], replicated, may hold values from 0.3 to 1.5
- tile_owner: int32 [1024, 1], P('span'), may hold values from 0 to 31; in each aligned block of 32 rows (0 to 31, 32 to 63, ...) at most 2 rows name the same one
Outputs:
- inlet: float32 [32, 32, 2, 32, 3, 16, 64], P('span', None, None, 'chan')
Inputs may be any that keep to these rules, and one draw needn't show every extreme that they name: `tile_owner`: among the 32 tiles of one vertical slab (an aligned block), no owner is named more than 2 times, and exactly 2 times in some block.
All inputs are finite; a program needn't handle non-finite values.
Results may differ from a plain program's by a relative error of at most 0.0027.
Values may be sent and summed in bfloat16 or wider, within the bound.
No kernel may reach another device: no remote copies, remote signals or barrier semaphores. Data moves between devices by JAX's collectives and lax.ppermute only.
A program may use at most 128 MiB of HBM per device.

v0:
```python
import functools
import math

import jax
import jax.numpy as jnp
import ml_dtypes
import numpy as np
from jax import lax
from jax.experimental import pallas as pl
from jax.experimental.pallas import tpu as pltpu
from jax.sharding import PartitionSpec as P

Y = 2048
Z = 512
KT = 128
KY = 96
KZ = 48
NW = 4
TY = 64
COMPS = 3
STEPS = 8
PLANES = 40
CHANS = 4
SPANS = 32
CAP = 2
ZD = Z // SPANS
ROWS = 16
GROUP = 4
LANES = GROUP * TY
VMEM_LIMIT = 56 * 1024 * 1024

PAIR_A = [(0, 1), (1, 0), (2, 3), (3, 2)]
PAIR_B = [(1, 2), (2, 1), (3, 0), (0, 3)]


def gaussian(offset, length_scale):
    return np.exp(-math.pi * offset * offset / (2.0 * length_scale * length_scale))


def time_taps():
    offset = np.arange(CHANS * PLANES)[None, :] - np.arange(CHANS * STEPS)[:, None]
    norm = np.sqrt(np.sum(gaussian(np.arange(KT) - KT // 2.0, KT / 4.0) ** 2))
    inside = (offset >= 0) & (offset < KT)
    return np.where(inside, gaussian(offset - KT // 2.0, KT / 4.0) / norm, 0.0)


def time_blocks():
    taps = time_taps().astype(np.float32).reshape(CHANS, STEPS, CHANS, PLANES)
    half = STEPS // 2
    blocks = []
    for d in range(CHANS):
        a, b, far = d ^ 1, CHANS - 1 - d, (d + 2) % CHANS
        first, second = slice(0, half), slice(half, STEPS)
        order = [(a, first), (far, first), (b, second), (far, second), (b, first), (a, second), (d, first), (d, second)]
        rows = np.concatenate([taps[block, steps, d] for block, steps in order])
        blocks.append(np.kron(rows, np.eye(ROWS, dtype=np.float32)))
    return np.stack(blocks).astype(ml_dtypes.bfloat16)


def split(values):
    high = values.astype(ml_dtypes.bfloat16)
    return high, (values - high.astype(np.float32)).astype(ml_dtypes.bfloat16)


def span_blocks():
    taps = gaussian(np.arange(KY) - KY // 2.0, KY / 4.0)
    taps = taps / np.sqrt(np.sum(taps**2))
    parts = []
    for shift in (-1, 0, 1):
        tap = np.arange(TY)[:, None] + TY * shift - np.arange(TY)[None, :] + KY // 2
        inside = (tap >= 0) & (tap < KY)
        band = np.where(inside, taps[np.clip(tap, 0, KY - 1)], 0.0).astype(np.float32)
        parts.append(np.kron(np.eye(GROUP, dtype=np.float32), band))
    return np.stack([np.stack(pair) for pair in zip(*[split(p) for p in parts])])


def vertical_filter_matrix(widths):
    def device_gaussian(offset, length_scale):
        offset_f = offset.astype(jnp.float32)
        return jnp.exp(-math.pi * offset_f * offset_f / (2.0 * length_scale * length_scale))

    offset = jnp.arange(Z)[None, :] - jnp.arange(Z)[:, None]
    length_scale = (KZ * (widths + 1)).astype(jnp.float32) / (4.0 * NW)
    tap_offsets = jnp.arange(KZ) - KZ // 2
    tap_norm = jnp.sqrt(
        jnp.sum(device_gaussian(tap_offsets[None, :], length_scale[:, None]) ** 2, axis=1)
    )
    inside = (offset >= -(KZ // 2)) & (offset < KZ - KZ // 2)
    return jnp.where(
        inside, device_gaussian(offset, length_scale[:, None]) / tap_norm[:, None], 0.0
    )


def time_kernel(chan_ref, taps_ref, noise_ref, to_a_ref, to_b_ref, kept_ref, own_ref):
    planes = noise_ref[...].reshape(PLANES * ROWS, Z)
    sums = jnp.dot(taps_ref[0], planes, preferred_element_type=jnp.float32)
    sums = sums.reshape(CHANS * STEPS, 1, ROWS, Z)
    to_a_ref[...] = sums[:8].astype(jnp.bfloat16)
    to_b_ref[...] = sums[8:16].astype(jnp.bfloat16)
    kept_ref[...] = sums[16:24]
    own_ref[...] = sums[24:]


def time_filter(noise, chan):
    part = pl.BlockSpec((STEPS, 1, ROWS, Z), lambda c, j, chan: (0, c, j, 0))
    shape = (STEPS, COMPS, TY, Z)
    return pl.pallas_call(
        time_kernel,
        grid_spec=pltpu.PrefetchScalarGridSpec(
            num_scalar_prefetch=1,
            grid=(COMPS, TY // ROWS),
            in_specs=[
                pl.BlockSpec((1, CHANS * STEPS * ROWS, PLANES * ROWS), lambda c, j, chan: (chan[0], 0, 0)),
                pl.BlockSpec((1, PLANES, ROWS, Z), lambda c, j, chan: (c, 0, j, 0)),
            ],
            out_specs=[part] * 4,
        ),
        out_shape=[
            jax.ShapeDtypeStruct(shape, jnp.bfloat16),
            jax.ShapeDtypeStruct(shape, jnp.bfloat16),
            jax.ShapeDtypeStruct(shape, jnp.float32),
            jax.ShapeDtypeStruct(shape, jnp.float32),
        ],
        compiler_params=pltpu.CompilerParams(vmem_limit_bytes=VMEM_LIMIT),
        name="time_filter",
    )(chan, time_blocks(), noise)


def vertical_kernel(high_ref, low_ref, own_ref, a_ref, b_ref, from_b_ref, from_a_ref, out_ref):
    half = STEPS // 2
    first = own_ref[:half] + a_ref[...].astype(jnp.float32) + from_b_ref[...].astype(jnp.float32)
    second = own_ref[half:] + b_ref[...].astype(jnp.float32) + from_a_ref[...].astype(jnp.float32)
    timed = jnp.concatenate([first, second]).reshape(STEPS * TY, Z)
    timed_high = timed.astype(jnp.bfloat16)
    timed_low = (timed - timed_high.astype(jnp.float32)).astype(jnp.bfloat16)

    def product(taps, values):
        return lax.dot_general(taps, values, (((1,), (1,)), ((), ())), preferred_element_type=jnp.float32)

    total = product(high_ref[...], timed_low) + product(low_ref[...], timed_high)
    total = total + product(high_ref[...], timed_high)
    out_ref[...] = total.astype(jnp.bfloat16)


def vertical_filter(taps_high, taps_low, own, from_a, from_b, second_b, second_a):
    half = pl.BlockSpec((STEPS // 2, 1, TY, Z), lambda c: (0, c, 0, 0))
    whole = pl.BlockSpec((Z, Z), lambda c: (0, 0))
    return pl.pallas_call(
        vertical_kernel,
        grid=(COMPS,),
        in_specs=[whole, whole, pl.BlockSpec((STEPS, 1, TY, Z), lambda c: (0, c, 0, 0)), half, half, half, half],
        out_specs=pl.BlockSpec((Z, STEPS * TY), lambda c: (0, c)),
        out_shape=jax.ShapeDtypeStruct((Z, COMPS * STEPS * TY), jnp.bfloat16),
        compiler_params=pltpu.CompilerParams(vmem_limit_bytes=VMEM_LIMIT),
        name="vertical_filter",
    )(taps_high, taps_low, own, from_a, from_b, second_b, second_a)


def span_kernel(owner_ref, taps_ref, rms_ref, x_ref, out_ref, count_ref, place_ref):
    def clear(o, carry):
        count_ref[o] = 0
        return carry

    lax.fori_loop(0, SPANS, clear, 0)

    def place(i, carry):
        owner = owner_ref[i]
        slot = count_ref[owner]
        count_ref[owner] = slot + 1
        place_ref[i] = owner * CAP + slot
        return carry

    lax.fori_loop(0, SPANS, place, 0)
    out_ref[...] = jnp.zeros_like(out_ref)
    for chunk in range(COMPS * STEPS // GROUP):
        lanes = pl.ds(chunk * LANES, LANES)
        x = x_ref[:, :, lanes]
        around = jnp.concatenate([x[SPANS - 1 :], x, x[:1]], axis=0).reshape((SPANS + 2) * ZD, LANES)
        total = None
        for part in (1, 0):
            for shift in range(3):
                rows = around[shift * ZD : (shift + SPANS) * ZD]
                term = jnp.dot(rows, taps_ref[part, shift], preferred_element_type=jnp.float32)
                total = term if total is None else total + term
        c = chunk * GROUP // STEPS
        velocity = total.reshape(SPANS, ZD, LANES) * rms_ref[:, c : c + 1][None]
        velocity = velocity.astype(jnp.bfloat16)
        for i in range(SPANS):
            out_ref[place_ref[i], :, lanes] = velocity[i]


def span_filter(owner, rms, moved):
    return pl.pallas_call(
        span_kernel,
        in_specs=[
            pl.BlockSpec(memory_space=pltpu.SMEM),
            pl.BlockSpec(memory_space=pltpu.VMEM),
            pl.BlockSpec(memory_space=pltpu.VMEM),
            pl.BlockSpec(memory_space=pltpu.VMEM),
        ],
        out_specs=pl.BlockSpec(memory_space=pltpu.VMEM),
        out_shape=jax.ShapeDtypeStruct((SPANS * CAP, ZD, COMPS * STEPS * TY), jnp.bfloat16),
        scratch_shapes=[pltpu.SMEM((SPANS,), jnp.int32), pltpu.SMEM((SPANS,), jnp.int32)],
        compiler_params=pltpu.CompilerParams(vmem_limit_bytes=VMEM_LIMIT),
        name="span_filter",
    )(owner, span_blocks(), rms, moved)


def inlet_kernel(x_ref, out_ref):
    for slot in range(CAP):
        for c in range(COMPS):
            for s in range(STEPS):
                first = (c * STEPS + s) * TY
                out_ref[0, :, slot, s, c] = x_ref[:, slot, :, first : first + TY].astype(jnp.float32)


def inlet_tiles(received):
    block = 4
    return pl.pallas_call(
        inlet_kernel,
        grid=(SPANS // block,),
        in_specs=[pl.BlockSpec((block, CAP, ZD, COMPS * STEPS * TY), lambda i: (i, 0, 0, 0))],
        out_specs=pl.BlockSpec((1, block, CAP, STEPS, COMPS, ZD, TY), lambda i: (0, i, 0, 0, 0, 0, 0)),
        out_shape=jax.ShapeDtypeStruct((1, SPANS, CAP, STEPS, COMPS, ZD, TY), jnp.float32),
        compiler_params=pltpu.CompilerParams(vmem_limit_bytes=VMEM_LIMIT),
        name="inlet_tiles",
    )(received)


def local(noise, widths, rms_profile, tile_owner):
    chan = lax.axis_index("chan").astype(jnp.int32).reshape(1)
    half = STEPS // 2
    to_a, to_b, kept, own = time_filter(noise, chan)
    from_a = lax.ppermute(to_a, "chan", PAIR_A)
    from_b = lax.ppermute(to_b, "chan", PAIR_B)
    for_b = (kept[:half] + from_a[half:].astype(jnp.float32)).astype(jnp.float16)
    for_a = (kept[half:] + from_b[half:].astype(jnp.float32)).astype(jnp.float16)
    second_b = lax.ppermute(for_b, "chan", PAIR_B).astype(jnp.float32)
    second_a = lax.ppermute(for_a, "chan", PAIR_A).astype(jnp.float32)
    taps = vertical_filter_matrix(widths)
    taps_high = lax.reduce_precision(taps, 8, 7)
    taps_low = (taps - taps_high).astype(jnp.bfloat16)
    taps_high = taps_high.astype(jnp.bfloat16)
    filtered = vertical_filter(taps_high, taps_low, own, from_a, from_b, second_b, second_a)
    filtered = filtered.reshape(SPANS, ZD, COMPS * STEPS * TY)
    moved = lax.all_to_all(filtered, "span", split_axis=0, concat_axis=0, tiled=True)
    rms = lax.dynamic_slice_in_dim(rms_profile, lax.axis_index("span") * ZD, ZD, 1).T
    sent = span_filter(tile_owner[:, 0], rms, moved)
    received = lax.all_to_all(sent, "span", split_axis=0, concat_axis=0, tiled=True)
    return inlet_tiles(received.reshape(SPANS, CAP, ZD, COMPS * STEPS * TY))


def solution(mesh):
    in_specs = (P(None, "chan", "span", None), P(), P(), P("span", None))
    out_specs = P("span", None, None, "chan", None, None, None)
    return jax.shard_map(local, mesh=mesh, in_specs=in_specs, out_specs=out_specs, check_vma=False)
```

profile of v0, /device:TPU:1, one launch (start us, length us, event | category | flops | bytes accessed | tf_op | source)
XLA Modules:
  0.0 176.8 jit_solution(2797245603078291260)
XLA Ops:
  0.0 0.0 copy-start
  0.0 13.4 %time_filter.1 = (bf16[8,3,64,512]{3,2,1,0:T(8,128)(2,1)}, bf16[8,3,64,512]{3,2,1,0:T(8,128)(2,1)}, f32[8,3,64,512]{3,2,1,0:T(8,128)}, f32[8,3,64,512]{3,2,1,0:T(8,128)}) custom-call(s32[1]{0:T(128)} %bitcast.2.chan_ref, bf16[4,512,640]{2,1,0:T(8,128)(2,1)} %constant.40.clone.taps_ref, bf16[3,40,64,512]{3,2,1,0:T(8,128)(2,1)} %noise_ref.1), custom_call_target="tpu_custom_call" | custom-call | tf_op jit(solution)/shard_map/time_filter/pallas_call | solution.py:107
  13.4 2.1 %collective-permute-start = (bf16[8,3,64,512]{3,2,1,0:T(8,128)(2,1)}, bf16[8,3,64,512]{3,2,1,0:T(8,128)(2,1)S(1)}, u32[]{:S(2)}, u32[]{:S(2)}) collective-permute-start(bf16[8,3,64,512]{3,2,1,0:T(8,128)(2,1)} %get-tuple-element.10), channel_id=1, source_target_pairs={{0,1},{1,0},{2,3},{3,2},{4,5},{5,4},{6,7},{7,6},{8,9},{9,8},{10,11... | collective-permute-start | bytes 4718600 | tf_op jit(solution)/shard_map/ppermute | solution.py:234
  15.5 1.9 %collective-permute-start.1 = (bf16[8,3,64,512]{3,2,1,0:T(8,128)(2,1)}, bf16[8,3,64,512]{3,2,1,0:T(8,128)(2,1)S(1)}, u32[]{:S(2)}, u32[]{:S(2)}) collective-permute-start(bf16[8,3,64,512]{3,2,1,0:T(8,128)(2,1)} %get-tuple-element.11), channel_id=1, source_target_pairs={{1,2},{2,1},{3,0},{0,3},{5,6},{6,5},{7,4},{4,7},{9,10},{10,9},{11,... | collective-permute-start | bytes 4718600 | tf_op jit(solution)/shard_map/ppermute | solution.py:235
  17.4 32.0 %collective-permute-done.a_ref = bf16[8,3,64,512]{3,2,1,0:T(8,128)(2,1)S(1)} collective-permute-done((bf16[8,3,64,512]{3,2,1,0:T(8,128)(2,1)}, bf16[8,3,64,512]{3,2,1,0:T(8,128)(2,1)S(1)}, u32[]{:S(2)}, u32[]{:S(2)}) %collective-permute-start) | collective-permute-done | bytes 1572896 | tf_op jit(solution)/shard_map/ppermute | solution.py:234
  49.4 0.0 copy-start.2
  49.4 2.4 %collective-permute-done.1.b_ref = bf16[8,3,64,512]{3,2,1,0:T(8,128)(2,1)S(1)} collective-permute-done((bf16[8,3,64,512]{3,2,1,0:T(8,128)(2,1)}, bf16[8,3,64,512]{3,2,1,0:T(8,128)(2,1)S(1)}, u32[]{:S(2)}, u32[]{:S(2)}) %collective-permute-start.1) | collective-permute-done | bytes 1572896 | tf_op jit(solution)/shard_map/ppermute | solution.py:235
  51.9 0.0 copy-start.3
  51.9 0.0 copy-start.4
  51.9 3.0 %add_convert_fusion = (f16[4,3,64,512]{3,2,1,0:T(8,128)(2,1)S(1)}, f16[4,3,64,512]{3,2,1,0:T(8,128)(2,1)S(1)}) fusion(f32[8,3,64,512]{3,2,1,0:T(8,128)} %get-tuple-element.12, bf16[8,3,64,512]{3,2,1,0:T(8,128)(2,1)S(1)} %collective-permute-done.1.b_ref, bf16[8,3,64,512]{3,2,1,0:T(8,128)(2,1)S(1)} %collective-permute-done.a_ref), kind=kLoop, calls=%fused_computation | loop fusion | flops 2359296 | bytes 6291456 | tf_op jit(solution)/shard_map/convert_element_type | solution.py:237
  54.9 0.0 copy-done.2
  54.9 0.0 copy-done.3
  54.9 0.1 collective-permute-start.3
  55.0 2.0 %collective-permute-start.2 = (f16[4,3,64,512]{3,2,1,0:T(8,128)(2,1)S(1)}, f16[4,3,64,512]{3,2,1,0:T(8,128)(2,1)S(1)}, u32[]{:S(2)}, u32[]{:S(2)}) collective-permute-start(f16[4,3,64,512]{3,2,1,0:T(8,128)(2,1)S(1)} %get-tuple-element.14), channel_id=1, source_target_pairs={{1,2},{2,1},{3,0},{0,3},{5,6},{6,5},{7,4},{4,7},{9,10},{10,9},{11,... | collective-permute-start | bytes 2359304 | tf_op jit(solution)/shard_map/ppermute | solution.py:238
  57.0 0.0 copy-done.4
  57.0 0.1 fusion.9
  57.1 1.3 fusion
  58.4 13.8 %collective-permute-done.3 = f16[4,3,64,512]{3,2,1,0:T(8,128)(2,1)S(1)} collective-permute-done((f16[4,3,64,512]{3,2,1,0:T(8,128)(2,1)S(1)}, f16[4,3,64,512]{3,2,1,0:T(8,128)(2,1)S(1)}, u32[]{:S(2)}, u32[]{:S(2)}) %collective-permute-start.3) | collective-permute-done | bytes 786464 | tf_op jit(solution)/shard_map/ppermute | solution.py:239
  72.2 1.4 convert_element_type.48.from_a_ref
  73.6 0.0 collective-permute-done.2
  73.6 1.3 convert_element_type.45.from_b_ref
  75.0 6.9 %vertical_filter.1 = bf16[512,1536]{1,0:T(8,128)(2,1)} custom-call(bf16[512,512]{1,0:T(8,128)(2,1)} %get-tuple-element.16.high_ref, bf16[512,512]{1,0:T(8,128)(2,1)} %get-tuple-element.15.low_ref, f32[8,3,64,512]{3,2,1,0:T(8,128)} %get-tuple-element.9.own_ref, bf16[8,3,64,512]{3,2,1,0:T(8,128)(2,1)} %copy-done.2, bf16[8,3,64,512]{3,2,1,0:T(8,128)(2,1)} %copy-done.3, ...), custom_call_target="tpu_custom_call" | custom-call | tf_op jit(solution)/shard_map/vertical_filter/pallas_call | solution.py:148
  81.9 10.7 %all-to-all-start = ((bf16[32,16,1536]{2,1,0:T(8,128)(2,1)}), bf16[32,16,1536]{2,1,0:T(8,128)(2,1)S(1)}, u32[]{:S(2)}, u32[]{:S(2)}) async-start(bf16[32,16,1536]{2,1,0:T(8,128)(2,1)} %bitcast.6), calls=%async_computation | async-start | bytes 3145728 | tf_op jit(solution)/shard_map/all_to_all | solution.py:246
  92.6 0.0 copy-done
  92.6 0.1 constant_dynamic-slice_fusion
  92.7 0.7 copy.9
  93.3 21.4 %all-to-all-done.x_ref = bf16[32,16,1536]{2,1,0:T(8,128)(2,1)S(1)} async-done(((bf16[32,16,1536]{2,1,0:T(8,128)(2,1)}), bf16[32,16,1536]{2,1,0:T(8,128)(2,1)S(1)}, u32[]{:S(2)}, u32[]{:S(2)}) %all-to-all-start) | async-done | bytes 1572896 | tf_op jit(solution)/shard_map/all_to_all | solution.py:246
  114.8 0.0 copy-start.1
  114.8 1.2 copy-done.1
  115.9 6.5 %span_filter.1 = bf16[64,16,1536]{2,1,0:T(8,128)(2,1)} custom-call(s32[32]{0:T(128)} %bitcast.8, bf16[2,3,256,256]{3,2,1,0:T(8,128)(2,1)} %constant.41.clone.taps_ref, f32[16,3]{1,0:T(8,128)} %bitcast.7, bf16[32,16,1536]{2,1,0:T(8,128)(2,1)} %copy-done.1), custom_call_target="tpu_custom_call" | custom-call | tf_op jit(solution)/shard_map/span_filter/pallas_call | solution.py:193
  122.4 46.2 %all_to_all.10 = bf16[64,16,1536]{2,1,0:T(8,128)(2,1)} all-to-all(bf16[64,16,1536]{2,1,0:T(8,128)(2,1)} %span_filter.1), channel_id=1, replica_groups=mesh['span'=32,'chan'=4] {'span'}, dimensions={0} | all-to-all | bytes 6291456 | tf_op jit(solution)/shard_map/all_to_all | solution.py:249
  168.6 8.1 %inlet_tiles.1 = f32[1,32,2,8,3,16,64]{6,5,4,3,2,1,0:T(8,128)} custom-call(bf16[32,2,16,1536]{3,2,1,0:T(8,128)(2,1)} %bitcast.5), custom_call_target="tpu_custom_call" | custom-call | tf_op jit(solution)/shard_map/inlet_tiles/pallas_call | solution.py:219
  (3 shorter events, 0.0 us)
Async XLA Ops:
  0.0 92.6 %copy-start = (f32[3,512]{1,0:T(4,128)S(1)}, f32[3,512]{1,0:T(4,128)}, u32[]{:S(2)}) copy-start(f32[3,512]{1,0:T(4,128)} %param.8) | copy-start | bytes 18436
  13.4 36.1 %collective-permute-start = (bf16[8,3,64,512]{3,2,1,0:T(8,128)(2,1)}, bf16[8,3,64,512]{3,2,1,0:T(8,128)(2,1)S(1)}, u32[]{:S(2)}, u32[]{:S(2)}) collective-permute-start(bf16[8,3,64,512]{3,2,1,0:T(8,128)(2,1)} %get-tuple-element.10), channel_id=1, source_target_pairs={{0,1},{1,0},{2,3},{3,2},{4,5},{5,4},{6,7},{7,6},{8,9},{9,8},{10,11... | collective-permute-start | bytes 4718600 | tf_op jit(solution)/shard_map/ppermute | solution.py:234
  15.5 36.4 %collective-permute-start.1 = (bf16[8,3,64,512]{3,2,1,0:T(8,128)(2,1)}, bf16[8,3,64,512]{3,2,1,0:T(8,128)(2,1)S(1)}, u32[]{:S(2)}, u32[]{:S(2)}) collective-permute-start(bf16[8,3,64,512]{3,2,1,0:T(8,128)(2,1)} %get-tuple-element.11), channel_id=1, source_target_pairs={{1,2},{2,1},{3,0},{0,3},{5,6},{6,5},{7,4},{4,7},{9,10},{10,9},{11,... | collective-permute-start | bytes 4718600 | tf_op jit(solution)/shard_map/ppermute | solution.py:235
  49.4 5.5 %copy-start.2 = (bf16[8,3,64,512]{3,2,1,0:T(8,128)(2,1)}, bf16[8,3,64,512]{3,2,1,0:T(8,128)(2,1)S(1)}, u32[]{:S(2)}) copy-start(bf16[8,3,64,512]{3,2,1,0:T(8,128)(2,1)S(1)} %collective-permute-done.a_ref) | copy-start | bytes 4718596
  51.9 3.0 %copy-start.3 = (bf16[8,3,64,512]{3,2,1,0:T(8,128)(2,1)}, bf16[8,3,64,512]{3,2,1,0:T(8,128)(2,1)S(1)}, u32[]{:S(2)}) copy-start(bf16[8,3,64,512]{3,2,1,0:T(8,128)(2,1)S(1)} %collective-permute-done.1.b_ref) | copy-start | bytes 4718596
  51.9 5.1 %copy-start.4 = (s32[512]{0:T(512)S(1)}, s32[512]{0:T(512)}, u32[]{:S(2)}) copy-start(s32[512]{0:T(512)} %param.7) | copy-start | bytes 6148
  54.9 17.2 %collective-permute-start.3 = (f16[4,3,64,512]{3,2,1,0:T(8,128)(2,1)S(1)}, f16[4,3,64,512]{3,2,1,0:T(8,128)(2,1)S(1)}, u32[]{:S(2)}, u32[]{:S(2)}) collective-permute-start(f16[4,3,64,512]{3,2,1,0:T(8,128)(2,1)S(1)} %get-tuple-element.13), channel_id=1, source_target_pairs={{0,1},{1,0},{2,3},{3,2},{4,5},{5,4},{6,7},{7,6},{8,9},{9,8},{10,11... | collective-permute-start | bytes 2359304 | tf_op jit(solution)/shard_map/ppermute | solution.py:239
  55.0 18.6 %collective-permute-start.2 = (f16[4,3,64,512]{3,2,1,0:T(8,128)(2,1)S(1)}, f16[4,3,64,512]{3,2,1,0:T(8,128)(2,1)S(1)}, u32[]{:S(2)}, u32[]{:S(2)}) collective-permute-start(f16[4,3,64,512]{3,2,1,0:T(8,128)(2,1)S(1)} %get-tuple-element.14), channel_id=1, source_target_pairs={{1,2},{2,1},{3,0},{0,3},{5,6},{6,5},{7,4},{4,7},{9,10},{10,9},{11,... | collective-permute-start | bytes 2359304 | tf_op jit(solution)/shard_map/ppermute | solution.py:238
  81.9 32.9 %all-to-all-start = ((bf16[32,16,1536]{2,1,0:T(8,128)(2,1)}), bf16[32,16,1536]{2,1,0:T(8,128)(2,1)S(1)}, u32[]{:S(2)}, u32[]{:S(2)}) async-start(bf16[32,16,1536]{2,1,0:T(8,128)(2,1)} %bitcast.6), calls=%async_computation | async-start | bytes 3145728 | tf_op jit(solution)/shard_map/all_to_all | solution.py:246
  114.8 1.2 copy-start.1
where the time goes:
time: 178 us; the launch traced here: 177 us
  waiting for transfers between devices  69.7 us (39%)
  blocking collectives  46.2 us (26%)
  Pallas kernels  34.9 us (20%)
  starting transfers between devices  16.8 us (9%)
  other arithmetic  7.19 us (4%)
  local copies, waits for them, and re-layouts  1.93 us (1%)
    all_to_all x1, blocking collectives, local(): lax.all_to_all(sent, 'span', split_axis=0, concat_axis=0, tiled=True)  46.2 us
    ppermute x1, waiting for transfers between devices, local(): from_a = lax.ppermute(to_a, 'chan', PAIR_A)  32 us
    all_to_all x1, waiting for transfers between devices, local(): lax.all_to_all(filtered, 'span', split_axis=0, concat_axis=0, tiled=True)  21.4 us
    ppermute x1, waiting for transfers between devices, local(): second_a = lax.ppermute(for_a, 'chan', PAIR_A).astype(jnp.float32)  13.8 us
    pallas_call x1, Pallas kernels, time_filter(): pl.pallas_call(time_kernel, grid_spec=pltpu.PrefetchScalarGridSpec(num_sc...  13.4 us
    all_to_all x1, starting transfers between devices, local(): lax.all_to_all(filtered, 'span', split_axis=0, concat_axis=0, tiled=True)  10.7 us
    pallas_call x1, Pallas kernels, inlet_tiles(): pl.pallas_call(inlet_kernel, grid=(SPANS // block,), in_specs=[pl.BlockSp...  8.14 us
    pallas_call x1, Pallas kernels, vertical_filter(): pl.pallas_call(vertical_kernel, grid=(COMPS,), in_specs=[whole, whole, pl...  6.88 us
  transfers between devices with their start and end apart: 5, of which 4 were waited for; matrix products, arithmetic and copies ran while one was open for 2% of the time, Pallas kernels for 0%

commit v1 on v0

v1 whole, which is shorter than its diff:
```python
import functools
import math

import jax
import jax.numpy as jnp
import ml_dtypes
import numpy as np
from jax import lax
from jax.experimental import pallas as pl
from jax.experimental.pallas import tpu as pltpu
from jax.sharding import PartitionSpec as P

Y = 2048
Z = 512
KT = 128
KY = 96
KZ = 48
NW = 4
TY = 64
COMPS = 3
STEPS = 8
PLANES = 40
CHANS = 4
SPANS = 32
CAP = 2
ZD = Z // SPANS
ROWS = 16
BLOCK = 32
LANES = 2 * TY
WIDTH = STEPS * TY
MIB = 1024 * 1024
TIME_VMEM = 57 * MIB
VMEM = 16 * MIB

PAIR_A = [(0, 1), (1, 0), (2, 3), (3, 2)]
PAIR_B = [(1, 2), (2, 1), (3, 0), (0, 3)]


def gaussian(offset, length_scale):
    return np.exp(-math.pi * offset * offset / (2.0 * length_scale * length_scale))


def time_taps():
    offset = np.arange(CHANS * PLANES)[None, :] - np.arange(CHANS * STEPS)[:, None]
    norm = np.sqrt(np.sum(gaussian(np.arange(KT) - KT // 2.0, KT / 4.0) ** 2))
    inside = (offset >= 0) & (offset < KT)
    return np.where(inside, gaussian(offset - KT // 2.0, KT / 4.0) / norm, 0.0)


def time_blocks():
    taps = time_taps().astype(np.float32).reshape(CHANS, STEPS, CHANS, PLANES)
    half = STEPS // 2
    blocks = []
    for d in range(CHANS):
        a, b, far = d ^ 1, CHANS - 1 - d, (d + 2) % CHANS
        first, second = slice(0, half), slice(half, STEPS)
        order = [(a, first), (far, first), (b, second), (far, second), (b, first), (a, second), (d, first), (d, second)]
        rows = np.concatenate([taps[block, steps, d] for block, steps in order])
        blocks.append(np.kron(rows, np.eye(ROWS, dtype=np.float32)))
    return np.stack(blocks).astype(ml_dtypes.bfloat16)


def split(values):
    high = values.astype(ml_dtypes.bfloat16)
    return high, (values - high.astype(np.float32)).astype(ml_dtypes.bfloat16)


def span_blocks():
    taps = gaussian(np.arange(KY) - KY // 2.0, KY / 4.0)
    taps = taps / np.sqrt(np.sum(taps**2))
    blocks = np.zeros((4, 2, TY, 2, 2, TY), np.float32)
    for source in range(4):
        for target in range(2):
            shift = TY * (source - 1 - target)
            tap = np.arange(TY)[:, None] + shift - np.arange(TY)[None, :] + KY // 2
            band = np.where((tap >= 0) & (tap < KY), taps[np.clip(tap, 0, KY - 1)], 0.0)
            for step in range(2):
                blocks[source, step, :, target, step, :] = band
    return np.stack(split(blocks.reshape(2, 4 * TY, 4 * TY)))


def vertical_filter_matrix(widths):
    def device_gaussian(offset, length_scale):
        offset_f = offset.astype(jnp.float32)
        return jnp.exp(-math.pi * offset_f * offset_f / (2.0 * length_scale * length_scale))

    offset = jnp.arange(Z)[None, :] - jnp.arange(Z)[:, None]
    length_scale = (KZ * (widths + 1)).astype(jnp.float32) / (4.0 * NW)
    tap_offsets = jnp.arange(KZ) - KZ // 2
    tap_norm = jnp.sqrt(
        jnp.sum(device_gaussian(tap_offsets[None, :], length_scale[:, None]) ** 2, axis=1)
    )
    inside = (offset >= -(KZ // 2)) & (offset < KZ - KZ // 2)
    return jnp.where(
        inside, device_gaussian(offset, length_scale[:, None]) / tap_norm[:, None], 0.0
    )


def time_kernel(chan_ref, taps_ref, noise_ref, to_a_ref, to_b_ref, kept_ref, own_ref):
    for first in range(0, BLOCK, ROWS):
        rows = slice(first, first + ROWS)
        planes = noise_ref[:, :, rows].reshape(PLANES * ROWS, Z)
        sums = jnp.dot(taps_ref[0], planes, preferred_element_type=jnp.float32)
        sums = sums.reshape(CHANS * STEPS, 1, ROWS, Z)
        to_a_ref[:, :, rows] = sums[:8].astype(jnp.bfloat16)
        to_b_ref[:, :, rows] = sums[8:16].astype(jnp.bfloat16)
        kept_ref[:, :, rows] = sums[16:24]
        own_ref[:, :, rows] = sums[24:]


def time_filter(noise, chan, comp):
    part = pl.BlockSpec((STEPS, 1, BLOCK, Z), lambda j, chan: (0, 0, j, 0))
    shape = (STEPS, 1, TY, Z)
    return pl.pallas_call(
        time_kernel,
        grid_spec=pltpu.PrefetchScalarGridSpec(
            num_scalar_prefetch=1,
            grid=(TY // BLOCK,),
            in_specs=[
                pl.BlockSpec((1, CHANS * STEPS * ROWS, PLANES * ROWS), lambda j, chan: (chan[0], 0, 0)),
                pl.BlockSpec((1, PLANES, BLOCK, Z), lambda j, chan: (comp, 0, j, 0)),
            ],
            out_specs=[part] * 4,
        ),
        out_shape=[
            jax.ShapeDtypeStruct(shape, jnp.bfloat16),
            jax.ShapeDtypeStruct(shape, jnp.bfloat16),
            jax.ShapeDtypeStruct(shape, jnp.float32),
            jax.ShapeDtypeStruct(shape, jnp.float32),
        ],
        compiler_params=pltpu.CompilerParams(vmem_limit_bytes=TIME_VMEM),
        name="time_filter",
    )(chan, time_blocks(), noise)


def vertical_kernel(high_ref, low_ref, first_ref, second_ref, *refs):
    out_ref = refs[-1]
    timed = jnp.concatenate([first_ref[...], second_ref[...]]).reshape(STEPS * TY, Z)
    timed_high = timed.astype(jnp.bfloat16)
    timed_low = (timed - timed_high.astype(jnp.float32)).astype(jnp.bfloat16)

    def product(taps, values):
        return lax.dot_general(taps, values, (((1,), (1,)), ((), ())), preferred_element_type=jnp.float32)

    total = product(high_ref[...], timed_low) + product(low_ref[...], timed_high)
    total = total + product(high_ref[...], timed_high)
    out_ref[...] = total.astype(jnp.bfloat16).reshape(out_ref.shape)


def vertical_filter(taps, sums, shape, place, so_far=None):
    half = pl.BlockSpec((STEPS // 2, 1, TY, Z), lambda i: (0, 0, 0, 0))
    in_specs = [pl.BlockSpec((Z, Z), lambda i: (0, 0))] * 2 + [half] * 2
    if so_far is not None:
        in_specs.append(pl.BlockSpec(memory_space=pl.ANY))
    return pl.pallas_call(
        vertical_kernel,
        grid=(1,),
        in_specs=in_specs,
        out_specs=pl.BlockSpec((SPANS, ZD, WIDTH), lambda i: place),
        out_shape=jax.ShapeDtypeStruct(shape, jnp.bfloat16),
        input_output_aliases={} if so_far is None else {4: 0},
        compiler_params=pltpu.CompilerParams(vmem_limit_bytes=VMEM),
        name="vertical_filter",
    )(*taps, *sums, *([] if so_far is None else [so_far]))


def span_kernel(owner_ref, slot_ref, taps_ref, rms_ref, x_ref, *refs):
    out_ref = refs[-1]
    out_ref[...] = jnp.zeros_like(out_ref)
    pairs = SPANS // 2
    for first in range(0, WIDTH, LANES):
        lanes = slice(first, first + LANES)
        x = x_ref[:, :, lanes]
        around = jnp.concatenate([x[SPANS - 1 :], x, x[:1]], axis=0).reshape(pairs + 1, 2, ZD, LANES)
        total = None
        for part in (1, 0):
            for half in range(2):
                tiles = [around[half : half + pairs, tile] for tile in range(2)]
                rows = jnp.concatenate(tiles, axis=-1).reshape(pairs * ZD, 2 * LANES)
                term = jnp.dot(rows, taps_ref[part, half], preferred_element_type=jnp.float32)
                total = term if total is None else total + term
        velocity = (total.reshape(pairs, ZD, 2 * LANES) * rms_ref[...]).astype(jnp.bfloat16)
        for i in range(SPANS):
            target = (i % 2) * LANES
            rows = pl.ds(pl.multiple_of(slot_ref[i] * ZD, ZD), ZD)
            out_ref[owner_ref[i], rows, lanes] = velocity[i // 2, :, target : target + LANES]


def span_filter(owner, slot, rms, moved, place, first, comps, shape, so_far=None):
    row, column = place
    in_specs = [
        pl.BlockSpec(memory_space=pltpu.SMEM),
        pl.BlockSpec(memory_space=pltpu.SMEM),
        pl.BlockSpec((2, 2, 2 * LANES, 2 * LANES), lambda i: (0, 0, 0, 0)),
        pl.BlockSpec((1, ZD, 1), lambda i: (first + i, 0, 0)),
        pl.BlockSpec((SPANS, ZD, WIDTH), lambda i: (0, row, column + i)),
    ]
    if so_far is not None:
        in_specs.append(pl.BlockSpec(memory_space=pl.ANY))
    return pl.pallas_call(
        span_kernel,
        grid=(comps,),
        in_specs=in_specs,
        out_specs=pl.BlockSpec((SPANS, CAP * ZD, WIDTH), lambda i: (0, i, 0)),
        out_shape=jax.ShapeDtypeStruct(shape, jnp.bfloat16),
        input_output_aliases={} if so_far is None else {5: 0},
        compiler_params=pltpu.CompilerParams(vmem_limit_bytes=VMEM),
        name="span_filter",
    )(owner, slot, span_blocks(), rms, moved, *([] if so_far is None else [so_far]))


def inlet_kernel(x_ref, *refs):
    out_ref = refs[-1]
    for slot in range(CAP):
        for s in range(STEPS):
            tile = x_ref[:, slot * ZD : (slot + 1) * ZD, s * TY : (s + 1) * TY]
            out_ref[0, :, slot, s, 0] = tile.astype(jnp.float32)


def inlet_tiles(received, first, comps, so_far=None):
    block = 8
    in_specs = [pl.BlockSpec((block, CAP * ZD, WIDTH), lambda c, i: (i, c, 0))]
    if so_far is not None:
        in_specs.append(pl.BlockSpec(memory_space=pl.ANY))
    return pl.pallas_call(
        inlet_kernel,
        grid=(comps, SPANS // block),
        in_specs=in_specs,
        out_specs=pl.BlockSpec((1, block, CAP, STEPS, 1, ZD, TY), lambda c, i: (0, i, 0, 0, first + c, 0, 0)),
        out_shape=jax.ShapeDtypeStruct((1, SPANS, CAP, STEPS, COMPS, ZD, TY), jnp.float32),
        input_output_aliases={} if so_far is None else {1: 0},
        compiler_params=pltpu.CompilerParams(vmem_limit_bytes=VMEM),
        name="inlet_tiles",
    )(received, *([] if so_far is None else [so_far]))


def after(values, others):
    return lax.optimization_barrier((*values, *others))[: len(values)]


def first_exchange(to_a, to_b):
    return lax.ppermute(to_a, "chan", PAIR_A), lax.ppermute(to_b, "chan", PAIR_B)


def for_second_exchange(kept, from_a, from_b):
    half = STEPS // 2
    for_b = (kept[:half] + from_a[half:].astype(jnp.float32)).astype(jnp.float16)
    for_a = (kept[half:] + from_b[half:].astype(jnp.float32)).astype(jnp.float16)
    return for_b, for_a


def second_exchange(for_b, for_a):
    return lax.ppermute(for_b, "chan", PAIR_B), lax.ppermute(for_a, "chan", PAIR_A)


def summed(own, from_a, from_b, second_b, second_a):
    half = STEPS // 2
    first = own[:half] + from_a[:half].astype(jnp.float32) + second_b.astype(jnp.float32)
    second = own[half:] + from_b[:half].astype(jnp.float32) + second_a.astype(jnp.float32)
    return first, second


def along_span(values):
    return lax.all_to_all(values, "span", split_axis=0, concat_axis=0, tiled=True)


def local(noise, widths, rms_profile, tile_owner):
    chan = lax.axis_index("chan").astype(jnp.int32).reshape(1)
    taps = vertical_filter_matrix(widths)
    taps_high = lax.reduce_precision(taps, 8, 7)
    taps_low = (taps - taps_high).astype(jnp.bfloat16)
    taps = (taps_high.astype(jnp.bfloat16), taps_low)
    rms = lax.dynamic_slice_in_dim(rms_profile, lax.axis_index("span") * ZD, ZD, 1)[:, :, None]
    owner = tile_owner[:, 0]
    tile = jnp.arange(SPANS, dtype=jnp.int32)
    earlier = (owner[:, None] == owner[None, :]) & (tile[None, :] < tile[:, None])
    slot = jnp.sum(earlier.astype(jnp.int32), axis=1)

    partial = [time_filter(noise, chan, c) for c in range(COMPS)]
    early = (*partial[1], *partial[2], *taps, owner, slot, rms)
    sums, got = [], None
    for to_a, to_b, kept, own in partial:
        if got is None:
            got = after(first_exchange(to_a, to_b), early)
        else:
            got = first_exchange(*after((to_a, to_b), got))
        sums.append(summed(own, *got, *second_exchange(*for_second_exchange(kept, *got))))

    planes = None
    for c in range(2):
        planes = vertical_filter(taps, sums[c], (SPANS, ZD, 2 * WIDTH), (0, 0, c), planes)
    moved = along_span(planes)
    shape = (SPANS, 2 * CAP * ZD + ZD, WIDTH)
    mixed = vertical_filter(taps, sums[2], shape, (0, 2 * CAP, 0))
    mixed = along_span(span_filter(owner, slot, rms, moved, (0, 0), 0, 2, shape, mixed))
    last = span_filter(owner, slot, rms, mixed, (2 * CAP, 0), 2, 1, (SPANS, CAP * ZD, WIDTH))
    last = along_span(last)
    return inlet_tiles(last, 2, 1, inlet_tiles(mixed, 0, 2))


def solution(mesh):
    in_specs = (P(None, "chan", "span", None), P(), P(), P("span", None))
    out_specs = P("span", None, None, "chan", None, None, None)
    return jax.shard_map(local, mesh=mesh, in_specs=in_specs, out_specs=out_specs, check_vma=False)
```

time: 178 us -> 148 us (0.83)
  waiting for transfers between devices: 69.7 us -> 34 us
  starting transfers between devices: 16.8 us -> 32.3 us
  blocking collectives: 46.2 us -> 38.6 us
  Pallas kernels: 34.9 us -> 31.2 us
  local copies, waits for them, and re-layouts: 1.93 us -> 5.53 us
    ppermute x4 -> x12, waiting for transfers between devices: 48.2 us -> 19.6 us  [the longest x3 7.37 us: second_exchange(): lax.ppermute(for_a, 'chan', PAIR_A)]
    ppermute x4 -> x12, starting transfers between devices: 6.09 us -> 14.6 us  [the longest x3 5.78 us: first_exchange(): lax.ppermute(to_b, 'chan', PAIR_B)]
    all_to_all x1, blocking collectives: 46.2 us -> 38.6 us  [along_span(): lax.all_to_all(values, 'span', split_axis=0, concat_axis=0, tiled=True)]
    all_to_all x1 -> x2, starting transfers between devices: 10.7 us -> 17.7 us  [along_span(): lax.all_to_all(values, 'span', split_axis=0, concat_axis=0, tiled=True)]
    all_to_all x1 -> x2, waiting for transfers between devices: 21.4 us -> 14.4 us  [along_span(): lax.all_to_all(values, 'span', split_axis=0, concat_axis=0, tiled=True)]
    pallas_call x3 -> x7, Pallas kernels: 21.5 us -> 17.1 us  [the longest x2 7.46 us: inlet_tiles(): pl.pallas_call(inlet_kernel, grid=(comps, SPANS // block), in_specs=in_sp...]
    unnamed x11 -> x34, local copies, waits for them, and re-layouts: 1.85 us -> 5.36 us
    convert_element_type x3, other arithmetic: 5.82 us -> 2.5 us  [for_second_exchange(): (kept[half:] + from_b[half:].astype(jnp.float32)).astype(jnp.float16)]
  transfers between devices with their start and end apart: 5 -> 14, of which waited for: 4 -> 10; matrix products, arithmetic and copies ran while one was open for 2% -> 4% of each run, Pallas kernels for 0% -> 13%
where the time goes in v1:
time: 148 us
  blocking collectives  38.6 us (26%)
  waiting for transfers between devices  34 us (23%)
  starting transfers between devices  32.3 us (22%)
  Pallas kernels  31.2 us (21%)
  other arithmetic  5.81 us (4%)
  local copies, waits for them, and re-layouts  5.53 us (4%)
    all_to_all x1, blocking collectives, along_span(): lax.all_to_all(values, 'span', split_axis=0, concat_axis=0, tiled=True)  38.6 us
    all_to_all x2, starting transfers between devices, along_span(): lax.all_to_all(values, 'span', split_axis=0, concat_axis=0, tiled=True)  17.7 us
    all_to_all x2, waiting for transfers between devices, along_span(): lax.all_to_all(values, 'span', split_axis=0, concat_axis=0, tiled=True)  14.4 us
    pallas_call x3, Pallas kernels, time_filter(): pl.pallas_call(time_kernel, grid_spec=pltpu.PrefetchScalarGridSpec(num_sc...  14.1 us
    pallas_call x2, Pallas kernels, inlet_tiles(): pl.pallas_call(inlet_kernel, grid=(comps, SPANS // block), in_specs=in_sp...  7.46 us
    ppermute x3, waiting for transfers between devices, second_exchange(): lax.ppermute(for_a, 'chan', PAIR_A)  7.37 us
    ppermute x3, waiting for transfers between devices, first_exchange(): lax.ppermute(to_a, 'chan', PAIR_A)  6.81 us
    ppermute x3, starting transfers between devices, first_exchange(): lax.ppermute(to_b, 'chan', PAIR_B)  5.78 us
  transfers between devices with their start and end apart: 14, of which 10 were waited for; matrix products, arithmetic and copies ran while one was open for 4% of the time, Pallas kernels for 13%

profile of v1, /device:TPU:1, one launch (start us, length us, event | category | flops | bytes accessed | tf_op | source)
XLA Modules:
  0.0 147.7 jit_solution(14355757368721102823)
XLA Ops:
  0.0 0.0 copy-start
  0.0 4.7 %time_filter.4 = (bf16[8,1,64,512]{3,2,1,0:T(8,128)(2,1)}, bf16[8,1,64,512]{3,2,1,0:T(8,128)(2,1)}, f32[8,1,64,512]{3,2,1,0:T(8,128)}, f32[8,1,64,512]{3,2,1,0:T(8,128)}) custom-call(s32[1]{0:T(128)} %bitcast.2.chan_ref, bf16[4,512,640]{2,1,0:T(8,128)(2,1)} %constant.40.clone.taps_ref, bf16[3,40,64,512]{3,2,1,0:T(8,128)(2,1)} %noise_ref.5), custom_call_target="tpu_custom_call" | custom-call | tf_op jit(solution)/shard_map/time_filter/pallas_call | solution.py:114
  4.7 2.1 %collective-permute-start = (bf16[8,1,64,512]{3,2,1,0:T(8,128)(2,1)}, bf16[8,1,64,512]{3,2,1,0:T(8,128)(2,1)S(1)}, u32[]{:S(2)}, u32[]{:S(2)}) collective-permute-start(bf16[8,1,64,512]{3,2,1,0:T(8,128)(2,1)} %get-tuple-element.26), channel_id=1, source_target_pairs={{0,1},{1,0},{2,3},{3,2},{4,5},{5,4},{6,7},{7,6},{8,9},{9,8},{10,11... | collective-permute-start | bytes 1572872 | tf_op jit(solution)/shard_map/ppermute | solution.py:242
  6.8 1.9 %collective-permute-start.1 = (bf16[8,1,64,512]{3,2,1,0:T(8,128)(2,1)}, bf16[8,1,64,512]{3,2,1,0:T(8,128)(2,1)}, u32[]{:S(2)}, u32[]{:S(2)}) collective-permute-start(bf16[8,1,64,512]{3,2,1,0:T(8,128)(2,1)} %get-tuple-element.27), channel_id=1, source_target_pairs={{1,2},{2,1},{3,0},{0,3},{5,6},{6,5},{7,4},{4,7},{9,10},{10,9},{11,... | collective-permute-start | bytes 1572872 | tf_op jit(solution)/shard_map/ppermute | solution.py:242
  8.7 0.0 copy-done.14
  8.7 0.1 fusion.9
  8.8 0.0 copy-done
  8.8 0.1 dynamic-slice_bitcast_fusion
  8.9 4.6 %time_filter.3 = (bf16[8,1,64,512]{3,2,1,0:T(8,128)(2,1)}, bf16[8,1,64,512]{3,2,1,0:T(8,128)(2,1)}, f32[8,1,64,512]{3,2,1,0:T(8,128)}, f32[8,1,64,512]{3,2,1,0:T(8,128)}) custom-call(s32[1]{0:T(128)} %bitcast.2.chan_ref, bf16[4,512,640]{2,1,0:T(8,128)(2,1)} %constant.40.clone.taps_ref, bf16[3,40,64,512]{3,2,1,0:T(8,128)(2,1)} %noise_ref.5), custom_call_target="tpu_custom_call" | custom-call | tf_op jit(solution)/shard_map/time_filter/pallas_call | solution.py:114
  13.6 0.0 copy-start.15
  13.6 0.0 copy-start.12
  13.6 4.8 %time_filter.5 = (bf16[8,1,64,512]{3,2,1,0:T(8,128)(2,1)}, bf16[8,1,64,512]{3,2,1,0:T(8,128)(2,1)}, f32[8,1,64,512]{3,2,1,0:T(8,128)}, f32[8,1,64,512]{3,2,1,0:T(8,128)}) custom-call(s32[1]{0:T(128)} %bitcast.2.chan_ref, bf16[4,512,640]{2,1,0:T(8,128)(2,1)} %constant.40.clone.taps_ref, bf16[3,40,64,512]{3,2,1,0:T(8,128)(2,1)} %noise_ref.5), custom_call_target="tpu_custom_call" | custom-call | tf_op jit(solution)/shard_map/time_filter/pallas_call | solution.py:114
  18.4 0.0 copy-done.7
  18.4 0.2 convert_reduce_fusion.slot_ref
  18.6 0.3 fusion
  18.8 0.0 copy-start.3
  18.9 0.0 collective-permute-done
  18.9 1.9 %collective-permute-done.1 = bf16[8,1,64,512]{3,2,1,0:T(8,128)(2,1)} collective-permute-done((bf16[8,1,64,512]{3,2,1,0:T(8,128)(2,1)}, bf16[8,1,64,512]{3,2,1,0:T(8,128)(2,1)}, u32[]{:S(2)}, u32[]{:S(2)}) %collective-permute-start.1) | collective-permute-done | bytes 524320 | tf_op jit(solution)/shard_map/ppermute | solution.py:242
  20.8 0.0 copy-done.16
  20.8 0.0 collective-permute-start.2
  20.8 2.0 %collective-permute-start.4 = (bf16[8,1,64,512]{3,2,1,0:T(8,128)(2,1)S(1)}, bf16[8,1,64,512]{3,2,1,0:T(8,128)(2,1)S(1)}, u32[]{:S(2)}, u32[]{:S(2)}) collective-permute-start(bf16[8,1,64,512]{3,2,1,0:T(8,128)(2,1)S(1)} %copy-done.15), channel_id=1, source_target_pairs={{1,2},{2,1},{3,0},{0,3},{5,6},{6,5},{7,4},{4,7},{9,10},{10,9},{11,... | collective-permute-start | bytes 1572872 | tf_op jit(solution)/shard_map/ppermute | solution.py:242
  22.8 1.1 add_convert_fusion.2
  23.9 0.9 collective-permute-start.7
  24.8 0.8 collective-permute-start.6
  25.5 6.8 %collective-permute-done.2 = bf16[8,1,64,512]{3,2,1,0:T(8,128)(2,1)S(1)} collective-permute-done((bf16[8,1,64,512]{3,2,1,0:T(8,128)(2,1)S(1)}, bf16[8,1,64,512]{3,2,1,0:T(8,128)(2,1)S(1)}, u32[]{:S(2)}, u32[]{:S(2)}) %collective-permute-start.2) | collective-permute-done | bytes 524320 | tf_op jit(solution)/shard_map/ppermute | solution.py:242
  32.3 1.3 collective-permute-done.4
  33.6 0.2 add_convert_fusion.4
  33.8 0.1 collective-permute-start.5
  33.9 2.0 %collective-permute-start.3 = (f16[4,1,64,512]{3,2,1,0:T(8,128)(2,1)S(1)}, f16[4,1,64,512]{3,2,1,0:T(8,128)(2,1)S(1)}, u32[]{:S(2)}, u32[]{:S(2)}) collective-permute-start(f16[4,1,64,512]{3,2,1,0:T(8,128)(2,1)S(1)} %get-tuple-element.52), channel_id=1, source_target_pairs={{1,2},{2,1},{3,0},{0,3},{5,6},{6,5},{7,4},{4,7},{9,10},{10,9},{11,... | collective-permute-start | bytes 786440 | tf_op jit(solution)/shard_map/ppermute | solution.py:253
  35.9 0.8 collective-permute-start.8
  36.7 1.3 collective-permute-done.7
  38.0 1.9 %collective-permute-start.10 = (bf16[8,1,64,512]{3,2,1,0:T(8,128)(2,1)}, bf16[8,1,64,512]{3,2,1,0:T(8,128)(2,1)}, u32[]{:S(2)}, u32[]{:S(2)}) collective-permute-start(bf16[8,1,64,512]{3,2,1,0:T(8,128)(2,1)} %get-tuple-element.40), channel_id=1, source_target_pairs={{1,2},{2,1},{3,0},{0,3},{5,6},{6,5},{7,4},{4,7},{9,10},{10,9},{11,... | collective-permute-start | bytes 1572872 | tf_op jit(solution)/shard_map/ppermute | solution.py:242
  39.9 0.0 collective-permute-done.6
  39.9 1.3 convert_add_fusion.2
  41.1 1.8 %vertical_filter.3.refs_0_ = bf16[32,16,1024]{2,1,0:T(8,128)(2,1)} custom-call(bf16[512,512]{1,0:T(8,128)(2,1)S(1)} %get-tuple-element.54.high_ref, bf16[512,512]{1,0:T(8,128)(2,1)S(1)} %get-tuple-element.53.low_ref, f32[4,1,64,512]{3,2,1,0:T(8,128)S(1)} %get-tuple-element.46.first_ref, f32[4,1,64,512]{3,2,1,0:T(8,128)S(1)} %get-tuple-element.45.second_ref), custom_call_target="tpu_custom_call" | custom-call | tf_op jit(solution)/shard_map/vertical_filter/pallas_call | solution.py:155
  42.9 0.6 collective-permute-done.5
  43.6 1.1 collective-permute-done.3
  44.7 0.2 convert_add_fusion.4
  44.9 1.8 %vertical_filter.4 = bf16[32,16,1024]{2,1,0:T(8,128)(2,1)} custom-call(bf16[512,512]{1,0:T(8,128)(2,1)S(1)} %get-tuple-element.54.high_ref, bf16[512,512]{1,0:T(8,128)(2,1)S(1)} %get-tuple-element.53.low_ref, f32[4,1,64,512]{3,2,1,0:T(8,128)S(1)} %get-tuple-element.50.first_ref, ...), custom_call_target="tpu_custom_call", output_to_operand_aliasing={{}: (4, {})} | custom-call | tf_op jit(solution)/shard_map/vertical_filter/pallas_call | solution.py:155
  46.7 13.7 %all-to-all-start = ((bf16[32,16,1024]{2,1,0:T(8,128)(2,1)}), bf16[32,16,1024]{2,1,0:T(8,128)(2,1)}, u32[]{:S(2)}, u32[]{:S(2)}) async-start(bf16[32,16,1024]{2,1,0:T(8,128)(2,1)} %vertical_filter.4), calls=%async_computation | async-start | bytes 2097152 | tf_op jit(solution)/shard_map/all_to_all | solution.py:264
  60.4 0.0 collective-permute-done.8
  60.5 0.0 collective-permute-done.10
  60.5 1.2 add_convert_fusion
  61.7 0.3 collective-permute-start.11
  62.0 1.9 %collective-permute-start.9 = (f16[4,1,64,512]{3,2,1,0:T(8,128)(2,1)S(1)}, f16[4,1,64,512]{3,2,1,0:T(8,128)(2,1)S(1)}, u32[]{:S(2)}, u32[]{:S(2)}) collective-permute-start(f16[4,1,64,512]{3,2,1,0:T(8,128)(2,1)S(1)} %get-tuple-element.44), channel_id=1, source_target_pairs={{1,2},{2,1},{3,0},{0,3},{5,6},{6,5},{7,4},{4,7},{9,10},{10,9},{11,... | collective-permute-start | bytes 786440 | tf_op jit(solution)/shard_map/ppermute | solution.py:253
  63.9 0.1 copy.16.rms_ref
  64.0 5.4 %collective-permute-done.11 = f16[4,1,64,512]{3,2,1,0:T(8,128)(2,1)S(1)} collective-permute-done((f16[4,1,64,512]{3,2,1,0:T(8,128)(2,1)S(1)}, f16[4,1,64,512]{3,2,1,0:T(8,128)(2,1)S(1)}, u32[]{:S(2)}, u32[]{:S(2)}) %collective-permute-start.11) | collective-permute-done | bytes 262176 | tf_op jit(solution)/shard_map/ppermute | solution.py:253
  69.5 1.1 collective-permute-done.9
  70.6 1.2 convert_add_fusion
  71.9 1.0 copy-done.4
  72.9 1.0 vertical_filter.5.refs_0_
  73.9 3.8 %all-to-all-done.x_ref = bf16[32,16,1024]{2,1,0:T(8,128)(2,1)} async-done(((bf16[32,16,1024]{2,1,0:T(8,128)(2,1)}), bf16[32,16,1024]{2,1,0:T(8,128)(2,1)}, u32[]{:S(2)}, u32[]{:S(2)}) %all-to-all-start) | async-done | bytes 1048608 | tf_op jit(solution)/shard_map/all_to_all | solution.py:264
  77.7 1.0 copy-done.5
  78.7 2.8 %span_filter.2 = bf16[32,80,512]{2,1,0:T(8,128)(2,1)S(1)} custom-call(s32[32]{0:T(128)S(1)} %bitcast.5, s32[32]{0:T(128)S(1)} %convert_reduce_fusion.slot_ref, bf16[2,2,256,256]{3,2,1,0:T(8,128)(2,1)S(1)} %copy-done.5, f32[3,16,1]{2,1,0:T(8,128)S(1)} %copy.16.rms_ref, bf16[32,16,1024]{2,1,0:T(8,128)(2,1)} %all-to-all-done.x_ref, ...), custom_call_target="tpu_custom_call", output_to_operand_aliasing={{}: (5, {})} | custom-call | tf_op jit(solution)/shard_map/span_filter/pallas_call | solution.py:200
  81.5 0.0 copy-start.6
  81.5 38.6 %all_to_all.15.x_ref = bf16[32,80,512]{2,1,0:T(8,128)(2,1)S(1)} all-to-all(bf16[32,80,512]{2,1,0:T(8,128)(2,1)S(1)} %span_filter.2), channel_id=1, replica_groups=mesh['span'=32,'chan'=4] {'span'}, dimensions={0} | all-to-all | bytes 5242880 | tf_op jit(solution)/shard_map/all_to_all | solution.py:264
  120.1 2.3 %span_filter.3 = bf16[32,32,512]{2,1,0:T(8,128)(2,1)} custom-call(s32[32]{0:T(128)S(1)} %bitcast.6, s32[32]{0:T(128)S(1)} %convert_reduce_fusion.slot_ref, bf16[2,2,256,256]{3,2,1,0:T(8,128)(2,1)S(1)} %copy-done.6, f32[3,16,1]{2,1,0:T(8,128)S(1)} %copy.16.rms_ref, bf16[32,80,512]{2,1,0:T(8,128)(2,1)S(1)} %all_to_all.15.x_ref), custom_call_target="tpu_custom_call" | custom-call | tf_op jit(solution)/shard_map/span_filter/pallas_call | solution.py:200
  122.3 1.5 %copy-done.1 = bf16[32,80,512]{2,1,0:T(8,128)(2,1)} copy-done((bf16[32,80,512]{2,1,0:T(8,128)(2,1)}, bf16[32,80,512]{2,1,0:T(8,128)(2,1)S(1)}, u32[]{:S(2)}) %copy-start.1) | copy-done | bytes 2621464
  123.8 4.0 %all-to-all-start.2 = ((bf16[32,32,512]{2,1,0:T(8,128)(2,1)}), bf16[32,32,512]{2,1,0:T(8,128)(2,1)S(1)}, u32[]{:S(2)}, u32[]{:S(2)}) async-start(bf16[32,32,512]{2,1,0:T(8,128)(2,1)} %span_filter.3), calls=%async_computation.2 | async-start | bytes 2097152 | tf_op jit(solution)/shard_map/all_to_all | solution.py:264
  127.9 0.0 copy-start.2
  127.9 1.7 %copy-done.2 = bf16[32,80,512]{2,1,0:T(8,128)(2,1)S(1)} copy-done((bf16[32,80,512]{2,1,0:T(8,128)(2,1)S(1)}, bf16[32,80,512]{2,1,0:T(8,128)(2,1)}, u32[]{:S(2)}) %copy-start.2) | copy-done | bytes 2621464
  129.6 4.9 %inlet_tiles.2.refs_0_ = f32[1,32,2,8,3,16,64]{6,5,4,3,2,1,0:T(8,128)} custom-call(bf16[32,80,512]{2,1,0:T(8,128)(2,1)S(1)} %copy-done.2), custom_call_target="tpu_custom_call" | custom-call | tf_op jit(solution)/shard_map/inlet_tiles/pallas_call | solution.py:225
  134.5 10.6 %all-to-all-done.2.x_ref = bf16[32,32,512]{2,1,0:T(8,128)(2,1)S(1)} async-done(((bf16[32,32,512]{2,1,0:T(8,128)(2,1)}), bf16[32,32,512]{2,1,0:T(8,128)(2,1)S(1)}, u32[]{:S(2)}, u32[]{:S(2)}) %all-to-all-start.2) | async-done | bytes 1048608 | tf_op jit(solution)/shard_map/all_to_all | solution.py:264
  145.2 2.6 %inlet_tiles.3 = f32[1,32,2,8,3,16,64]{6,5,4,3,2,1,0:T(8,128)} custom-call(bf16[32,32,512]{2,1,0:T(8,128)(2,1)S(1)} %all-to-all-done.2.x_ref, f32[1,32,2,8,3,16,64]{6,5,4,3,2,1,0:T(8,128)} %inlet_tiles.2.refs_0_), custom_call_target="tpu_custom_call", output_to_operand_aliasing={{}: (1, {})} | custom-call | tf_op jit(solution)/shard_map/inlet_tiles/pallas_call | solution.py:225
  (23 shorter events, 0.1 us)
Async XLA Ops:
  0.0 8.8 %copy-start = (f32[3,512]{1,0:T(4,128)S(1)}, f32[3,512]{1,0:T(4,128)}, u32[]{:S(2)}) copy-start(f32[3,512]{1,0:T(4,128)} %param.11) | copy-start | bytes 18436
  0.0 8.7 %copy-start.14 = (s32[512]{0:T(512)S(1)}, s32[512]{0:T(512)}, u32[]{:S(2)}) copy-start(s32[512]{0:T(512)} %param.10) | copy-start | bytes 6148
  4.7 14.2 %collective-permute-start = (bf16[8,1,64,512]{3,2,1,0:T(8,128)(2,1)}, bf16[8,1,64,512]{3,2,1,0:T(8,128)(2,1)S(1)}, u32[]{:S(2)}, u32[]{:S(2)}) collective-permute-start(bf16[8,1,64,512]{3,2,1,0:T(8,128)(2,1)} %get-tuple-element.26), channel_id=1, source_target_pairs={{0,1},{1,0},{2,3},{3,2},{4,5},{5,4},{6,7},{7,6},{8,9},{9,8},{10,11... | collective-permute-start | bytes 1572872 | tf_op jit(solution)/shard_map/ppermute | solution.py:242
  6.8 14.0 %collective-permute-start.1 = (bf16[8,1,64,512]{3,2,1,0:T(8,128)(2,1)}, bf16[8,1,64,512]{3,2,1,0:T(8,128)(2,1)}, u32[]{:S(2)}, u32[]{:S(2)}) collective-permute-start(bf16[8,1,64,512]{3,2,1,0:T(8,128)(2,1)} %get-tuple-element.27), channel_id=1, source_target_pairs={{1,2},{2,1},{3,0},{0,3},{5,6},{6,5},{7,4},{4,7},{9,10},{10,9},{11,... | collective-permute-start | bytes 1572872 | tf_op jit(solution)/shard_map/ppermute | solution.py:242
  13.5 4.8 %copy-start.7 = (s32[32,1]{0,1:T(1,128)S(1)}, s32[32,1]{0,1:T(1,128)}, u32[]{:S(2)}) copy-start(s32[32,1]{0,1:T(1,128)} %param.12) | copy-start | bytes 388
  13.5 7.2 %copy-start.16 = (bf16[8,1,64,512]{3,2,1,0:T(8,128)(2,1)S(1)}, bf16[8,1,64,512]{3,2,1,0:T(8,128)(2,1)}, u32[]{:S(2)}) copy-start(bf16[8,1,64,512]{3,2,1,0:T(8,128)(2,1)} %get-tuple-element.35) | copy-start | bytes 1572868
  13.6 7.2 %copy-start.15 = (bf16[8,1,64,512]{3,2,1,0:T(8,128)(2,1)S(1)}, bf16[8,1,64,512]{3,2,1,0:T(8,128)(2,1)}, u32[]{:S(2)}) copy-start(bf16[8,1,64,512]{3,2,1,0:T(8,128)(2,1)} %get-tuple-element.36) | copy-start | bytes 1572868
  13.6 9.2 %copy-start.12 = (f32[8,1,64,512]{3,2,1,0:T(8,128)S(1)}, f32[8,1,64,512]{3,2,1,0:T(8,128)}, u32[]{:S(2)}) copy-start(f32[8,1,64,512]{3,2,1,0:T(8,128)} %get-tuple-element.38) | copy-start | bytes 3145732
  18.4 15.3 %copy-start.13 = (f32[8,1,64,512]{3,2,1,0:T(8,128)S(1)}, f32[8,1,64,512]{3,2,1,0:T(8,128)}, u32[]{:S(2)}) copy-start(f32[8,1,64,512]{3,2,1,0:T(8,128)} %get-tuple-element.28) | copy-start | bytes 3145732
  18.6 21.3 %copy-start.9 = (f32[8,1,64,512]{3,2,1,0:T(8,128)S(1)}, f32[8,1,64,512]{3,2,1,0:T(8,128)}, u32[]{:S(2)}) copy-start(f32[8,1,64,512]{3,2,1,0:T(8,128)} %get-tuple-element.37) | copy-start | bytes 3145732
  18.8 26.1 %copy-start.3 = (bf16[512,512]{1,0:T(8,128)(2,1)}, bf16[512,512]{1,0:T(8,128)(2,1)S(1)}, u32[]{:S(2)}) copy-start(bf16[512,512]{1,0:T(8,128)(2,1)S(1)} %get-tuple-element.54.high_ref) | copy-start | bytes 1572868
  20.8 11.6 %collective-permute-start.2 = (bf16[8,1,64,512]{3,2,1,0:T(8,128)(2,1)S(1)}, bf16[8,1,64,512]{3,2,1,0:T(8,128)(2,1)S(1)}, u32[]{:S(2)}, u32[]{:S(2)}) collective-permute-start(bf16[8,1,64,512]{3,2,1,0:T(8,128)(2,1)S(1)} %copy-done.16), channel_id=1, source_target_pairs={{0,1},{1,0},{2,3},{3,2},{4,5},{5,4},{6,7},{7,6},{8,9},{9,8},{10,11... | collective-permute-start | bytes 1572872 | tf_op jit(solution)/shard_map/ppermute | solution.py:242
  20.8 12.8 %collective-permute-start.4 = (bf16[8,1,64,512]{3,2,1,0:T(8,128)(2,1)S(1)}, bf16[8,1,64,512]{3,2,1,0:T(8,128)(2,1)S(1)}, u32[]{:S(2)}, u32[]{:S(2)}) collective-permute-start(bf16[8,1,64,512]{3,2,1,0:T(8,128)(2,1)S(1)} %copy-done.15), channel_id=1, source_target_pairs={{1,2},{2,1},{3,0},{0,3},{5,6},{6,5},{7,4},{4,7},{9,10},{10,9},{11,... | collective-permute-start | bytes 1572872 | tf_op jit(solution)/shard_map/ppermute | solution.py:242
  23.9 14.1 %collective-permute-start.7 = (f16[4,1,64,512]{3,2,1,0:T(8,128)(2,1)S(1)}, f16[4,1,64,512]{3,2,1,0:T(8,128)(2,1)S(1)}, u32[]{:S(2)}, u32[]{:S(2)}) collective-permute-start(f16[4,1,64,512]{3,2,1,0:T(8,128)(2,1)S(1)} %get-tuple-element.47), channel_id=1, source_target_pairs={{0,1},{1,0},{2,3},{3,2},{4,5},{5,4},{6,7},{7,6},{8,9},{9,8},{10,11... | collective-permute-start | bytes 786440 | tf_op jit(solution)/shard_map/ppermute | solution.py:253
  24.8 15.1 %collective-permute-start.6 = (f16[4,1,64,512]{3,2,1,0:T(8,128)(2,1)S(1)}, f16[4,1,64,512]{3,2,1,0:T(8,128)(2,1)S(1)}, u32[]{:S(2)}, u32[]{:S(2)}) collective-permute-start(f16[4,1,64,512]{3,2,1,0:T(8,128)(2,1)S(1)} %get-tuple-element.48), channel_id=1, source_target_pairs={{1,2},{2,1},{3,0},{0,3},{5,6},{6,5},{7,4},{4,7},{9,10},{10,9},{11,... | collective-permute-start | bytes 786440 | tf_op jit(solution)/shard_map/ppermute | solution.py:253
  33.8 9.8 %collective-permute-start.5 = (f16[4,1,64,512]{3,2,1,0:T(8,128)(2,1)S(1)}, f16[4,1,64,512]{3,2,1,0:T(8,128)(2,1)S(1)}, u32[]{:S(2)}, u32[]{:S(2)}) collective-permute-start(f16[4,1,64,512]{3,2,1,0:T(8,128)(2,1)S(1)} %get-tuple-element.51), channel_id=1, source_target_pairs={{0,1},{1,0},{2,3},{3,2},{4,5},{5,4},{6,7},{7,6},{8,9},{9,8},{10,11... | collective-permute-start | bytes 786440 | tf_op jit(solution)/shard_map/ppermute | solution.py:253
  33.9 10.8 %collective-permute-start.3 = (f16[4,1,64,512]{3,2,1,0:T(8,128)(2,1)S(1)}, f16[4,1,64,512]{3,2,1,0:T(8,128)(2,1)S(1)}, u32[]{:S(2)}, u32[]{:S(2)}) collective-permute-start(f16[4,1,64,512]{3,2,1,0:T(8,128)(2,1)S(1)} %get-tuple-element.52), channel_id=1, source_target_pairs={{1,2},{2,1},{3,0},{0,3},{5,6},{6,5},{7,4},{4,7},{9,10},{10,9},{11,... | collective-permute-start | bytes 786440 | tf_op jit(solution)/shard_map/ppermute | solution.py:253
  35.9 24.6 %collective-permute-start.8 = (bf16[8,1,64,512]{3,2,1,0:T(8,128)(2,1)}, bf16[8,1,64,512]{3,2,1,0:T(8,128)(2,1)}, u32[]{:S(2)}, u32[]{:S(2)}) collective-permute-start(bf16[8,1,64,512]{3,2,1,0:T(8,128)(2,1)} %get-tuple-element.39), channel_id=1, source_target_pairs={{0,1},{1,0},{2,3},{3,2},{4,5},{5,4},{6,7},{7,6},{8,9},{9,8},{10,11... | collective-permute-start | bytes 1572872 | tf_op jit(solution)/shard_map/ppermute | solution.py:242
  38.0 22.5 %collective-permute-start.10 = (bf16[8,1,64,512]{3,2,1,0:T(8,128)(2,1)}, bf16[8,1,64,512]{3,2,1,0:T(8,128)(2,1)}, u32[]{:S(2)}, u32[]{:S(2)}) collective-permute-start(bf16[8,1,64,512]{3,2,1,0:T(8,128)(2,1)} %get-tuple-element.40), channel_id=1, source_target_pairs={{1,2},{2,1},{3,0},{0,3},{5,6},{6,5},{7,4},{4,7},{9,10},{10,9},{11,... | collective-permute-start | bytes 1572872 | tf_op jit(solution)/shard_map/ppermute | solution.py:242
  39.9 4.8 %copy-start.10 = (f32[8,1,64,512]{3,2,1,0:T(8,128)S(1)}, f32[8,1,64,512]{3,2,1,0:T(8,128)}, u32[]{:S(2)}) copy-start(f32[8,1,64,512]{3,2,1,0:T(8,128)} %get-tuple-element.23) | copy-start | bytes 3145732
  44.9 15.6 %copy-start.11 = (f32[8,1,64,512]{3,2,1,0:T(8,128)S(1)}, f32[8,1,64,512]{3,2,1,0:T(8,128)}, u32[]{:S(2)}) copy-start(f32[8,1,64,512]{3,2,1,0:T(8,128)} %get-tuple-element.31) | copy-start | bytes 3145732
  46.7 23.9 %copy-start.8 = (f32[8,1,64,512]{3,2,1,0:T(8,128)S(1)}, f32[8,1,64,512]{3,2,1,0:T(8,128)}, u32[]{:S(2)}) copy-start(f32[8,1,64,512]{3,2,1,0:T(8,128)} %get-tuple-element.32) | copy-start | bytes 3145732
  46.7 30.9 %all-to-all-start = ((bf16[32,16,1024]{2,1,0:T(8,128)(2,1)}), bf16[32,16,1024]{2,1,0:T(8,128)(2,1)}, u32[]{:S(2)}, u32[]{:S(2)}) async-start(bf16[32,16,1024]{2,1,0:T(8,128)(2,1)} %vertical_filter.4), calls=%async_computation | async-start | bytes 2097152 | tf_op jit(solution)/shard_map/all_to_all | solution.py:264
  61.7 7.8 %collective-permute-start.11 = (f16[4,1,64,512]{3,2,1,0:T(8,128)(2,1)S(1)}, f16[4,1,64,512]{3,2,1,0:T(8,128)(2,1)S(1)}, u32[]{:S(2)}, u32[]{:S(2)}) collective-permute-start(f16[4,1,64,512]{3,2,1,0:T(8,128)(2,1)S(1)} %get-tuple-element.43), channel_id=1, source_target_pairs={{0,1},{1,0},{2,3},{3,2},{4,5},{5,4},{6,7},{7,6},{8,9},{9,8},{10,11... | collective-permute-start | bytes 786440 | tf_op jit(solution)/shard_map/ppermute | solution.py:253
  62.0 8.6 %collective-permute-start.9 = (f16[4,1,64,512]{3,2,1,0:T(8,128)(2,1)S(1)}, f16[4,1,64,512]{3,2,1,0:T(8,128)(2,1)S(1)}, u32[]{:S(2)}, u32[]{:S(2)}) collective-permute-start(f16[4,1,64,512]{3,2,1,0:T(8,128)(2,1)S(1)} %get-tuple-element.44), channel_id=1, source_target_pairs={{1,2},{2,1},{3,0},{0,3},{5,6},{6,5},{7,4},{4,7},{9,10},{10,9},{11,... | collective-permute-start | bytes 786440 | tf_op jit(solution)/shard_map/ppermute | solution.py:253
  71.8 1.0 copy-start.4
  77.7 1.0 copy-start.5
  81.5 38.6 %copy-start.6 = (bf16[2,2,256,256]{3,2,1,0:T(8,128)(2,1)S(1)}, bf16[2,2,256,256]{3,2,1,0:T(8,128)(2,1)}, u32[]{:S(2)}) copy-start(bf16[2,2,256,256]{3,2,1,0:T(8,128)(2,1)} %constant.41.clone.taps_ref) | copy-start | bytes 1572868
  122.3 1.5 %copy-start.1 = (bf16[32,80,512]{2,1,0:T(8,128)(2,1)}, bf16[32,80,512]{2,1,0:T(8,128)(2,1)S(1)}, u32[]{:S(2)}) copy-start(bf16[32,80,512]{2,1,0:T(8,128)(2,1)S(1)} %all_to_all.15.x_ref) | copy-start | bytes 7864324
  123.8 21.3 %all-to-all-start.2 = ((bf16[32,32,512]{2,1,0:T(8,128)(2,1)}), bf16[32,32,512]{2,1,0:T(8,128)(2,1)S(1)}, u32[]{:S(2)}, u32[]{:S(2)}) async-start(bf16[32,32,512]{2,1,0:T(8,128)(2,1)} %span_filter.3), calls=%async_computation.2 | async-start | bytes 2097152 | tf_op jit(solution)/shard_map/all_to_all | solution.py:264
  127.9 1.7 %copy-start.2 = (bf16[32,80,512]{2,1,0:T(8,128)(2,1)S(1)}, bf16[32,80,512]{2,1,0:T(8,128)(2,1)}, u32[]{:S(2)}) copy-start(bf16[32,80,512]{2,1,0:T(8,128)(2,1)} %copy-done.1) | copy-start | bytes 7864324

commit v2 on v1

--- a/solution.py
+++ b/solution.py
@@ -65,18 +65,15 @@
     return high, (values - high.astype(np.float32)).astype(ml_dtypes.bfloat16)
 
 
-def span_blocks():
+def span_bands():
     taps = gaussian(np.arange(KY) - KY // 2.0, KY / 4.0)
     taps = taps / np.sqrt(np.sum(taps**2))
-    blocks = np.zeros((4, 2, TY, 2, 2, TY), np.float32)
-    for source in range(4):
-        for target in range(2):
-            shift = TY * (source - 1 - target)
-            tap = np.arange(TY)[:, None] + shift - np.arange(TY)[None, :] + KY // 2
-            band = np.where((tap >= 0) & (tap < KY), taps[np.clip(tap, 0, KY - 1)], 0.0)
-            for step in range(2):
-                blocks[source, step, :, target, step, :] = band
-    return np.stack(split(blocks.reshape(2, 4 * TY, 4 * TY)))
+    bands = np.zeros((3, 2, TY, 2, TY), np.float32)
+    for shift in range(3):
+        tap = np.arange(TY)[:, None] + TY * (shift - 1) - np.arange(TY)[None, :] + KY // 2
+        for step in range(2):
+            bands[shift, step, :, step, :] = np.where((tap >= 0) & (tap < KY), taps[np.clip(tap, 0, KY - 1)], 0.0)
+    return np.stack(split(bands.reshape(3, 2, TY, LANES)))
 
 
 def vertical_filter_matrix(widths):
@@ -96,38 +93,32 @@
     )
 
 
-def time_kernel(chan_ref, taps_ref, noise_ref, to_a_ref, to_b_ref, kept_ref, own_ref):
+def time_kernel(chan_ref, taps_ref, noise_ref, *out_refs):
     for first in range(0, BLOCK, ROWS):
         rows = slice(first, first + ROWS)
         planes = noise_ref[:, :, rows].reshape(PLANES * ROWS, Z)
         sums = jnp.dot(taps_ref[0], planes, preferred_element_type=jnp.float32)
-        sums = sums.reshape(CHANS * STEPS, 1, ROWS, Z)
-        to_a_ref[:, :, rows] = sums[:8].astype(jnp.bfloat16)
-        to_b_ref[:, :, rows] = sums[8:16].astype(jnp.bfloat16)
-        kept_ref[:, :, rows] = sums[16:24]
-        own_ref[:, :, rows] = sums[24:]
-
-
-def time_filter(noise, chan, comp):
-    part = pl.BlockSpec((STEPS, 1, BLOCK, Z), lambda j, chan: (0, 0, j, 0))
-    shape = (STEPS, 1, TY, Z)
+        sums = sums.reshape(2, STEPS, 1, ROWS, Z)
+        for block, out_ref in enumerate(out_refs):
+            out_ref[:, :, rows] = sums[block].astype(out_ref.dtype)
+
+
+def time_filter(noise, chan, comp, leaving):
+    out = pl.BlockSpec((STEPS, 1, BLOCK, Z), lambda j, chan: (0, 0, j, 0))
+    part = 0 if leaving else 1
+    kind = jnp.bfloat16 if leaving else jnp.float32
     return pl.pallas_call(
         time_kernel,
         grid_spec=pltpu.PrefetchScalarGridSpec(
             num_scalar_prefetch=1,
             grid=(TY // BLOCK,),
             in_specs=[
-                pl.BlockSpec((1, CHANS * STEPS * ROWS, PLANES * ROWS), lambda j, chan: (chan[0], 0, 0)),
+                pl.BlockSpec((1, 2 * STEPS * ROWS, PLANES * ROWS), lambda j, chan: (chan[0], part, 0)),
                 pl.BlockSpec((1, PLANES, BLOCK, Z), lambda j, chan: (comp, 0, j, 0)),
             ],
-            out_specs=[part] * 4,
+            out_specs=[out] * 2,
         ),
-        out_shape=[
-            jax.ShapeDtypeStruct(shape, jnp.bfloat16),
-            jax.ShapeDtypeStruct(shape, jnp.bfloat16),
-            jax.ShapeDtypeStruct(shape, jnp.float32),
-            jax.ShapeDtypeStruct(shape, jnp.float32),
-        ],
+        out_shape=[jax.ShapeDtypeStruct((STEPS, 1, TY, Z), kind)] * 2,
         compiler_params=pltpu.CompilerParams(vmem_limit_bytes=TIME_VMEM),
         name="time_filter",
     )(chan, time_blocks(), noise)
@@ -164,8 +155,26 @@
     )(*taps, *sums, *([] if so_far is None else [so_far]))
 
 
-def span_kernel(owner_ref, slot_ref, taps_ref, rms_ref, x_ref, *refs):
-    out_ref = refs[-1]
+def span_kernel(keep, owner_ref, slot_ref, bands_ref, rms_ref, x_ref, *refs):
+    if keep:
+        whole_ref, out_ref, kept_ref, taps_ref, sem = refs
+        copy = pltpu.make_async_copy(whole_ref.at[:, : kept_ref.shape[1]], kept_ref, sem)
+        copy.start()
+    else:
+        out_ref, taps_ref, sem = refs[-3:]
+
+    @pl.when(pl.program_id(0) == 0)
+    def _():
+        for part in range(2):
+            for source in range(4):
+                for step in range(2):
+                    rows = pl.ds((source % 2) * LANES + step * TY, TY)
+                    for target in range(2):
+                        shift = source - target
+                        columns = pl.ds(target * LANES, LANES)
+                        band = bands_ref[part, shift, step] if 0 <= shift < 3 else jnp.zeros((TY, LANES), jnp.bfloat16)
+                        taps_ref[part, source // 2, rows, columns] = band
+
     out_ref[...] = jnp.zeros_like(out_ref)
     pairs = SPANS // 2
     for first in range(0, WIDTH, LANES):
@@ -184,29 +193,41 @@
             target = (i % 2) * LANES
             rows = pl.ds(pl.multiple_of(slot_ref[i] * ZD, ZD), ZD)
             out_ref[owner_ref[i], rows, lanes] = velocity[i // 2, :, target : target + LANES]
-
-
-def span_filter(owner, slot, rms, moved, place, first, comps, shape, so_far=None):
+    if keep:
+        copy.wait()
+
+
+def span_filter(owner, slot, rms, moved, place, first, comps, shape, so_far=None, keep=0):
     row, column = place
     in_specs = [
         pl.BlockSpec(memory_space=pltpu.SMEM),
         pl.BlockSpec(memory_space=pltpu.SMEM),
-        pl.BlockSpec((2, 2, 2 * LANES, 2 * LANES), lambda i: (0, 0, 0, 0)),
+        pl.BlockSpec((2, 3, 2, TY, LANES), lambda i: (0, 0, 0, 0, 0)),
         pl.BlockSpec((1, ZD, 1), lambda i: (first + i, 0, 0)),
         pl.BlockSpec((SPANS, ZD, WIDTH), lambda i: (0, row, column + i)),
     ]
+    out_specs = [pl.BlockSpec((SPANS, CAP * ZD, WIDTH), lambda i: (0, i, 0))]
+    out_shape = [jax.ShapeDtypeStruct(shape, jnp.bfloat16)]
+    more = []
     if so_far is not None:
         in_specs.append(pl.BlockSpec(memory_space=pl.ANY))
+        more.append(so_far)
+    if keep:
+        in_specs.append(pl.BlockSpec(memory_space=pl.ANY))
+        more.append(moved)
+        out_specs.append(pl.BlockSpec(memory_space=pl.ANY))
+        out_shape.append(jax.ShapeDtypeStruct((SPANS, keep, WIDTH), jnp.bfloat16))
     return pl.pallas_call(
-        span_kernel,
+        functools.partial(span_kernel, keep > 0),
         grid=(comps,),
         in_specs=in_specs,
-        out_specs=pl.BlockSpec((SPANS, CAP * ZD, WIDTH), lambda i: (0, i, 0)),
-        out_shape=jax.ShapeDtypeStruct(shape, jnp.bfloat16),
+        out_specs=out_specs,
+        out_shape=out_shape,
         input_output_aliases={} if so_far is None else {5: 0},
+        scratch_shapes=[pltpu.VMEM((2, 2, 2 * LANES, 2 * LANES), jnp.bfloat16), pltpu.SemaphoreType.DMA],
         compiler_params=pltpu.CompilerParams(vmem_limit_bytes=VMEM),
         name="span_filter",
-    )(owner, slot, span_blocks(), rms, moved, *([] if so_far is None else [so_far]))
+    )(owner, slot, span_bands(), rms, moved, *more)
 
 
 def inlet_kernel(x_ref, *refs):
@@ -235,7 +256,7 @@
 
 
 def after(values, others):
-    return lax.optimization_barrier((*values, *others))[: len(values)]
+    return lax.optimization_barrier((*values, *others))[: len(values)] if others else values
 
 
 def first_exchange(to_a, to_b):
@@ -276,15 +297,22 @@
     earlier = (owner[:, None] == owner[None, :]) & (tile[None, :] < tile[:, None])
     slot = jnp.sum(earlier.astype(jnp.int32), axis=1)
 
-    partial = [time_filter(noise, chan, c) for c in range(COMPS)]
-    early = (*partial[1], *partial[2], *taps, owner, slot, rms)
-    sums, got = [], None
-    for to_a, to_b, kept, own in partial:
-        if got is None:
-            got = after(first_exchange(to_a, to_b), early)
-        else:
-            got = first_exchange(*after((to_a, to_b), got))
-        sums.append(summed(own, *got, *second_exchange(*for_second_exchange(kept, *got))))
+    leave0, leave1 = [time_filter(noise, chan, c, True) for c in range(2)]
+    stay0 = time_filter(noise, chan, 0, False)
+    got0 = after(first_exchange(*leave0), (*leave1, *stay0, *taps, owner, slot, rms))
+    got1 = first_exchange(*after(leave1, got0))
+    sends0 = for_second_exchange(stay0[0], *got0)
+    (chan,) = after((chan,), sends0)
+    stay1, stay2 = [time_filter(noise, chan, c, False) for c in (1, 2)]
+    leave2 = time_filter(noise, chan, 2, True)
+    got1 = after(got1, (*stay1, *stay2, *leave2))
+    sends1 = for_second_exchange(stay1[0], *got1)
+    got2 = first_exchange(*after(leave2, sends1))
+    sends2 = for_second_exchange(stay2[0], *got2)
+    sums = [
+        summed(stay[1], *got, *second_exchange(*sends))
+        for stay, got, sends in ((stay0, got0, sends0), (stay1, got1, sends1), (stay2, got2, sends2))
+    ]
 
     planes = None
     for c in range(2):
@@ -292,10 +320,11 @@
     moved = along_span(planes)
     shape = (SPANS, 2 * CAP * ZD + ZD, WIDTH)
     mixed = vertical_filter(taps, sums[2], shape, (0, 2 * CAP, 0))
-    mixed = along_span(span_filter(owner, slot, rms, moved, (0, 0), 0, 2, shape, mixed))
-    last = span_filter(owner, slot, rms, mixed, (2 * CAP, 0), 2, 1, (SPANS, CAP * ZD, WIDTH))
-    last = along_span(last)
-    return inlet_tiles(last, 2, 1, inlet_tiles(mixed, 0, 2))
+    mixed = along_span(span_filter(owner, slot, rms, moved, (0, 0), 0, 2, shape, mixed)[0])
+    last, tiles = span_filter(
+        owner, slot, rms, mixed, (2 * CAP, 0), 2, 1, (SPANS, CAP * ZD, WIDTH), keep=2 * CAP * ZD
+    )
+    return inlet_tiles(along_span(last), 2, 1, inlet_tiles(tiles, 0, 2))
 
 
 def solution(mesh):

time: 148 us -> 146 us (0.986)
  waiting for transfers between devices: 34 us -> 27.9 us
  Pallas kernels: 31.2 us -> 37.2 us
  local copies, waits for them, and re-layouts: 5.53 us -> 2.22 us
    pallas_call x3 -> x6, Pallas kernels: 14.1 us -> 20.7 us  [time_filter(): pl.pallas_call(time_kernel, grid_spec=pltpu.PrefetchScalarGridSpec(num_sc...]
    ppermute x3, waiting for transfers between devices: 6.81 us -> 1.84 us  [first_exchange(): lax.ppermute(to_a, 'chan', PAIR_A)]
    unnamed x34 -> x26, local copies, waits for them, and re-layouts: 5.36 us -> 2.04 us
    ppermute x3, waiting for transfers between devices: 7.37 us -> 5.38 us  [second_exchange(): lax.ppermute(for_a, 'chan', PAIR_A)]
    all_to_all x2, waiting for transfers between devices: 14.4 us -> 16 us  [along_span(): lax.all_to_all(values, 'span', split_axis=0, concat_axis=0, tiled=True)]
    convert_element_type x3, other arithmetic: 2.5 us -> 4.04 us  [for_second_exchange(): (kept[half:] + from_b[half:].astype(jnp.float32)).astype(jnp.float16)]
    all_to_all x2, starting transfers between devices: 17.7 us -> 19.3 us  [along_span(): lax.all_to_all(values, 'span', split_axis=0, concat_axis=0, tiled=True)]
  transfers between devices with their start and end apart: 14 -> 14, of which waited for: 10 -> 7; matrix products, arithmetic and copies ran while one was open for 4% -> 5% of each run, Pallas kernels for 13% -> 19%
where the time goes in v2:
time: 146 us; the launch traced here: 145 us
  blocking collectives  38.6 us (26%)
  Pallas kernels  37.2 us (25%)
  starting transfers between devices  32.8 us (22%)
  waiting for transfers between devices  27.9 us (19%)
  other arithmetic  6.36 us (4%)
  local copies, waits for them, and re-layouts  2.22 us (2%)
    all_to_all x1, blocking collectives, along_span(): lax.all_to_all(values, 'span', split_axis=0, concat_axis=0, tiled=True)  38.6 us
    pallas_call x6, Pallas kernels, time_filter(): pl.pallas_call(time_kernel, grid_spec=pltpu.PrefetchScalarGridSpec(num_sc...  20.7 us
    all_to_all x2, starting transfers between devices, along_span(): lax.all_to_all(values, 'span', split_axis=0, concat_axis=0, tiled=True)  19.3 us
    all_to_all x2, waiting for transfers between devices, along_span(): lax.all_to_all(values, 'span', split_axis=0, concat_axis=0, tiled=True)  16 us
    pallas_call x2, Pallas kernels, inlet_tiles(): pl.pallas_call(inlet_kernel, grid=(comps, SPANS // block), in_specs=in_sp...  7.45 us
    ppermute x3, waiting for transfers between devices, second_exchange(): lax.ppermute(for_a, 'chan', PAIR_A)  5.38 us
    ppermute x3, starting transfers between devices, first_exchange(): lax.ppermute(to_b, 'chan', PAIR_B)  4.66 us
    pallas_call x3, Pallas kernels, vertical_filter(): pl.pallas_call(vertical_kernel, grid=(1,), in_specs=in_specs, out_specs=p...  4.63 us
  transfers between devices with their start and end apart: 14, of which 7 were waited for; matrix products, arithmetic and copies ran while one was open for 5% of the time, Pallas kernels for 19%

profile of v2, /device:TPU:1, one launch (start us, length us, event | category | flops | bytes accessed | tf_op | source)
XLA Modules:
  0.0 145.3 jit_solution(13472042831510736476)
XLA Ops:
  0.0 0.0 copy-start
  0.0 3.4 %time_filter.7 = (bf16[8,1,64,512]{3,2,1,0:T(8,128)(2,1)}, bf16[8,1,64,512]{3,2,1,0:T(8,128)(2,1)}) custom-call(s32[1]{0:T(128)} %bitcast.2.chan_ref, bf16[4,512,640]{2,1,0:T(8,128)(2,1)} %constant.40.clone.taps_ref, bf16[3,40,64,512]{3,2,1,0:T(8,128)(2,1)} %noise_ref.11), custom_call_target="tpu_custom_call" | custom-call | tf_op jit(solution)/shard_map/time_filter/pallas_call | solution.py:110
  3.4 2.1 %collective-permute-start = (bf16[8,1,64,512]{3,2,1,0:T(8,128)(2,1)}, bf16[8,1,64,512]{3,2,1,0:T(8,128)(2,1)S(1)}, u32[]{:S(2)}, u32[]{:S(2)}) collective-permute-start(bf16[8,1,64,512]{3,2,1,0:T(8,128)(2,1)} %get-tuple-element.29), channel_id=1, source_target_pairs={{0,1},{1,0},{2,3},{3,2},{4,5},{5,4},{6,7},{7,6},{8,9},{9,8},{10,11... | collective-permute-start | bytes 1572872 | tf_op jit(solution)/shard_map/ppermute | solution.py:263
  5.5 1.9 %collective-permute-start.1 = (bf16[8,1,64,512]{3,2,1,0:T(8,128)(2,1)}, bf16[8,1,64,512]{3,2,1,0:T(8,128)(2,1)S(1)}, u32[]{:S(2)}, u32[]{:S(2)}) collective-permute-start(bf16[8,1,64,512]{3,2,1,0:T(8,128)(2,1)} %get-tuple-element.30), channel_id=1, source_target_pairs={{1,2},{2,1},{3,0},{0,3},{5,6},{6,5},{7,4},{4,7},{9,10},{10,9},{11,... | collective-permute-start | bytes 1572872 | tf_op jit(solution)/shard_map/ppermute | solution.py:263
  7.4 0.0 copy-done.10
  7.4 0.1 fusion.9
  7.5 0.0 copy-done
  7.5 0.1 dynamic-slice_bitcast_fusion
  7.6 3.4 %time_filter.8 = (bf16[8,1,64,512]{3,2,1,0:T(8,128)(2,1)}, bf16[8,1,64,512]{3,2,1,0:T(8,128)(2,1)}) custom-call(s32[1]{0:T(128)} %bitcast.2.chan_ref, bf16[4,512,640]{2,1,0:T(8,128)(2,1)} %constant.40.clone.taps_ref, bf16[3,40,64,512]{3,2,1,0:T(8,128)(2,1)} %noise_ref.11), custom_call_target="tpu_custom_call" | custom-call | tf_op jit(solution)/shard_map/time_filter/pallas_call | solution.py:110
  11.0 3.6 %time_filter.6 = (f32[8,1,64,512]{3,2,1,0:T(8,128)}, f32[8,1,64,512]{3,2,1,0:T(8,128)}) custom-call(s32[1]{0:T(128)} %bitcast.2.chan_ref, bf16[4,512,640]{2,1,0:T(8,128)(2,1)} %constant.40.clone.taps_ref, bf16[3,40,64,512]{3,2,1,0:T(8,128)(2,1)} %noise_ref.11), custom_call_target="tpu_custom_call" | custom-call | tf_op jit(solution)/shard_map/time_filter/pallas_call | solution.py:110
  14.6 0.0 copy-done.5
  14.6 0.2 convert_reduce_fusion.slot_ref
  14.8 0.3 fusion
  15.1 0.0 copy-start.1
  15.1 1.8 %collective-permute-done = bf16[8,1,64,512]{3,2,1,0:T(8,128)(2,1)S(1)} collective-permute-done((bf16[8,1,64,512]{3,2,1,0:T(8,128)(2,1)}, bf16[8,1,64,512]{3,2,1,0:T(8,128)(2,1)S(1)}, u32[]{:S(2)}, u32[]{:S(2)}) %collective-permute-start) | collective-permute-done | bytes 524320 | tf_op jit(solution)/shard_map/ppermute | solution.py:263
  16.9 2.4 %collective-permute-done.1 = bf16[8,1,64,512]{3,2,1,0:T(8,128)(2,1)S(1)} collective-permute-done((bf16[8,1,64,512]{3,2,1,0:T(8,128)(2,1)}, bf16[8,1,64,512]{3,2,1,0:T(8,128)(2,1)S(1)}, u32[]{:S(2)}, u32[]{:S(2)}) %collective-permute-start.1) | collective-permute-done | bytes 524320 | tf_op jit(solution)/shard_map/ppermute | solution.py:263
  19.4 0.0 copy-done.12
  19.4 0.0 collective-permute-start.2
  19.4 0.0 copy-done.11
  19.4 2.0 %collective-permute-start.3 = (bf16[8,1,64,512]{3,2,1,0:T(8,128)(2,1)S(1)}, bf16[8,1,64,512]{3,2,1,0:T(8,128)(2,1)S(1)}, u32[]{:S(2)}, u32[]{:S(2)}) collective-permute-start(bf16[8,1,64,512]{3,2,1,0:T(8,128)(2,1)S(1)} %copy-done.11), channel_id=1, source_target_pairs={{1,2},{2,1},{3,0},{0,3},{5,6},{6,5},{7,4},{4,7},{9,10},{10,9},{11,... | collective-permute-start | bytes 1572872 | tf_op jit(solution)/shard_map/ppermute | solution.py:263
  21.4 1.4 add_convert_fusion.4
  22.8 0.9 collective-permute-start.7
  23.6 0.8 collective-permute-start.6
  24.4 3.3 %time_filter.11 = (bf16[8,1,64,512]{3,2,1,0:T(8,128)(2,1)}, bf16[8,1,64,512]{3,2,1,0:T(8,128)(2,1)}) custom-call(s32[1]{0:T(128)} %bitcast.2.chan_ref, bf16[4,512,640]{2,1,0:T(8,128)(2,1)} %constant.40.clone.taps_ref, bf16[3,40,64,512]{3,2,1,0:T(8,128)(2,1)} %noise_ref.11), custom_call_target="tpu_custom_call" | custom-call | tf_op jit(solution)/shard_map/time_filter/pallas_call | solution.py:110
  27.7 3.5 %time_filter.10 = (f32[8,1,64,512]{3,2,1,0:T(8,128)}, f32[8,1,64,512]{3,2,1,0:T(8,128)}) custom-call(s32[1]{0:T(128)} %bitcast.2.chan_ref, bf16[4,512,640]{2,1,0:T(8,128)(2,1)} %constant.40.clone.taps_ref, bf16[3,40,64,512]{3,2,1,0:T(8,128)(2,1)} %noise_ref.11), custom_call_target="tpu_custom_call" | custom-call | tf_op jit(solution)/shard_map/time_filter/pallas_call | solution.py:110
  31.3 3.5 %time_filter.9 = (f32[8,1,64,512]{3,2,1,0:T(8,128)}, f32[8,1,64,512]{3,2,1,0:T(8,128)}) custom-call(s32[1]{0:T(128)} %bitcast.2.chan_ref, bf16[4,512,640]{2,1,0:T(8,128)(2,1)} %constant.40.clone.taps_ref, bf16[3,40,64,512]{3,2,1,0:T(8,128)(2,1)} %noise_ref.11), custom_call_target="tpu_custom_call" | custom-call | tf_op jit(solution)/shard_map/time_filter/pallas_call | solution.py:110
  34.8 0.0 collective-permute-done.2
  34.8 0.0 collective-permute-done.3
  34.8 1.5 %add_convert_fusion.2 = (f16[4,1,64,512]{3,2,1,0:T(8,128)(2,1)S(1)}, f16[4,1,64,512]{3,2,1,0:T(8,128)(2,1)S(1)}) fusion(f32[8,1,64,512]{3,2,1,0:T(8,128)} %get-tuple-element.40, bf16[8,1,64,512]{3,2,1,0:T(8,128)(2,1)S(1)} %collective-permute-done.3, bf16[8,1,64,512]{3,2,1,0:T(8,128)(2,1)S(1)} %collective-permute-done.2), kind=kLoop, calls=%fused_computation.19 | loop fusion | flops 786432 | bytes 2097152 | tf_op jit(solution)/shard_map/convert_element_type | solution.py:269
  36.3 0.2 collective-permute-start.5
  36.4 1.9 %collective-permute-start.4 = (f16[4,1,64,512]{3,2,1,0:T(8,128)(2,1)S(1)}, f16[4,1,64,512]{3,2,1,0:T(8,128)(2,1)S(1)}, u32[]{:S(2)}, u32[]{:S(2)}) collective-permute-start(f16[4,1,64,512]{3,2,1,0:T(8,128)(2,1)S(1)} %get-tuple-element.60), channel_id=1, source_target_pairs={{1,2},{2,1},{3,0},{0,3},{5,6},{6,5},{7,4},{4,7},{9,10},{10,9},{11,... | collective-permute-start | bytes 786440 | tf_op jit(solution)/shard_map/ppermute | solution.py:274
  38.4 0.8 collective-permute-start.8
  39.1 0.0 collective-permute-done.7
  39.1 0.8 collective-permute-start.10
  39.9 0.0 collective-permute-done.6
  39.9 0.2 convert_add_fusion.2
  40.1 1.8 %vertical_filter.3.refs_0_ = bf16[32,16,1024]{2,1,0:T(8,128)(2,1)} custom-call(bf16[512,512]{1,0:T(8,128)(2,1)S(1)} %get-tuple-element.64.high_ref, bf16[512,512]{1,0:T(8,128)(2,1)S(1)} %get-tuple-element.63.low_ref, f32[4,1,64,512]{3,2,1,0:T(8,128)S(1)} %get-tuple-element.56.first_ref, f32[4,1,64,512]{3,2,1,0:T(8,128)S(1)} %get-tuple-element.55.second_ref), custom_call_target="tpu_custom_call" | custom-call | tf_op jit(solution)/shard_map/vertical_filter/pallas_call | solution.py:146
  41.9 0.0 collective-permute-done.5
  42.0 0.9 collective-permute-done.4
  42.9 0.2 convert_add_fusion.4
  43.1 1.8 %vertical_filter.4 = bf16[32,16,1024]{2,1,0:T(8,128)(2,1)} custom-call(bf16[512,512]{1,0:T(8,128)(2,1)S(1)} %get-tuple-element.64.high_ref, bf16[512,512]{1,0:T(8,128)(2,1)S(1)} %get-tuple-element.63.low_ref, f32[4,1,64,512]{3,2,1,0:T(8,128)S(1)} %get-tuple-element.58.first_ref, ...), custom_call_target="tpu_custom_call", output_to_operand_aliasing={{}: (4, {})} | custom-call | tf_op jit(solution)/shard_map/vertical_filter/pallas_call | solution.py:146
  45.0 15.2 %all-to-all-start = ((bf16[32,16,1024]{2,1,0:T(8,128)(2,1)}), bf16[32,16,1024]{2,1,0:T(8,128)(2,1)}, u32[]{:S(2)}, u32[]{:S(2)}) async-start(bf16[32,16,1024]{2,1,0:T(8,128)(2,1)} %vertical_filter.4), calls=%async_computation | async-start | bytes 2097152 | tf_op jit(solution)/shard_map/all_to_all | solution.py:285
  60.2 0.0 collective-permute-done.8
  60.2 0.0 collective-permute-done.10
  60.2 1.2 add_convert_fusion
  61.4 0.4 collective-permute-start.11
  61.8 1.9 %collective-permute-start.9 = (f16[4,1,64,512]{3,2,1,0:T(8,128)(2,1)S(1)}, f16[4,1,64,512]{3,2,1,0:T(8,128)(2,1)S(1)}, u32[]{:S(2)}, u32[]{:S(2)}) collective-permute-start(f16[4,1,64,512]{3,2,1,0:T(8,128)(2,1)S(1)} %get-tuple-element.54), channel_id=1, source_target_pairs={{1,2},{2,1},{3,0},{0,3},{5,6},{6,5},{7,4},{4,7},{9,10},{10,9},{11,... | collective-permute-start | bytes 786440 | tf_op jit(solution)/shard_map/ppermute | solution.py:274
  63.7 0.1 copy.19.rms_ref
  63.8 5.4 %collective-permute-done.11 = f16[4,1,64,512]{3,2,1,0:T(8,128)(2,1)S(1)} collective-permute-done((f16[4,1,64,512]{3,2,1,0:T(8,128)(2,1)S(1)}, f16[4,1,64,512]{3,2,1,0:T(8,128)(2,1)S(1)}, u32[]{:S(2)}, u32[]{:S(2)}) %collective-permute-start.11) | collective-permute-done | bytes 262176 | tf_op jit(solution)/shard_map/ppermute | solution.py:274
  69.2 1.2 collective-permute-done.9
  70.4 0.0 copy-done.6
  70.4 1.3 convert_add_fusion
  71.7 0.0 copy-start.2
  71.7 1.0 copy-done.2
  72.8 1.0 vertical_filter.5.refs_0_
  73.8 3.6 %all-to-all-done.x_ref = bf16[32,16,1024]{2,1,0:T(8,128)(2,1)} async-done(((bf16[32,16,1024]{2,1,0:T(8,128)(2,1)}), bf16[32,16,1024]{2,1,0:T(8,128)(2,1)}, u32[]{:S(2)}, u32[]{:S(2)}) %all-to-all-start) | async-done | bytes 1048608 | tf_op jit(solution)/shard_map/all_to_all | solution.py:285
  77.4 2.8 %span_filter.2 = bf16[32,80,512]{2,1,0:T(8,128)(2,1)S(1)} custom-call(s32[32]{0:T(128)S(1)} %bitcast.5, s32[32]{0:T(128)S(1)} %convert_reduce_fusion.slot_ref, bf16[2,3,2,64,128]{4,3,2,1,0:T(8,128)(2,1)S(1)} %copy-done.4, f32[3,16,1]{2,1,0:T(8,128)S(1)} %copy.19.rms_ref, bf16[32,16,1024]{2,1,0:T(8,128)(2,1)} %all-to-all-done.x_ref, ...), custom_call_target="tpu_custom_call", output_to_operand_aliasing={{}: (5, {})} | custom-call | tf_op jit(solution)/shard_map/span_filter/pallas_call | solution.py:220
  80.3 38.6 %all_to_all.15.x_ref.refs_0_ = bf16[32,80,512]{2,1,0:T(8,128)(2,1)S(1)} all-to-all(bf16[32,80,512]{2,1,0:T(8,128)(2,1)S(1)} %span_filter.2), channel_id=1, replica_groups=mesh['span'=32,'chan'=4] {'span'}, dimensions={0} | all-to-all | bytes 5242880 | tf_op jit(solution)/shard_map/all_to_all | solution.py:285
  118.9 1.5 %span_filter.3 = (bf16[32,32,512]{2,1,0:T(8,128)(2,1)S(1)}, bf16[32,64,512]{2,1,0:T(8,128)(2,1)S(1)}) custom-call(s32[32]{0:T(128)S(1)} %bitcast.6, s32[32]{0:T(128)S(1)} %convert_reduce_fusion.slot_ref, bf16[2,3,2,64,128]{4,3,2,1,0:T(8,128)(2,1)S(1)} %copy-done.4, f32[3,16,1]{2,1,0:T(8,128)S(1)} %copy.19.rms_ref, ...), custom_call_target="tpu_custom_call" | custom-call | tf_op jit(solution)/shard_map/span_filter/pallas_call | solution.py:220
  120.4 1.0 copy-done.3
  121.4 4.0 %all-to-all-start.2 = ((bf16[32,32,512]{2,1,0:T(8,128)(2,1)}), bf16[32,32,512]{2,1,0:T(8,128)(2,1)S(1)}, u32[]{:S(2)}, u32[]{:S(2)}) async-start(bf16[32,32,512]{2,1,0:T(8,128)(2,1)} %copy-done.3), calls=%async_computation.2 | async-start | bytes 2097152 | tf_op jit(solution)/shard_map/all_to_all | solution.py:285
  125.4 4.9 %inlet_tiles.2.refs_0_ = f32[1,32,2,8,3,16,64]{6,5,4,3,2,1,0:T(8,128)} custom-call(bf16[32,64,512]{2,1,0:T(8,128)(2,1)S(1)} %get-tuple-element.50.x_ref), custom_call_target="tpu_custom_call" | custom-call | tf_op jit(solution)/shard_map/inlet_tiles/pallas_call | solution.py:246
  130.3 12.4 %all-to-all-done.2.x_ref = bf16[32,32,512]{2,1,0:T(8,128)(2,1)S(1)} async-done(((bf16[32,32,512]{2,1,0:T(8,128)(2,1)}), bf16[32,32,512]{2,1,0:T(8,128)(2,1)S(1)}, u32[]{:S(2)}, u32[]{:S(2)}) %all-to-all-start.2) | async-done | bytes 1048608 | tf_op jit(solution)/shard_map/all_to_all | solution.py:285
  142.7 2.6 %inlet_tiles.3 = f32[1,32,2,8,3,16,64]{6,5,4,3,2,1,0:T(8,128)} custom-call(bf16[32,32,512]{2,1,0:T(8,128)(2,1)S(1)} %all-to-all-done.2.x_ref, f32[1,32,2,8,3,16,64]{6,5,4,3,2,1,0:T(8,128)} %inlet_tiles.2.refs_0_), custom_call_target="tpu_custom_call", output_to_operand_aliasing={{}: (1, {})} | custom-call | tf_op jit(solution)/shard_map/inlet_tiles/pallas_call | solution.py:246
  (18 shorter events, 0.0 us)
Async XLA Ops:
  0.0 7.5 %copy-start = (f32[3,512]{1,0:T(4,128)S(1)}, f32[3,512]{1,0:T(4,128)}, u32[]{:S(2)}) copy-start(f32[3,512]{1,0:T(4,128)} %param.14) | copy-start | bytes 18436
  0.0 7.4 %copy-start.10 = (s32[512]{0:T(512)S(1)}, s32[512]{0:T(512)}, u32[]{:S(2)}) copy-start(s32[512]{0:T(512)} %param.13) | copy-start | bytes 6148
  3.4 13.6 %collective-permute-start = (bf16[8,1,64,512]{3,2,1,0:T(8,128)(2,1)}, bf16[8,1,64,512]{3,2,1,0:T(8,128)(2,1)S(1)}, u32[]{:S(2)}, u32[]{:S(2)}) collective-permute-start(bf16[8,1,64,512]{3,2,1,0:T(8,128)(2,1)} %get-tuple-element.29), channel_id=1, source_target_pairs={{0,1},{1,0},{2,3},{3,2},{4,5},{5,4},{6,7},{7,6},{8,9},{9,8},{10,11... | collective-permute-start | bytes 1572872 | tf_op jit(solution)/shard_map/ppermute | solution.py:263
  5.5 13.9 %collective-permute-start.1 = (bf16[8,1,64,512]{3,2,1,0:T(8,128)(2,1)}, bf16[8,1,64,512]{3,2,1,0:T(8,128)(2,1)S(1)}, u32[]{:S(2)}, u32[]{:S(2)}) collective-permute-start(bf16[8,1,64,512]{3,2,1,0:T(8,128)(2,1)} %get-tuple-element.30), channel_id=1, source_target_pairs={{1,2},{2,1},{3,0},{0,3},{5,6},{6,5},{7,4},{4,7},{9,10},{10,9},{11,... | collective-permute-start | bytes 1572872 | tf_op jit(solution)/shard_map/ppermute | solution.py:263
  11.0 3.6 %copy-start.5 = (s32[32,1]{0,1:T(1,128)S(1)}, s32[32,1]{0,1:T(1,128)}, u32[]{:S(2)}) copy-start(s32[32,1]{0,1:T(1,128)} %param.15) | copy-start | bytes 388
  11.0 8.4 %copy-start.12 = (bf16[8,1,64,512]{3,2,1,0:T(8,128)(2,1)S(1)}, bf16[8,1,64,512]{3,2,1,0:T(8,128)(2,1)}, u32[]{:S(2)}) copy-start(bf16[8,1,64,512]{3,2,1,0:T(8,128)(2,1)} %get-tuple-element.38) | copy-start | bytes 1572868
  11.0 8.4 %copy-start.11 = (bf16[8,1,64,512]{3,2,1,0:T(8,128)(2,1)S(1)}, bf16[8,1,64,512]{3,2,1,0:T(8,128)(2,1)}, u32[]{:S(2)}) copy-start(bf16[8,1,64,512]{3,2,1,0:T(8,128)(2,1)} %get-tuple-element.39) | copy-start | bytes 1572868
  15.1 28.0 %copy-start.1 = (bf16[512,512]{1,0:T(8,128)(2,1)}, bf16[512,512]{1,0:T(8,128)(2,1)S(1)}, u32[]{:S(2)}) copy-start(bf16[512,512]{1,0:T(8,128)(2,1)S(1)} %get-tuple-element.64.high_ref) | copy-start | bytes 1572868
  19.4 15.4 %collective-permute-start.2 = (bf16[8,1,64,512]{3,2,1,0:T(8,128)(2,1)S(1)}, bf16[8,1,64,512]{3,2,1,0:T(8,128)(2,1)S(1)}, u32[]{:S(2)}, u32[]{:S(2)}) collective-permute-start(bf16[8,1,64,512]{3,2,1,0:T(8,128)(2,1)S(1)} %copy-done.12), channel_id=1, source_target_pairs={{0,1},{1,0},{2,3},{3,2},{4,5},{5,4},{6,7},{7,6},{8,9},{9,8},{10,11... | collective-permute-start | bytes 1572872 | tf_op jit(solution)/shard_map/ppermute | solution.py:263
  19.4 15.4 %collective-permute-start.3 = (bf16[8,1,64,512]{3,2,1,0:T(8,128)(2,1)S(1)}, bf16[8,1,64,512]{3,2,1,0:T(8,128)(2,1)S(1)}, u32[]{:S(2)}, u32[]{:S(2)}) collective-permute-start(bf16[8,1,64,512]{3,2,1,0:T(8,128)(2,1)S(1)} %copy-done.11), channel_id=1, source_target_pairs={{1,2},{2,1},{3,0},{0,3},{5,6},{6,5},{7,4},{4,7},{9,10},{10,9},{11,... | collective-permute-start | bytes 1572872 | tf_op jit(solution)/shard_map/ppermute | solution.py:263
  22.8 16.4 %collective-permute-start.7 = (f16[4,1,64,512]{3,2,1,0:T(8,128)(2,1)S(1)}, f16[4,1,64,512]{3,2,1,0:T(8,128)(2,1)S(1)}, u32[]{:S(2)}, u32[]{:S(2)}) collective-permute-start(f16[4,1,64,512]{3,2,1,0:T(8,128)(2,1)S(1)} %get-tuple-element.61), channel_id=1, source_target_pairs={{0,1},{1,0},{2,3},{3,2},{4,5},{5,4},{6,7},{7,6},{8,9},{9,8},{10,11... | collective-permute-start | bytes 786440 | tf_op jit(solution)/shard_map/ppermute | solution.py:274
  23.6 16.3 %collective-permute-start.6 = (f16[4,1,64,512]{3,2,1,0:T(8,128)(2,1)S(1)}, f16[4,1,64,512]{3,2,1,0:T(8,128)(2,1)S(1)}, u32[]{:S(2)}, u32[]{:S(2)}) collective-permute-start(f16[4,1,64,512]{3,2,1,0:T(8,128)(2,1)S(1)} %get-tuple-element.62), channel_id=1, source_target_pairs={{1,2},{2,1},{3,0},{0,3},{5,6},{6,5},{7,4},{4,7},{9,10},{10,9},{11,... | collective-permute-start | bytes 786440 | tf_op jit(solution)/shard_map/ppermute | solution.py:274
  34.8 5.1 %copy-start.7 = (f32[8,1,64,512]{3,2,1,0:T(8,128)S(1)}, f32[8,1,64,512]{3,2,1,0:T(8,128)}, u32[]{:S(2)}) copy-start(f32[8,1,64,512]{3,2,1,0:T(8,128)} %get-tuple-element.33) | copy-start | bytes 3145732
  36.3 5.7 %collective-permute-start.5 = (f16[4,1,64,512]{3,2,1,0:T(8,128)(2,1)S(1)}, f16[4,1,64,512]{3,2,1,0:T(8,128)(2,1)S(1)}, u32[]{:S(2)}, u32[]{:S(2)}) collective-permute-start(f16[4,1,64,512]{3,2,1,0:T(8,128)(2,1)S(1)} %get-tuple-element.59), channel_id=1, source_target_pairs={{0,1},{1,0},{2,3},{3,2},{4,5},{5,4},{6,7},{7,6},{8,9},{9,8},{10,11... | collective-permute-start | bytes 786440 | tf_op jit(solution)/shard_map/ppermute | solution.py:274
  36.4 6.5 %copy-start.8 = (f32[8,1,64,512]{3,2,1,0:T(8,128)S(1)}, f32[8,1,64,512]{3,2,1,0:T(8,128)}, u32[]{:S(2)}) copy-start(f32[8,1,64,512]{3,2,1,0:T(8,128)} %get-tuple-element.37) | copy-start | bytes 3145732
  36.4 6.4 %collective-permute-start.4 = (f16[4,1,64,512]{3,2,1,0:T(8,128)(2,1)S(1)}, f16[4,1,64,512]{3,2,1,0:T(8,128)(2,1)S(1)}, u32[]{:S(2)}, u32[]{:S(2)}) collective-permute-start(f16[4,1,64,512]{3,2,1,0:T(8,128)(2,1)S(1)} %get-tuple-element.60), channel_id=1, source_target_pairs={{1,2},{2,1},{3,0},{0,3},{5,6},{6,5},{7,4},{4,7},{9,10},{10,9},{11,... | collective-permute-start | bytes 786440 | tf_op jit(solution)/shard_map/ppermute | solution.py:274
  38.4 21.8 %collective-permute-start.8 = (bf16[8,1,64,512]{3,2,1,0:T(8,128)(2,1)}, bf16[8,1,64,512]{3,2,1,0:T(8,128)(2,1)}, u32[]{:S(2)}, u32[]{:S(2)}) collective-permute-start(bf16[8,1,64,512]{3,2,1,0:T(8,128)(2,1)} %get-tuple-element.47), channel_id=1, source_target_pairs={{0,1},{1,0},{2,3},{3,2},{4,5},{5,4},{6,7},{7,6},{8,9},{9,8},{10,11... | collective-permute-start | bytes 1572872 | tf_op jit(solution)/shard_map/ppermute | solution.py:263
  39.1 21.1 %collective-permute-start.10 = (bf16[8,1,64,512]{3,2,1,0:T(8,128)(2,1)}, bf16[8,1,64,512]{3,2,1,0:T(8,128)(2,1)}, u32[]{:S(2)}, u32[]{:S(2)}) collective-permute-start(bf16[8,1,64,512]{3,2,1,0:T(8,128)(2,1)} %get-tuple-element.48), channel_id=1, source_target_pairs={{1,2},{2,1},{3,0},{0,3},{5,6},{6,5},{7,4},{4,7},{9,10},{10,9},{11,... | collective-permute-start | bytes 1572872 | tf_op jit(solution)/shard_map/ppermute | solution.py:263
  43.1 17.1 %copy-start.9 = (f32[8,1,64,512]{3,2,1,0:T(8,128)S(1)}, f32[8,1,64,512]{3,2,1,0:T(8,128)}, u32[]{:S(2)}) copy-start(f32[8,1,64,512]{3,2,1,0:T(8,128)} %get-tuple-element.41) | copy-start | bytes 3145732
  45.0 25.5 %copy-start.6 = (f32[8,1,64,512]{3,2,1,0:T(8,128)S(1)}, f32[8,1,64,512]{3,2,1,0:T(8,128)}, u32[]{:S(2)}) copy-start(f32[8,1,64,512]{3,2,1,0:T(8,128)} %get-tuple-element.42) | copy-start | bytes 3145732
  45.0 32.5 %all-to-all-start = ((bf16[32,16,1024]{2,1,0:T(8,128)(2,1)}), bf16[32,16,1024]{2,1,0:T(8,128)(2,1)}, u32[]{:S(2)}, u32[]{:S(2)}) async-start(bf16[32,16,1024]{2,1,0:T(8,128)(2,1)} %vertical_filter.4), calls=%async_computation | async-start | bytes 2097152 | tf_op jit(solution)/shard_map/all_to_all | solution.py:285
  61.4 7.8 %collective-permute-start.11 = (f16[4,1,64,512]{3,2,1,0:T(8,128)(2,1)S(1)}, f16[4,1,64,512]{3,2,1,0:T(8,128)(2,1)S(1)}, u32[]{:S(2)}, u32[]{:S(2)}) collective-permute-start(f16[4,1,64,512]{3,2,1,0:T(8,128)(2,1)S(1)} %get-tuple-element.53), channel_id=1, source_target_pairs={{0,1},{1,0},{2,3},{3,2},{4,5},{5,4},{6,7},{7,6},{8,9},{9,8},{10,11... | collective-permute-start | bytes 786440 | tf_op jit(solution)/shard_map/ppermute | solution.py:274
  61.8 8.6 %collective-permute-start.9 = (f16[4,1,64,512]{3,2,1,0:T(8,128)(2,1)S(1)}, f16[4,1,64,512]{3,2,1,0:T(8,128)(2,1)S(1)}, u32[]{:S(2)}, u32[]{:S(2)}) collective-permute-start(f16[4,1,64,512]{3,2,1,0:T(8,128)(2,1)S(1)} %get-tuple-element.54), channel_id=1, source_target_pairs={{1,2},{2,1},{3,0},{0,3},{5,6},{6,5},{7,4},{4,7},{9,10},{10,9},{11,... | collective-permute-start | bytes 786440 | tf_op jit(solution)/shard_map/ppermute | solution.py:274
  70.4 7.0 %copy-start.4 = (bf16[2,3,2,64,128]{4,3,2,1,0:T(8,128)(2,1)S(1)}, bf16[2,3,2,64,128]{4,3,2,1,0:T(8,128)(2,1)}, u32[]{:S(2)}) copy-start(bf16[2,3,2,64,128]{4,3,2,1,0:T(8,128)(2,1)} %constant.41.clone.bands_ref) | copy-start | bytes 589828
  71.7 1.0 copy-start.2
  120.4 1.0 copy-start.3
  121.4 21.3 %all-to-all-start.2 = ((bf16[32,32,512]{2,1,0:T(8,128)(2,1)}), bf16[32,32,512]{2,1,0:T(8,128)(2,1)S(1)}, u32[]{:S(2)}, u32[]{:S(2)}) async-start(bf16[32,32,512]{2,1,0:T(8,128)(2,1)} %copy-done.3), calls=%async_computation.2 | async-start | bytes 2097152 | tf_op jit(solution)/shard_map/all_to_all | solution.py:285

commit v3 on v2

--- a/solution.py
+++ b/solution.py
@@ -106,7 +106,7 @@
 def time_filter(noise, chan, comp, leaving):
     out = pl.BlockSpec((STEPS, 1, BLOCK, Z), lambda j, chan: (0, 0, j, 0))
     part = 0 if leaving else 1
-    kind = jnp.bfloat16 if leaving else jnp.float32
+    kind = jnp.bfloat16 if leaving and comp == 0 else jnp.float32
     return pl.pallas_call(
         time_kernel,
         grid_spec=pltpu.PrefetchScalarGridSpec(
@@ -297,22 +297,26 @@
     earlier = (owner[:, None] == owner[None, :]) & (tile[None, :] < tile[:, None])
     slot = jnp.sum(earlier.astype(jnp.int32), axis=1)
 
-    leave0, leave1 = [time_filter(noise, chan, c, True) for c in range(2)]
+    leave0 = time_filter(noise, chan, 0, True)
+    leave1 = [v.astype(jnp.float16) for v in time_filter(noise, chan, 1, True)]
     stay0 = time_filter(noise, chan, 0, False)
     got0 = after(first_exchange(*leave0), (*leave1, *stay0, *taps, owner, slot, rms))
     got1 = first_exchange(*after(leave1, got0))
     sends0 = for_second_exchange(stay0[0], *got0)
     (chan,) = after((chan,), sends0)
-    stay1, stay2 = [time_filter(noise, chan, c, False) for c in (1, 2)]
-    leave2 = time_filter(noise, chan, 2, True)
-    got1 = after(got1, (*stay1, *stay2, *leave2))
+    stay1 = time_filter(noise, chan, 1, False)
+    leave2 = [v.astype(jnp.float16) for v in time_filter(noise, chan, 2, True)]
+    got1 = after(got1, (*stay1, *leave2))
     sends1 = for_second_exchange(stay1[0], *got1)
     got2 = first_exchange(*after(leave2, sends1))
+    (chan,) = after((chan,), sends1)
+    stay2 = time_filter(noise, chan, 2, False)
     sends2 = for_second_exchange(stay2[0], *got2)
     sums = [
         summed(stay[1], *got, *second_exchange(*sends))
         for stay, got, sends in ((stay0, got0, sends0), (stay1, got1, sends1), (stay2, got2, sends2))
     ]
+    sums[1] = after(sums[1], stay2)
 
     planes = None
     for c in range(2):

time: 146 us -> 146 us (level)
    all_to_all x2, starting transfers between devices: 19.3 us -> 17.6 us  [along_span(): lax.all_to_all(values, 'span', split_axis=0, concat_axis=0, tiled=True)]
    convert_element_type x3, other arithmetic: 4.04 us -> 2.52 us  [for_second_exchange(): (kept[half:] + from_b[half:].astype(jnp.float32)).astype(jnp.float16)]
    ppermute x3, waiting for transfers between devices: 5.38 us -> 6.87 us  [second_exchange(): lax.ppermute(for_a, 'chan', PAIR_A)]
where the time goes in v3:
time: 146 us
  blocking collectives  38.4 us (26%)
  Pallas kernels  38 us (26%)
  starting transfers between devices  31.5 us (22%)
  waiting for transfers between devices  27.6 us (19%)
  other arithmetic  7.1 us (5%)
  local copies, waits for them, and re-layouts  2.98 us (2%)
    all_to_all x1, blocking collectives, along_span(): lax.all_to_all(values, 'span', split_axis=0, concat_axis=0, tiled=True)  38.4 us
    pallas_call x6, Pallas kernels, time_filter(): pl.pallas_call(time_kernel, grid_spec=pltpu.PrefetchScalarGridSpec(num_sc...  21.5 us
    all_to_all x2, starting transfers between devices, along_span(): lax.all_to_all(values, 'span', split_axis=0, concat_axis=0, tiled=True)  17.6 us
    all_to_all x2, waiting for transfers between devices, along_span(): lax.all_to_all(values, 'span', split_axis=0, concat_axis=0, tiled=True)  15.9 us
    pallas_call x2, Pallas kernels, inlet_tiles(): pl.pallas_call(inlet_kernel, grid=(comps, SPANS // block), in_specs=in_sp...  7.45 us
    ppermute x3, waiting for transfers between devices, second_exchange(): lax.ppermute(for_a, 'chan', PAIR_A)  6.87 us
    ppermute x3, starting transfers between devices, first_exchange(): lax.ppermute(to_b, 'chan', PAIR_B)  5.72 us
    pallas_call x3, Pallas kernels, vertical_filter(): pl.pallas_call(vertical_kernel, grid=(1,), in_specs=in_specs, out_specs=p...  4.63 us
  transfers between devices with their start and end apart: 14, of which 7 were waited for; matrix products, arithmetic and copies ran while one was open for 5% of the time, Pallas kernels for 19%

profile of v3, /device:TPU:1, one launch (start us, length us, event | category | flops | bytes accessed | tf_op | source)
XLA Modules:
  0.0 145.8 jit_solution(8570311577565983241)
XLA Ops:
  0.0 3.4 %time_filter.7 = (bf16[8,1,64,512]{3,2,1,0:T(8,128)(2,1)}, bf16[8,1,64,512]{3,2,1,0:T(8,128)(2,1)}) custom-call(s32[1]{0:T(128)} %bitcast.2.chan_ref, bf16[4,512,640]{2,1,0:T(8,128)(2,1)} %constant.40.clone.taps_ref, bf16[3,40,64,512]{3,2,1,0:T(8,128)(2,1)} %noise_ref.11), custom_call_target="tpu_custom_call" | custom-call | tf_op jit(solution)/shard_map/time_filter/pallas_call | solution.py:110
  3.4 2.1 %collective-permute-start = (bf16[8,1,64,512]{3,2,1,0:T(8,128)(2,1)}, bf16[8,1,64,512]{3,2,1,0:T(8,128)(2,1)S(1)}, u32[]{:S(2)}, u32[]{:S(2)}) collective-permute-start(bf16[8,1,64,512]{3,2,1,0:T(8,128)(2,1)} %get-tuple-element.32), channel_id=1, source_target_pairs={{0,1},{1,0},{2,3},{3,2},{4,5},{5,4},{6,7},{7,6},{8,9},{9,8},{10,11... | collective-permute-start | bytes 1572872 | tf_op jit(solution)/shard_map/ppermute | solution.py:263
  5.5 1.9 %collective-permute-start.1 = (bf16[8,1,64,512]{3,2,1,0:T(8,128)(2,1)}, bf16[8,1,64,512]{3,2,1,0:T(8,128)(2,1)}, u32[]{:S(2)}, u32[]{:S(2)}) collective-permute-start(bf16[8,1,64,512]{3,2,1,0:T(8,128)(2,1)} %get-tuple-element.33), channel_id=1, source_target_pairs={{1,2},{2,1},{3,0},{0,3},{5,6},{6,5},{7,4},{4,7},{9,10},{10,9},{11,... | collective-permute-start | bytes 1572872 | tf_op jit(solution)/shard_map/ppermute | solution.py:263
  7.4 0.0 copy-done.18
  7.4 0.1 fusion.9
  7.6 0.0 copy-done
  7.6 0.1 dynamic-slice_bitcast_fusion
  7.6 3.6 %time_filter.8 = (f32[8,1,64,512]{3,2,1,0:T(8,128)}, f32[8,1,64,512]{3,2,1,0:T(8,128)}) custom-call(s32[1]{0:T(128)} %bitcast.2.chan_ref, bf16[4,512,640]{2,1,0:T(8,128)(2,1)} %constant.40.clone.taps_ref, bf16[3,40,64,512]{3,2,1,0:T(8,128)(2,1)} %noise_ref.11), custom_call_target="tpu_custom_call" | custom-call | tf_op jit(solution)/shard_map/time_filter/pallas_call | solution.py:110
  11.2 3.7 %time_filter.6 = (f32[8,1,64,512]{3,2,1,0:T(8,128)}, f32[8,1,64,512]{3,2,1,0:T(8,128)}) custom-call(s32[1]{0:T(128)} %bitcast.2.chan_ref, bf16[4,512,640]{2,1,0:T(8,128)(2,1)} %constant.40.clone.taps_ref, bf16[3,40,64,512]{3,2,1,0:T(8,128)(2,1)} %noise_ref.11), custom_call_target="tpu_custom_call" | custom-call | tf_op jit(solution)/shard_map/time_filter/pallas_call | solution.py:110
  14.9 0.0 copy-done.10
  14.9 0.1 convert_element_type.113
  15.1 0.1 convert_element_type.114
  15.2 0.4 copy-done.5
  15.6 0.2 convert_reduce_fusion.slot_ref
  15.8 0.3 fusion
  16.1 1.0 collective-permute-done
  17.1 2.4 %collective-permute-done.1 = bf16[8,1,64,512]{3,2,1,0:T(8,128)(2,1)} collective-permute-done((bf16[8,1,64,512]{3,2,1,0:T(8,128)(2,1)}, bf16[8,1,64,512]{3,2,1,0:T(8,128)(2,1)}, u32[]{:S(2)}, u32[]{:S(2)}) %collective-permute-start.1) | collective-permute-done | bytes 524320 | tf_op jit(solution)/shard_map/ppermute | solution.py:263
  19.5 0.0 collective-permute-start.2
  19.5 1.9 %collective-permute-start.3 = (f16[8,1,64,512]{3,2,1,0:T(8,128)(2,1)S(1)}, f16[8,1,64,512]{3,2,1,0:T(8,128)(2,1)S(1)}, u32[]{:S(2)}, u32[]{:S(2)}) collective-permute-start(f16[8,1,64,512]{3,2,1,0:T(8,128)(2,1)S(1)} %convert_element_type.114), channel_id=1, source_target_pairs={{1,2},{2,1},{3,0},{0,3},{5,6},{6,5},{7,4},{4,7},{9,10},{10,9},{11,... | collective-permute-start | bytes 1572872 | tf_op jit(solution)/shard_map/ppermute | solution.py:263
  21.4 1.1 add_convert_fusion.4
  22.6 0.9 collective-permute-start.7
  23.5 0.8 collective-permute-start.6
  24.3 3.6 %time_filter.10 = (f32[8,1,64,512]{3,2,1,0:T(8,128)}, f32[8,1,64,512]{3,2,1,0:T(8,128)}) custom-call(s32[1]{0:T(128)} %bitcast.2.chan_ref, bf16[4,512,640]{2,1,0:T(8,128)(2,1)} %constant.40.clone.taps_ref, bf16[3,40,64,512]{3,2,1,0:T(8,128)(2,1)} %noise_ref.11), custom_call_target="tpu_custom_call" | custom-call | tf_op jit(solution)/shard_map/time_filter/pallas_call | solution.py:110
  27.8 3.7 %time_filter.9 = (f32[8,1,64,512]{3,2,1,0:T(8,128)}, f32[8,1,64,512]{3,2,1,0:T(8,128)}) custom-call(s32[1]{0:T(128)} %bitcast.2.chan_ref, bf16[4,512,640]{2,1,0:T(8,128)(2,1)} %constant.40.clone.taps_ref, bf16[3,40,64,512]{3,2,1,0:T(8,128)(2,1)} %noise_ref.11), custom_call_target="tpu_custom_call" | custom-call | tf_op jit(solution)/shard_map/time_filter/pallas_call | solution.py:110
  31.5 0.9 convert_element_type.119
  32.5 0.1 convert_element_type.120
  32.6 0.0 collective-permute-done.2
  32.6 0.0 collective-permute-done.3
  32.6 0.3 copy-done.15
  32.9 0.2 add_convert_fusion.2
  33.1 0.1 collective-permute-start.5
  33.2 2.0 %collective-permute-start.4 = (f16[4,1,64,512]{3,2,1,0:T(8,128)(2,1)S(1)}, f16[4,1,64,512]{3,2,1,0:T(8,128)(2,1)S(1)}, u32[]{:S(2)}, u32[]{:S(2)}) collective-permute-start(f16[4,1,64,512]{3,2,1,0:T(8,128)(2,1)S(1)} %get-tuple-element.66), channel_id=1, source_target_pairs={{1,2},{2,1},{3,0},{0,3},{5,6},{6,5},{7,4},{4,7},{9,10},{10,9},{11,... | collective-permute-start | bytes 786440 | tf_op jit(solution)/shard_map/ppermute | solution.py:274
  35.2 0.8 collective-permute-start.8
  36.0 0.7 collective-permute-done.7
  36.7 1.9 %collective-permute-start.10 = (f16[8,1,64,512]{3,2,1,0:T(8,128)(2,1)S(1)}, f16[8,1,64,512]{3,2,1,0:T(8,128)(2,1)}, u32[]{:S(2)}, u32[]{:S(2)}) collective-permute-start(f16[8,1,64,512]{3,2,1,0:T(8,128)(2,1)S(1)} %convert_element_type.120), channel_id=1, source_target_pairs={{1,2},{2,1},{3,0},{0,3},{5,6},{6,5},{7,4},{4,7},{9,10},{10,9},{11,... | collective-permute-start | bytes 1572872 | tf_op jit(solution)/shard_map/ppermute | solution.py:263
  38.6 0.0 collective-permute-done.6
  38.6 1.2 convert_add_fusion.2
  39.8 1.8 %vertical_filter.3.refs_0_ = bf16[32,16,1024]{2,1,0:T(8,128)(2,1)} custom-call(bf16[512,512]{1,0:T(8,128)(2,1)S(1)} %get-tuple-element.70.high_ref, bf16[512,512]{1,0:T(8,128)(2,1)S(1)} %get-tuple-element.69.low_ref, f32[4,1,64,512]{3,2,1,0:T(8,128)S(1)} %get-tuple-element.62.first_ref, f32[4,1,64,512]{3,2,1,0:T(8,128)S(1)} %get-tuple-element.61.second_ref), custom_call_target="tpu_custom_call" | custom-call | tf_op jit(solution)/shard_map/vertical_filter/pallas_call | solution.py:146
  41.6 3.6 %time_filter.11 = (f32[8,1,64,512]{3,2,1,0:T(8,128)}, f32[8,1,64,512]{3,2,1,0:T(8,128)}) custom-call(s32[1]{0:T(128)} %bitcast.2.chan_ref, bf16[4,512,640]{2,1,0:T(8,128)(2,1)} %constant.40.clone.taps_ref, bf16[3,40,64,512]{3,2,1,0:T(8,128)(2,1)} %noise_ref.11), custom_call_target="tpu_custom_call" | custom-call | tf_op jit(solution)/shard_map/time_filter/pallas_call | solution.py:110
  45.2 0.0 collective-permute-done.5
  45.2 0.0 collective-permute-done.4
  45.2 0.2 convert_add_fusion.4
  45.5 1.8 %vertical_filter.4 = bf16[32,16,1024]{2,1,0:T(8,128)(2,1)} custom-call(bf16[512,512]{1,0:T(8,128)(2,1)S(1)} %get-tuple-element.70.high_ref, bf16[512,512]{1,0:T(8,128)(2,1)S(1)} %get-tuple-element.69.low_ref, f32[4,1,64,512]{3,2,1,0:T(8,128)S(1)} %get-tuple-element.51.first_ref, ...), custom_call_target="tpu_custom_call", output_to_operand_aliasing={{}: (4, {})} | custom-call | tf_op jit(solution)/shard_map/vertical_filter/pallas_call | solution.py:146
  47.3 13.6 %all-to-all-start = ((bf16[32,16,1024]{2,1,0:T(8,128)(2,1)}), bf16[32,16,1024]{2,1,0:T(8,128)(2,1)}, u32[]{:S(2)}, u32[]{:S(2)}) async-start(bf16[32,16,1024]{2,1,0:T(8,128)(2,1)} %vertical_filter.4), calls=%async_computation | async-start | bytes 2097152 | tf_op jit(solution)/shard_map/all_to_all | solution.py:285
  60.9 0.0 collective-permute-done.8
  60.9 0.0 collective-permute-done.10
  60.9 1.2 add_convert_fusion
  62.2 0.1 collective-permute-start.11
  62.3 1.4 collective-permute-start.9
  63.7 0.1 copy.19.rms_ref
  63.8 6.1 %collective-permute-done.11 = f16[4,1,64,512]{3,2,1,0:T(8,128)(2,1)S(1)} collective-permute-done((f16[4,1,64,512]{3,2,1,0:T(8,128)(2,1)S(1)}, f16[4,1,64,512]{3,2,1,0:T(8,128)(2,1)S(1)}, u32[]{:S(2)}, u32[]{:S(2)}) %collective-permute-start.11) | collective-permute-done | bytes 262176 | tf_op jit(solution)/shard_map/ppermute | solution.py:274
  69.9 1.3 collective-permute-done.9
  71.2 1.3 convert_add_fusion
  72.6 1.0 copy-done.2
  73.6 1.0 vertical_filter.5.refs_0_
  74.6 3.5 %all-to-all-done.x_ref = bf16[32,16,1024]{2,1,0:T(8,128)(2,1)} async-done(((bf16[32,16,1024]{2,1,0:T(8,128)(2,1)}), bf16[32,16,1024]{2,1,0:T(8,128)(2,1)}, u32[]{:S(2)}, u32[]{:S(2)}) %all-to-all-start) | async-done | bytes 1048608 | tf_op jit(solution)/shard_map/all_to_all | solution.py:285
  78.1 2.8 %span_filter.2 = bf16[32,80,512]{2,1,0:T(8,128)(2,1)S(1)} custom-call(s32[32]{0:T(128)S(1)} %bitcast.5, s32[32]{0:T(128)S(1)} %convert_reduce_fusion.slot_ref, bf16[2,3,2,64,128]{4,3,2,1,0:T(8,128)(2,1)S(1)} %copy-done.4, f32[3,16,1]{2,1,0:T(8,128)S(1)} %copy.19.rms_ref, bf16[32,16,1024]{2,1,0:T(8,128)(2,1)} %all-to-all-done.x_ref, ...), custom_call_target="tpu_custom_call", output_to_operand_aliasing={{}: (5, {})} | custom-call | tf_op jit(solution)/shard_map/span_filter/pallas_call | solution.py:220
  81.0 38.4 %all_to_all.15.x_ref.refs_0_ = bf16[32,80,512]{2,1,0:T(8,128)(2,1)S(1)} all-to-all(bf16[32,80,512]{2,1,0:T(8,128)(2,1)S(1)} %span_filter.2), channel_id=1, replica_groups=mesh['span'=32,'chan'=4] {'span'}, dimensions={0} | all-to-all | bytes 5242880 | tf_op jit(solution)/shard_map/all_to_all | solution.py:285
  119.4 1.5 %span_filter.3 = (bf16[32,32,512]{2,1,0:T(8,128)(2,1)S(1)}, bf16[32,64,512]{2,1,0:T(8,128)(2,1)S(1)}) custom-call(s32[32]{0:T(128)S(1)} %bitcast.6, s32[32]{0:T(128)S(1)} %convert_reduce_fusion.slot_ref, bf16[2,3,2,64,128]{4,3,2,1,0:T(8,128)(2,1)S(1)} %copy-done.4, f32[3,16,1]{2,1,0:T(8,128)S(1)} %copy.19.rms_ref, ...), custom_call_target="tpu_custom_call" | custom-call | tf_op jit(solution)/shard_map/span_filter/pallas_call | solution.py:220
  120.9 1.0 copy-done.3
  121.9 4.0 %all-to-all-start.2 = ((bf16[32,32,512]{2,1,0:T(8,128)(2,1)}), bf16[32,32,512]{2,1,0:T(8,128)(2,1)S(1)}, u32[]{:S(2)}, u32[]{:S(2)}) async-start(bf16[32,32,512]{2,1,0:T(8,128)(2,1)} %copy-done.3), calls=%async_computation.2 | async-start | bytes 2097152 | tf_op jit(solution)/shard_map/all_to_all | solution.py:285
  126.0 4.9 %inlet_tiles.2.refs_0_ = f32[1,32,2,8,3,16,64]{6,5,4,3,2,1,0:T(8,128)} custom-call(bf16[32,64,512]{2,1,0:T(8,128)(2,1)S(1)} %get-tuple-element.56.x_ref), custom_call_target="tpu_custom_call" | custom-call | tf_op jit(solution)/shard_map/inlet_tiles/pallas_call | solution.py:246
  130.8 12.4 %all-to-all-done.2.x_ref = bf16[32,32,512]{2,1,0:T(8,128)(2,1)S(1)} async-done(((bf16[32,32,512]{2,1,0:T(8,128)(2,1)}), bf16[32,32,512]{2,1,0:T(8,128)(2,1)S(1)}, u32[]{:S(2)}, u32[]{:S(2)}) %all-to-all-start.2) | async-done | bytes 1048608 | tf_op jit(solution)/shard_map/all_to_all | solution.py:285
  143.2 2.6 %inlet_tiles.3 = f32[1,32,2,8,3,16,64]{6,5,4,3,2,1,0:T(8,128)} custom-call(bf16[32,32,512]{2,1,0:T(8,128)(2,1)S(1)} %all-to-all-done.2.x_ref, f32[1,32,2,8,3,16,64]{6,5,4,3,2,1,0:T(8,128)} %inlet_tiles.2.refs_0_), custom_call_target="tpu_custom_call", output_to_operand_aliasing={{}: (1, {})} | custom-call | tf_op jit(solution)/shard_map/inlet_tiles/pallas_call | solution.py:246
  (34 shorter events, 0.1 us)
Async XLA Ops:
  0.0 7.6 %copy-start = (f32[3,512]{1,0:T(4,128)S(1)}, f32[3,512]{1,0:T(4,128)}, u32[]{:S(2)}) copy-start(f32[3,512]{1,0:T(4,128)} %param.14) | copy-start | bytes 18436
  0.0 7.4 %copy-start.18 = (s32[512]{0:T(512)S(1)}, s32[512]{0:T(512)}, u32[]{:S(2)}) copy-start(s32[512]{0:T(512)} %param.13) | copy-start | bytes 6148
  3.4 13.7 %collective-permute-start = (bf16[8,1,64,512]{3,2,1,0:T(8,128)(2,1)}, bf16[8,1,64,512]{3,2,1,0:T(8,128)(2,1)S(1)}, u32[]{:S(2)}, u32[]{:S(2)}) collective-permute-start(bf16[8,1,64,512]{3,2,1,0:T(8,128)(2,1)} %get-tuple-element.32), channel_id=1, source_target_pairs={{0,1},{1,0},{2,3},{3,2},{4,5},{5,4},{6,7},{7,6},{8,9},{9,8},{10,11... | collective-permute-start | bytes 1572872 | tf_op jit(solution)/shard_map/ppermute | solution.py:263
  5.5 14.0 %collective-permute-start.1 = (bf16[8,1,64,512]{3,2,1,0:T(8,128)(2,1)}, bf16[8,1,64,512]{3,2,1,0:T(8,128)(2,1)}, u32[]{:S(2)}, u32[]{:S(2)}) collective-permute-start(bf16[8,1,64,512]{3,2,1,0:T(8,128)(2,1)} %get-tuple-element.33), channel_id=1, source_target_pairs={{1,2},{2,1},{3,0},{0,3},{5,6},{6,5},{7,4},{4,7},{9,10},{10,9},{11,... | collective-permute-start | bytes 1572872 | tf_op jit(solution)/shard_map/ppermute | solution.py:263
  11.2 3.7 %copy-start.10 = (f32[8,1,64,512]{3,2,1,0:T(8,128)S(1)}, f32[8,1,64,512]{3,2,1,0:T(8,128)}, u32[]{:S(2)}) copy-start(f32[8,1,64,512]{3,2,1,0:T(8,128)} %get-tuple-element.34) | copy-start | bytes 3145732
  11.2 3.8 %copy-start.9 = (f32[8,1,64,512]{3,2,1,0:T(8,128)S(1)}, f32[8,1,64,512]{3,2,1,0:T(8,128)}, u32[]{:S(2)}) copy-start(f32[8,1,64,512]{3,2,1,0:T(8,128)} %get-tuple-element.35) | copy-start | bytes 3145732
  14.9 0.7 copy-start.5
  14.9 6.5 %copy-start.14 = (f32[8,1,64,512]{3,2,1,0:T(8,128)S(1)}, f32[8,1,64,512]{3,2,1,0:T(8,128)}, u32[]{:S(2)}) copy-start(f32[8,1,64,512]{3,2,1,0:T(8,128)} %get-tuple-element.31) | copy-start | bytes 3145732
  16.0 29.4 %copy-start.1 = (bf16[512,512]{1,0:T(8,128)(2,1)}, bf16[512,512]{1,0:T(8,128)(2,1)S(1)}, u32[]{:S(2)}) copy-start(bf16[512,512]{1,0:T(8,128)(2,1)S(1)} %get-tuple-element.70.high_ref) | copy-start | bytes 1572868
  17.1 7.2 %copy-start.16 = (bf16[8,1,64,512]{3,2,1,0:T(8,128)(2,1)}, bf16[8,1,64,512]{3,2,1,0:T(8,128)(2,1)S(1)}, u32[]{:S(2)}) copy-start(bf16[8,1,64,512]{3,2,1,0:T(8,128)(2,1)S(1)} %collective-permute-done) | copy-start | bytes 1572868
  19.5 13.1 %collective-permute-start.2 = (f16[8,1,64,512]{3,2,1,0:T(8,128)(2,1)S(1)}, f16[8,1,64,512]{3,2,1,0:T(8,128)(2,1)S(1)}, u32[]{:S(2)}, u32[]{:S(2)}) collective-permute-start(f16[8,1,64,512]{3,2,1,0:T(8,128)(2,1)S(1)} %convert_element_type.113), channel_id=1, source_target_pairs={{0,1},{1,0},{2,3},{3,2},{4,5},{5,4},{6,7},{7,6},{8,9},{9,8},{10,11... | collective-permute-start | bytes 1572872 | tf_op jit(solution)/shard_map/ppermute | solution.py:263
  19.5 13.1 %collective-permute-start.3 = (f16[8,1,64,512]{3,2,1,0:T(8,128)(2,1)S(1)}, f16[8,1,64,512]{3,2,1,0:T(8,128)(2,1)S(1)}, u32[]{:S(2)}, u32[]{:S(2)}) collective-permute-start(f16[8,1,64,512]{3,2,1,0:T(8,128)(2,1)S(1)} %convert_element_type.114), channel_id=1, source_target_pairs={{1,2},{2,1},{3,0},{0,3},{5,6},{6,5},{7,4},{4,7},{9,10},{10,9},{11,... | collective-permute-start | bytes 1572872 | tf_op jit(solution)/shard_map/ppermute | solution.py:263
  22.6 14.1 %collective-permute-start.7 = (f16[4,1,64,512]{3,2,1,0:T(8,128)(2,1)S(1)}, f16[4,1,64,512]{3,2,1,0:T(8,128)(2,1)S(1)}, u32[]{:S(2)}, u32[]{:S(2)}) collective-permute-start(f16[4,1,64,512]{3,2,1,0:T(8,128)(2,1)S(1)} %get-tuple-element.67), channel_id=1, source_target_pairs={{0,1},{1,0},{2,3},{3,2},{4,5},{5,4},{6,7},{7,6},{8,9},{9,8},{10,11... | collective-permute-start | bytes 786440 | tf_op jit(solution)/shard_map/ppermute | solution.py:274
  23.5 15.1 %collective-permute-start.6 = (f16[4,1,64,512]{3,2,1,0:T(8,128)(2,1)S(1)}, f16[4,1,64,512]{3,2,1,0:T(8,128)(2,1)S(1)}, u32[]{:S(2)}, u32[]{:S(2)}) collective-permute-start(f16[4,1,64,512]{3,2,1,0:T(8,128)(2,1)S(1)} %get-tuple-element.68), channel_id=1, source_target_pairs={{1,2},{2,1},{3,0},{0,3},{5,6},{6,5},{7,4},{4,7},{9,10},{10,9},{11,... | collective-permute-start | bytes 786440 | tf_op jit(solution)/shard_map/ppermute | solution.py:274
  27.8 3.7 %copy-start.12 = (f32[8,1,64,512]{3,2,1,0:T(8,128)S(1)}, f32[8,1,64,512]{3,2,1,0:T(8,128)}, u32[]{:S(2)}) copy-start(f32[8,1,64,512]{3,2,1,0:T(8,128)} %get-tuple-element.44) | copy-start | bytes 3145732
  27.8 4.7 %copy-start.11 = (f32[8,1,64,512]{3,2,1,0:T(8,128)S(1)}, f32[8,1,64,512]{3,2,1,0:T(8,128)}, u32[]{:S(2)}) copy-start(f32[8,1,64,512]{3,2,1,0:T(8,128)} %get-tuple-element.45) | copy-start | bytes 3145732
  31.5 1.4 copy-start.15
  31.5 7.1 %copy-start.6 = (f32[8,1,64,512]{3,2,1,0:T(8,128)S(1)}, f32[8,1,64,512]{3,2,1,0:T(8,128)}, u32[]{:S(2)}) copy-start(f32[8,1,64,512]{3,2,1,0:T(8,128)} %get-tuple-element.36) | copy-start | bytes 3145732
  31.5 7.1 %copy-start.17 = (bf16[8,1,64,512]{3,2,1,0:T(8,128)(2,1)S(1)}, bf16[8,1,64,512]{3,2,1,0:T(8,128)(2,1)}, u32[]{:S(2)}) copy-start(bf16[8,1,64,512]{3,2,1,0:T(8,128)(2,1)} %copy-done.16) | copy-start | bytes 1572868
  33.1 12.1 %collective-permute-start.5 = (f16[4,1,64,512]{3,2,1,0:T(8,128)(2,1)S(1)}, f16[4,1,64,512]{3,2,1,0:T(8,128)(2,1)S(1)}, u32[]{:S(2)}, u32[]{:S(2)}) collective-permute-start(f16[4,1,64,512]{3,2,1,0:T(8,128)(2,1)S(1)} %get-tuple-element.65), channel_id=1, source_target_pairs={{0,1},{1,0},{2,3},{3,2},{4,5},{5,4},{6,7},{7,6},{8,9},{9,8},{10,11... | collective-permute-start | bytes 786440 | tf_op jit(solution)/shard_map/ppermute | solution.py:274
  33.2 12.0 %collective-permute-start.4 = (f16[4,1,64,512]{3,2,1,0:T(8,128)(2,1)S(1)}, f16[4,1,64,512]{3,2,1,0:T(8,128)(2,1)S(1)}, u32[]{:S(2)}, u32[]{:S(2)}) collective-permute-start(f16[4,1,64,512]{3,2,1,0:T(8,128)(2,1)S(1)} %get-tuple-element.66), channel_id=1, source_target_pairs={{1,2},{2,1},{3,0},{0,3},{5,6},{6,5},{7,4},{4,7},{9,10},{10,9},{11,... | collective-permute-start | bytes 786440 | tf_op jit(solution)/shard_map/ppermute | solution.py:274
  35.2 25.7 %collective-permute-start.8 = (f16[8,1,64,512]{3,2,1,0:T(8,128)(2,1)}, f16[8,1,64,512]{3,2,1,0:T(8,128)(2,1)}, u32[]{:S(2)}, u32[]{:S(2)}) collective-permute-start(f16[8,1,64,512]{3,2,1,0:T(8,128)(2,1)} %convert_element_type.119), channel_id=1, source_target_pairs={{0,1},{1,0},{2,3},{3,2},{4,5},{5,4},{6,7},{7,6},{8,9},{9,8},{10,11... | collective-permute-start | bytes 1572872 | tf_op jit(solution)/shard_map/ppermute | solution.py:263
  36.7 24.2 %collective-permute-start.10 = (f16[8,1,64,512]{3,2,1,0:T(8,128)(2,1)S(1)}, f16[8,1,64,512]{3,2,1,0:T(8,128)(2,1)}, u32[]{:S(2)}, u32[]{:S(2)}) collective-permute-start(f16[8,1,64,512]{3,2,1,0:T(8,128)(2,1)S(1)} %convert_element_type.120), channel_id=1, source_target_pairs={{1,2},{2,1},{3,0},{0,3},{5,6},{6,5},{7,4},{4,7},{9,10},{10,9},{11,... | collective-permute-start | bytes 1572872 | tf_op jit(solution)/shard_map/ppermute | solution.py:263
  41.6 3.6 %copy-start.7 = (f32[8,1,64,512]{3,2,1,0:T(8,128)S(1)}, f32[8,1,64,512]{3,2,1,0:T(8,128)}, u32[]{:S(2)}) copy-start(f32[8,1,64,512]{3,2,1,0:T(8,128)} %get-tuple-element.40) | copy-start | bytes 3145732
  45.5 15.4 %copy-start.13 = (f32[8,1,64,512]{3,2,1,0:T(8,128)S(1)}, f32[8,1,64,512]{3,2,1,0:T(8,128)}, u32[]{:S(2)}) copy-start(f32[8,1,64,512]{3,2,1,0:T(8,128)} %get-tuple-element.49) | copy-start | bytes 3145732
  47.3 23.9 %copy-start.8 = (f32[8,1,64,512]{3,2,1,0:T(8,128)S(1)}, f32[8,1,64,512]{3,2,1,0:T(8,128)}, u32[]{:S(2)}) copy-start(f32[8,1,64,512]{3,2,1,0:T(8,128)} %get-tuple-element.50) | copy-start | bytes 3145732
  47.3 30.8 %all-to-all-start = ((bf16[32,16,1024]{2,1,0:T(8,128)(2,1)}), bf16[32,16,1024]{2,1,0:T(8,128)(2,1)}, u32[]{:S(2)}, u32[]{:S(2)}) async-start(bf16[32,16,1024]{2,1,0:T(8,128)(2,1)} %vertical_filter.4), calls=%async_computation | async-start | bytes 2097152 | tf_op jit(solution)/shard_map/all_to_all | solution.py:285
  62.2 7.8 %collective-permute-start.11 = (f16[4,1,64,512]{3,2,1,0:T(8,128)(2,1)S(1)}, f16[4,1,64,512]{3,2,1,0:T(8,128)(2,1)S(1)}, u32[]{:S(2)}, u32[]{:S(2)}) collective-permute-start(f16[4,1,64,512]{3,2,1,0:T(8,128)(2,1)S(1)} %get-tuple-element.59), channel_id=1, source_target_pairs={{0,1},{1,0},{2,3},{3,2},{4,5},{5,4},{6,7},{7,6},{8,9},{9,8},{10,11... | collective-permute-start | bytes 786440 | tf_op jit(solution)/shard_map/ppermute | solution.py:274
  62.3 9.0 %collective-permute-start.9 = (f16[4,1,64,512]{3,2,1,0:T(8,128)(2,1)S(1)}, f16[4,1,64,512]{3,2,1,0:T(8,128)(2,1)S(1)}, u32[]{:S(2)}, u32[]{:S(2)}) collective-permute-start(f16[4,1,64,512]{3,2,1,0:T(8,128)(2,1)S(1)} %get-tuple-element.60), channel_id=1, source_target_pairs={{1,2},{2,1},{3,0},{0,3},{5,6},{6,5},{7,4},{4,7},{9,10},{10,9},{11,... | collective-permute-start | bytes 786440 | tf_op jit(solution)/shard_map/ppermute | solution.py:274
  71.2 6.9 %copy-start.4 = (bf16[2,3,2,64,128]{4,3,2,1,0:T(8,128)(2,1)S(1)}, bf16[2,3,2,64,128]{4,3,2,1,0:T(8,128)(2,1)}, u32[]{:S(2)}) copy-start(bf16[2,3,2,64,128]{4,3,2,1,0:T(8,128)(2,1)} %constant.41.clone.bands_ref) | copy-start | bytes 589828
  72.6 1.0 copy-start.2
  120.9 1.0 copy-start.3
  121.9 21.3 %all-to-all-start.2 = ((bf16[32,32,512]{2,1,0:T(8,128)(2,1)}), bf16[32,32,512]{2,1,0:T(8,128)(2,1)S(1)}, u32[]{:S(2)}, u32[]{:S(2)}) async-start(bf16[32,32,512]{2,1,0:T(8,128)(2,1)} %copy-done.3), calls=%async_computation.2 | async-start | bytes 2097152 | tf_op jit(solution)/shard_map/all_to_all | solution.py:285

commit v4 on v3

--- a/solution.py
+++ b/solution.py
@@ -197,14 +197,13 @@
         copy.wait()
 
 
-def span_filter(owner, slot, rms, moved, place, first, comps, shape, so_far=None, keep=0):
-    row, column = place
+def span_filter(owner, slot, rms, moved, row, first, comps, shape, so_far=None, keep=0):
     in_specs = [
         pl.BlockSpec(memory_space=pltpu.SMEM),
         pl.BlockSpec(memory_space=pltpu.SMEM),
         pl.BlockSpec((2, 3, 2, TY, LANES), lambda i: (0, 0, 0, 0, 0)),
         pl.BlockSpec((1, ZD, 1), lambda i: (first + i, 0, 0)),
-        pl.BlockSpec((SPANS, ZD, WIDTH), lambda i: (0, row, column + i)),
+        pl.BlockSpec((SPANS, ZD, WIDTH), lambda i: (0, row + i, 0)),
     ]
     out_specs = [pl.BlockSpec((SPANS, CAP * ZD, WIDTH), lambda i: (0, i, 0))]
     out_shape = [jax.ShapeDtypeStruct(shape, jnp.bfloat16)]
@@ -299,34 +298,31 @@
 
     leave0 = time_filter(noise, chan, 0, True)
     leave1 = [v.astype(jnp.float16) for v in time_filter(noise, chan, 1, True)]
-    stay0 = time_filter(noise, chan, 0, False)
-    got0 = after(first_exchange(*leave0), (*leave1, *stay0, *taps, owner, slot, rms))
+    stay0, stay1 = [time_filter(noise, chan, c, False) for c in range(2)]
+    got0 = after(first_exchange(*leave0), (*leave1, *stay0, *stay1, *taps, owner, slot, rms))
     got1 = first_exchange(*after(leave1, got0))
     sends0 = for_second_exchange(stay0[0], *got0)
     (chan,) = after((chan,), sends0)
-    stay1 = time_filter(noise, chan, 1, False)
     leave2 = [v.astype(jnp.float16) for v in time_filter(noise, chan, 2, True)]
-    got1 = after(got1, (*stay1, *leave2))
+    stay2 = time_filter(noise, chan, 2, False)
+    got1 = after(got1, (*leave2, *stay2))
     sends1 = for_second_exchange(stay1[0], *got1)
     got2 = first_exchange(*after(leave2, sends1))
-    (chan,) = after((chan,), sends1)
-    stay2 = time_filter(noise, chan, 2, False)
     sends2 = for_second_exchange(stay2[0], *got2)
     sums = [
         summed(stay[1], *got, *second_exchange(*sends))
         for stay, got, sends in ((stay0, got0, sends0), (stay1, got1, sends1), (stay2, got2, sends2))
     ]
-    sums[1] = after(sums[1], stay2)
 
     planes = None
     for c in range(2):
-        planes = vertical_filter(taps, sums[c], (SPANS, ZD, 2 * WIDTH), (0, 0, c), planes)
+        planes = vertical_filter(taps, sums[c], (SPANS, 2 * ZD, WIDTH), (0, c, 0), planes)
     moved = along_span(planes)
     shape = (SPANS, 2 * CAP * ZD + ZD, WIDTH)
     mixed = vertical_filter(taps, sums[2], shape, (0, 2 * CAP, 0))
-    mixed = along_span(span_filter(owner, slot, rms, moved, (0, 0), 0, 2, shape, mixed)[0])
+    mixed = along_span(span_filter(owner, slot, rms, moved, 0, 0, 2, shape, mixed)[0])
     last, tiles = span_filter(
-        owner, slot, rms, mixed, (2 * CAP, 0), 2, 1, (SPANS, CAP * ZD, WIDTH), keep=2 * CAP * ZD
+        owner, slot, rms, mixed, 2 * CAP, 2, 1, (SPANS, CAP * ZD, WIDTH), keep=2 * CAP * ZD
     )
     return inlet_tiles(along_span(last), 2, 1, inlet_tiles(tiles, 0, 2))
 

time: 146 us -> 145 us (level)
  waiting for transfers between devices: 27.6 us -> 24.8 us
  other arithmetic: 7.1 us -> 9.72 us
    convert_element_type x2, other arithmetic: 1.05 us -> 3.64 us  [local(): leave2 = [v.astype(jnp.float16) for v in time_filter(noise, chan, 2, True)]]
    ppermute x3, waiting for transfers between devices: 2.45 us -> 0.03 us  [first_exchange(): lax.ppermute(to_b, 'chan', PAIR_B)]
    ppermute x3, waiting for transfers between devices: 1.31 us -> 2.93 us  [second_exchange(): lax.ppermute(for_b, 'chan', PAIR_B)]
    ppermute x3, starting transfers between devices: 5.72 us -> 4.18 us  [first_exchange(): lax.ppermute(to_b, 'chan', PAIR_B)]
  transfers between devices with their start and end apart: 14 -> 14, of which waited for: 7 -> 6; matrix products, arithmetic and copies ran while one was open for 5% -> 7% of each run, Pallas kernels for 19% -> 19%
where the time goes in v4:
time: 145 us; the launch traced here: 144 us
  blocking collectives  38.6 us (27%)
  Pallas kernels  37.6 us (26%)
  starting transfers between devices  30.6 us (21%)
  waiting for transfers between devices  24.8 us (17%)
  other arithmetic  9.72 us (7%)
  local copies, waits for them, and re-layouts  2.66 us (2%)
    all_to_all x1, blocking collectives, along_span(): lax.all_to_all(values, 'span', split_axis=0, concat_axis=0, tiled=True)  38.6 us
    pallas_call x6, Pallas kernels, time_filter(): pl.pallas_call(time_kernel, grid_spec=pltpu.PrefetchScalarGridSpec(num_sc...  21.2 us
    all_to_all x2, starting transfers between devices, along_span(): lax.all_to_all(values, 'span', split_axis=0, concat_axis=0, tiled=True)  17.1 us
    all_to_all x2, waiting for transfers between devices, along_span(): lax.all_to_all(values, 'span', split_axis=0, concat_axis=0, tiled=True)  16 us
    pallas_call x2, Pallas kernels, inlet_tiles(): pl.pallas_call(inlet_kernel, grid=(comps, SPANS // block), in_specs=in_sp...  7.45 us
    ppermute x3, waiting for transfers between devices, second_exchange(): lax.ppermute(for_a, 'chan', PAIR_A)  5.83 us
    pallas_call x3, Pallas kernels, vertical_filter(): pl.pallas_call(vertical_kernel, grid=(1,), in_specs=in_specs, out_specs=p...  4.64 us
    pallas_call x2, Pallas kernels, span_filter(): pl.pallas_call(functools.partial(span_kernel, keep > 0), grid=(comps,), i...  4.38 us
  transfers between devices with their start and end apart: 14, of which 6 were waited for; matrix products, arithmetic and copies ran while one was open for 7% of the time, Pallas kernels for 19%

profile of v4, /device:TPU:1, one launch (start us, length us, event | category | flops | bytes accessed | tf_op | source)
XLA Modules:
  0.0 144.3 jit_solution(17780496796771356612)
XLA Ops:
  0.0 0.0 copy-start
  0.0 3.4 %time_filter.8 = (bf16[8,1,64,512]{3,2,1,0:T(8,128)(2,1)}, bf16[8,1,64,512]{3,2,1,0:T(8,128)(2,1)}) custom-call(s32[1]{0:T(128)} %bitcast.2.chan_ref, bf16[4,512,640]{2,1,0:T(8,128)(2,1)} %constant.40.clone.taps_ref, bf16[3,40,64,512]{3,2,1,0:T(8,128)(2,1)} %noise_ref.11), custom_call_target="tpu_custom_call" | custom-call | tf_op jit(solution)/shard_map/time_filter/pallas_call | solution.py:110
  3.4 2.1 %collective-permute-start = (bf16[8,1,64,512]{3,2,1,0:T(8,128)(2,1)}, bf16[8,1,64,512]{3,2,1,0:T(8,128)(2,1)S(1)}, u32[]{:S(2)}, u32[]{:S(2)}) collective-permute-start(bf16[8,1,64,512]{3,2,1,0:T(8,128)(2,1)} %get-tuple-element.31), channel_id=1, source_target_pairs={{0,1},{1,0},{2,3},{3,2},{4,5},{5,4},{6,7},{7,6},{8,9},{9,8},{10,11... | collective-permute-start | bytes 1572872 | tf_op jit(solution)/shard_map/ppermute | solution.py:262
  5.5 1.9 %collective-permute-start.1 = (bf16[8,1,64,512]{3,2,1,0:T(8,128)(2,1)}, bf16[8,1,64,512]{3,2,1,0:T(8,128)(2,1)}, u32[]{:S(2)}, u32[]{:S(2)}) collective-permute-start(bf16[8,1,64,512]{3,2,1,0:T(8,128)(2,1)} %get-tuple-element.32), channel_id=1, source_target_pairs={{1,2},{2,1},{3,0},{0,3},{5,6},{6,5},{7,4},{4,7},{9,10},{10,9},{11,... | collective-permute-start | bytes 1572872 | tf_op jit(solution)/shard_map/ppermute | solution.py:262
  7.4 0.0 copy-done.16
  7.4 0.1 fusion.9
  7.5 0.0 copy-done
  7.6 0.1 dynamic-slice_bitcast_fusion
  7.6 3.5 %time_filter.9 = (f32[8,1,64,512]{3,2,1,0:T(8,128)}, f32[8,1,64,512]{3,2,1,0:T(8,128)}) custom-call(s32[1]{0:T(128)} %bitcast.2.chan_ref, bf16[4,512,640]{2,1,0:T(8,128)(2,1)} %constant.40.clone.taps_ref, bf16[3,40,64,512]{3,2,1,0:T(8,128)(2,1)} %noise_ref.11), custom_call_target="tpu_custom_call" | custom-call | tf_op jit(solution)/shard_map/time_filter/pallas_call | solution.py:110
  11.1 3.5 %time_filter.7 = (f32[8,1,64,512]{3,2,1,0:T(8,128)}, f32[8,1,64,512]{3,2,1,0:T(8,128)}) custom-call(s32[1]{0:T(128)} %bitcast.2.chan_ref, bf16[4,512,640]{2,1,0:T(8,128)(2,1)} %constant.40.clone.taps_ref, bf16[3,40,64,512]{3,2,1,0:T(8,128)(2,1)} %noise_ref.11), custom_call_target="tpu_custom_call" | custom-call | tf_op jit(solution)/shard_map/time_filter/pallas_call | solution.py:110
  14.7 3.7 %time_filter.6 = (f32[8,1,64,512]{3,2,1,0:T(8,128)}, f32[8,1,64,512]{3,2,1,0:T(8,128)}) custom-call(s32[1]{0:T(128)} %bitcast.2.chan_ref, bf16[4,512,640]{2,1,0:T(8,128)(2,1)} %constant.40.clone.taps_ref, bf16[3,40,64,512]{3,2,1,0:T(8,128)(2,1)} %noise_ref.11), custom_call_target="tpu_custom_call" | custom-call | tf_op jit(solution)/shard_map/time_filter/pallas_call | solution.py:110
  18.4 0.1 convert_element_type.113
  18.5 0.1 convert_element_type.114
  18.6 0.4 copy-done.5
  19.0 0.2 convert_reduce_fusion.slot_ref
  19.2 0.3 fusion
  19.5 0.0 collective-permute-done
  19.5 0.0 collective-permute-done.1
  19.5 0.5 collective-permute-start.2
  20.0 1.4 %collective-permute-start.3 = (f16[8,1,64,512]{3,2,1,0:T(8,128)(2,1)S(1)}, f16[8,1,64,512]{3,2,1,0:T(8,128)(2,1)S(1)}, u32[]{:S(2)}, u32[]{:S(2)}) collective-permute-start(f16[8,1,64,512]{3,2,1,0:T(8,128)(2,1)S(1)} %convert_element_type.114), channel_id=1, source_target_pairs={{1,2},{2,1},{3,0},{0,3},{5,6},{6,5},{7,4},{4,7},{9,10},{10,9},{11,... | collective-permute-start | bytes 1572872 | tf_op jit(solution)/shard_map/ppermute | solution.py:262
  21.4 1.1 add_convert_fusion.4
  22.6 0.9 collective-permute-start.7
  23.5 0.8 collective-permute-start.6
  24.3 3.5 %time_filter.11 = (f32[8,1,64,512]{3,2,1,0:T(8,128)}, f32[8,1,64,512]{3,2,1,0:T(8,128)}) custom-call(s32[1]{0:T(128)} %bitcast.2.chan_ref, bf16[4,512,640]{2,1,0:T(8,128)(2,1)} %constant.40.clone.taps_ref, bf16[3,40,64,512]{3,2,1,0:T(8,128)(2,1)} %noise_ref.11), custom_call_target="tpu_custom_call" | custom-call | tf_op jit(solution)/shard_map/time_filter/pallas_call | solution.py:110
  27.9 3.5 %time_filter.10 = (f32[8,1,64,512]{3,2,1,0:T(8,128)}, f32[8,1,64,512]{3,2,1,0:T(8,128)}) custom-call(s32[1]{0:T(128)} %bitcast.2.chan_ref, bf16[4,512,640]{2,1,0:T(8,128)(2,1)} %constant.40.clone.taps_ref, bf16[3,40,64,512]{3,2,1,0:T(8,128)(2,1)} %noise_ref.11), custom_call_target="tpu_custom_call" | custom-call | tf_op jit(solution)/shard_map/time_filter/pallas_call | solution.py:110
  31.4 2.3 %convert_element_type.119 = f16[8,1,64,512]{3,2,1,0:T(8,128)(2,1)} convert(f32[8,1,64,512]{3,2,1,0:T(8,128)} %get-tuple-element.41) | non-fusion elementwise | flops 262144 | bytes 1572864 | tf_op jit(solution)/shard_map/convert_element_type | solution.py:306
  33.7 1.3 convert_element_type.120
  35.1 0.0 collective-permute-done.2
  35.1 0.0 collective-permute-done.3
  35.1 0.2 add_convert_fusion.2
  35.3 0.5 collective-permute-start.5
  35.8 1.5 %collective-permute-start.4 = (f16[4,1,64,512]{3,2,1,0:T(8,128)(2,1)S(1)}, f16[4,1,64,512]{3,2,1,0:T(8,128)(2,1)S(1)}, u32[]{:S(2)}, u32[]{:S(2)}) collective-permute-start(f16[4,1,64,512]{3,2,1,0:T(8,128)(2,1)S(1)} %get-tuple-element.60), channel_id=1, source_target_pairs={{1,2},{2,1},{3,0},{0,3},{5,6},{6,5},{7,4},{4,7},{9,10},{10,9},{11,... | collective-permute-start | bytes 786440 | tf_op jit(solution)/shard_map/ppermute | solution.py:273
  37.3 0.8 collective-permute-start.8
  38.1 0.0 collective-permute-done.7
  38.1 0.8 collective-permute-start.10
  38.9 0.0 collective-permute-done.6
  38.9 0.0 copy-done.8
  38.9 1.2 convert_add_fusion.2
  40.1 1.8 %vertical_filter.3.refs_0_ = bf16[32,32,512]{2,1,0:T(8,128)(2,1)} custom-call(bf16[512,512]{1,0:T(8,128)(2,1)S(1)} %get-tuple-element.64.high_ref, bf16[512,512]{1,0:T(8,128)(2,1)S(1)} %get-tuple-element.63.low_ref, f32[4,1,64,512]{3,2,1,0:T(8,128)S(1)} %get-tuple-element.56.first_ref, f32[4,1,64,512]{3,2,1,0:T(8,128)S(1)} %get-tuple-element.55.second_ref), custom_call_target="tpu_custom_call" | custom-call | tf_op jit(solution)/shard_map/vertical_filter/pallas_call | solution.py:146
  41.9 0.4 collective-permute-done.5
  42.4 1.8 %collective-permute-done.4 = f16[4,1,64,512]{3,2,1,0:T(8,128)(2,1)S(1)} collective-permute-done((f16[4,1,64,512]{3,2,1,0:T(8,128)(2,1)S(1)}, f16[4,1,64,512]{3,2,1,0:T(8,128)(2,1)S(1)}, u32[]{:S(2)}, u32[]{:S(2)}) %collective-permute-start.4) | collective-permute-done | bytes 262176 | tf_op jit(solution)/shard_map/ppermute | solution.py:273
  44.1 0.2 convert_add_fusion.4
  44.4 1.8 %vertical_filter.4 = bf16[32,32,512]{2,1,0:T(8,128)(2,1)} custom-call(bf16[512,512]{1,0:T(8,128)(2,1)S(1)} %get-tuple-element.64.high_ref, bf16[512,512]{1,0:T(8,128)(2,1)S(1)} %get-tuple-element.63.low_ref, f32[4,1,64,512]{3,2,1,0:T(8,128)S(1)} %get-tuple-element.58.first_ref, ...), custom_call_target="tpu_custom_call", output_to_operand_aliasing={{}: (4, {})} | custom-call | tf_op jit(solution)/shard_map/vertical_filter/pallas_call | solution.py:146
  46.2 13.0 %all-to-all-start = ((bf16[32,32,512]{2,1,0:T(8,128)(2,1)}), bf16[32,32,512]{2,1,0:T(8,128)(2,1)}, u32[]{:S(2)}, u32[]{:S(2)}) async-start(bf16[32,32,512]{2,1,0:T(8,128)(2,1)} %vertical_filter.4), calls=%async_computation | async-start | bytes 2097152 | tf_op jit(solution)/shard_map/all_to_all | solution.py:284
  59.2 0.0 collective-permute-done.8
  59.2 0.0 collective-permute-done.10
  59.3 1.2 add_convert_fusion
  60.5 0.4 collective-permute-start.11
  60.9 1.9 %collective-permute-start.9 = (f16[4,1,64,512]{3,2,1,0:T(8,128)(2,1)S(1)}, f16[4,1,64,512]{3,2,1,0:T(8,128)(2,1)S(1)}, u32[]{:S(2)}, u32[]{:S(2)}) collective-permute-start(f16[4,1,64,512]{3,2,1,0:T(8,128)(2,1)S(1)} %get-tuple-element.54), channel_id=1, source_target_pairs={{1,2},{2,1},{3,0},{0,3},{5,6},{6,5},{7,4},{4,7},{9,10},{10,9},{11,... | collective-permute-start | bytes 786440 | tf_op jit(solution)/shard_map/ppermute | solution.py:273
  62.8 0.1 copy.19.rms_ref
  62.9 5.4 %collective-permute-done.11 = f16[4,1,64,512]{3,2,1,0:T(8,128)(2,1)S(1)} collective-permute-done((f16[4,1,64,512]{3,2,1,0:T(8,128)(2,1)S(1)}, f16[4,1,64,512]{3,2,1,0:T(8,128)(2,1)S(1)}, u32[]{:S(2)}, u32[]{:S(2)}) %collective-permute-start.11) | collective-permute-done | bytes 262176 | tf_op jit(solution)/shard_map/ppermute | solution.py:273
  68.3 1.2 collective-permute-done.9
  69.4 1.3 convert_add_fusion
  70.8 1.0 copy-done.2
  71.8 1.0 vertical_filter.5.refs_0_
  72.8 3.6 %all-to-all-done.x_ref = bf16[32,32,512]{2,1,0:T(8,128)(2,1)} async-done(((bf16[32,32,512]{2,1,0:T(8,128)(2,1)}), bf16[32,32,512]{2,1,0:T(8,128)(2,1)}, u32[]{:S(2)}, u32[]{:S(2)}) %all-to-all-start) | async-done | bytes 1048608 | tf_op jit(solution)/shard_map/all_to_all | solution.py:284
  76.5 2.8 %span_filter.2 = bf16[32,80,512]{2,1,0:T(8,128)(2,1)S(1)} custom-call(s32[32]{0:T(128)S(1)} %bitcast.5, s32[32]{0:T(128)S(1)} %convert_reduce_fusion.slot_ref, bf16[2,3,2,64,128]{4,3,2,1,0:T(8,128)(2,1)S(1)} %copy-done.4, f32[3,16,1]{2,1,0:T(8,128)S(1)} %copy.19.rms_ref, bf16[32,32,512]{2,1,0:T(8,128)(2,1)} %all-to-all-done.x_ref, ...), custom_call_target="tpu_custom_call", output_to_operand_aliasing={{}: (5, {})} | custom-call | tf_op jit(solution)/shard_map/span_filter/pallas_call | solution.py:219
  79.3 38.6 %all_to_all.15.x_ref.refs_0_ = bf16[32,80,512]{2,1,0:T(8,128)(2,1)S(1)} all-to-all(bf16[32,80,512]{2,1,0:T(8,128)(2,1)S(1)} %span_filter.2), channel_id=1, replica_groups=mesh['span'=32,'chan'=4] {'span'}, dimensions={0} | all-to-all | bytes 5242880 | tf_op jit(solution)/shard_map/all_to_all | solution.py:284
  117.9 1.5 %span_filter.3 = (bf16[32,32,512]{2,1,0:T(8,128)(2,1)S(1)}, bf16[32,64,512]{2,1,0:T(8,128)(2,1)S(1)}) custom-call(s32[32]{0:T(128)S(1)} %bitcast.6, s32[32]{0:T(128)S(1)} %convert_reduce_fusion.slot_ref, bf16[2,3,2,64,128]{4,3,2,1,0:T(8,128)(2,1)S(1)} %copy-done.4, f32[3,16,1]{2,1,0:T(8,128)S(1)} %copy.19.rms_ref, ...), custom_call_target="tpu_custom_call" | custom-call | tf_op jit(solution)/shard_map/span_filter/pallas_call | solution.py:219
  119.5 1.0 copy-done.3
  120.4 4.0 %all-to-all-start.2 = ((bf16[32,32,512]{2,1,0:T(8,128)(2,1)}), bf16[32,32,512]{2,1,0:T(8,128)(2,1)S(1)}, u32[]{:S(2)}, u32[]{:S(2)}) async-start(bf16[32,32,512]{2,1,0:T(8,128)(2,1)} %copy-done.3), calls=%async_computation.2 | async-start | bytes 2097152 | tf_op jit(solution)/shard_map/all_to_all | solution.py:284
  124.5 4.9 %inlet_tiles.2.refs_0_ = f32[1,32,2,8,3,16,64]{6,5,4,3,2,1,0:T(8,128)} custom-call(bf16[32,64,512]{2,1,0:T(8,128)(2,1)S(1)} %get-tuple-element.50.x_ref), custom_call_target="tpu_custom_call" | custom-call | tf_op jit(solution)/shard_map/inlet_tiles/pallas_call | solution.py:245
  129.4 12.4 %all-to-all-done.2.x_ref = bf16[32,32,512]{2,1,0:T(8,128)(2,1)S(1)} async-done(((bf16[32,32,512]{2,1,0:T(8,128)(2,1)}), bf16[32,32,512]{2,1,0:T(8,128)(2,1)S(1)}, u32[]{:S(2)}, u32[]{:S(2)}) %all-to-all-start.2) | async-done | bytes 1048608 | tf_op jit(solution)/shard_map/all_to_all | solution.py:284
  141.8 2.6 %inlet_tiles.3 = f32[1,32,2,8,3,16,64]{6,5,4,3,2,1,0:T(8,128)} custom-call(bf16[32,32,512]{2,1,0:T(8,128)(2,1)S(1)} %all-to-all-done.2.x_ref, f32[1,32,2,8,3,16,64]{6,5,4,3,2,1,0:T(8,128)} %inlet_tiles.2.refs_0_), custom_call_target="tpu_custom_call", output_to_operand_aliasing={{}: (1, {})} | custom-call | tf_op jit(solution)/shard_map/inlet_tiles/pallas_call | solution.py:245
  (30 shorter events, 0.1 us)
Async XLA Ops:
  0.0 7.5 %copy-start = (f32[3,512]{1,0:T(4,128)S(1)}, f32[3,512]{1,0:T(4,128)}, u32[]{:S(2)}) copy-start(f32[3,512]{1,0:T(4,128)} %param.14) | copy-start | bytes 18436
  0.0 7.4 %copy-start.16 = (s32[512]{0:T(512)S(1)}, s32[512]{0:T(512)}, u32[]{:S(2)}) copy-start(s32[512]{0:T(512)} %param.13) | copy-start | bytes 6148
  3.4 16.1 %collective-permute-start = (bf16[8,1,64,512]{3,2,1,0:T(8,128)(2,1)}, bf16[8,1,64,512]{3,2,1,0:T(8,128)(2,1)S(1)}, u32[]{:S(2)}, u32[]{:S(2)}) collective-permute-start(bf16[8,1,64,512]{3,2,1,0:T(8,128)(2,1)} %get-tuple-element.31), channel_id=1, source_target_pairs={{0,1},{1,0},{2,3},{3,2},{4,5},{5,4},{6,7},{7,6},{8,9},{9,8},{10,11... | collective-permute-start | bytes 1572872 | tf_op jit(solution)/shard_map/ppermute | solution.py:262
  5.5 14.0 %collective-permute-start.1 = (bf16[8,1,64,512]{3,2,1,0:T(8,128)(2,1)}, bf16[8,1,64,512]{3,2,1,0:T(8,128)(2,1)}, u32[]{:S(2)}, u32[]{:S(2)}) collective-permute-start(bf16[8,1,64,512]{3,2,1,0:T(8,128)(2,1)} %get-tuple-element.32), channel_id=1, source_target_pairs={{1,2},{2,1},{3,0},{0,3},{5,6},{6,5},{7,4},{4,7},{9,10},{10,9},{11,... | collective-permute-start | bytes 1572872 | tf_op jit(solution)/shard_map/ppermute | solution.py:262
  14.7 3.7 %copy-start.10 = (f32[8,1,64,512]{3,2,1,0:T(8,128)S(1)}, f32[8,1,64,512]{3,2,1,0:T(8,128)}, u32[]{:S(2)}) copy-start(f32[8,1,64,512]{3,2,1,0:T(8,128)} %get-tuple-element.29) | copy-start | bytes 3145732
  14.7 3.8 %copy-start.9 = (f32[8,1,64,512]{3,2,1,0:T(8,128)S(1)}, f32[8,1,64,512]{3,2,1,0:T(8,128)}, u32[]{:S(2)}) copy-start(f32[8,1,64,512]{3,2,1,0:T(8,128)} %get-tuple-element.30) | copy-start | bytes 3145732
  18.3 0.7 copy-start.5
  18.3 3.1 %copy-start.13 = (f32[8,1,64,512]{3,2,1,0:T(8,128)S(1)}, f32[8,1,64,512]{3,2,1,0:T(8,128)}, u32[]{:S(2)}) copy-start(f32[8,1,64,512]{3,2,1,0:T(8,128)} %get-tuple-element.33) | copy-start | bytes 3145732
  19.5 24.9 %copy-start.1 = (bf16[512,512]{1,0:T(8,128)(2,1)}, bf16[512,512]{1,0:T(8,128)(2,1)S(1)}, u32[]{:S(2)}) copy-start(bf16[512,512]{1,0:T(8,128)(2,1)S(1)} %get-tuple-element.64.high_ref) | copy-start | bytes 1572868
  19.5 8.4 %copy-start.14 = (bf16[8,1,64,512]{3,2,1,0:T(8,128)(2,1)}, bf16[8,1,64,512]{3,2,1,0:T(8,128)(2,1)S(1)}, u32[]{:S(2)}) copy-start(bf16[8,1,64,512]{3,2,1,0:T(8,128)(2,1)S(1)} %collective-permute-done) | copy-start | bytes 1572868
  19.5 15.5 %collective-permute-start.2 = (f16[8,1,64,512]{3,2,1,0:T(8,128)(2,1)S(1)}, f16[8,1,64,512]{3,2,1,0:T(8,128)(2,1)S(1)}, u32[]{:S(2)}, u32[]{:S(2)}) collective-permute-start(f16[8,1,64,512]{3,2,1,0:T(8,128)(2,1)S(1)} %convert_element_type.113), channel_id=1, source_target_pairs={{0,1},{1,0},{2,3},{3,2},{4,5},{5,4},{6,7},{7,6},{8,9},{9,8},{10,11... | collective-permute-start | bytes 1572872 | tf_op jit(solution)/shard_map/ppermute | solution.py:262
  20.0 15.1 %collective-permute-start.3 = (f16[8,1,64,512]{3,2,1,0:T(8,128)(2,1)S(1)}, f16[8,1,64,512]{3,2,1,0:T(8,128)(2,1)S(1)}, u32[]{:S(2)}, u32[]{:S(2)}) collective-permute-start(f16[8,1,64,512]{3,2,1,0:T(8,128)(2,1)S(1)} %convert_element_type.114), channel_id=1, source_target_pairs={{1,2},{2,1},{3,0},{0,3},{5,6},{6,5},{7,4},{4,7},{9,10},{10,9},{11,... | collective-permute-start | bytes 1572872 | tf_op jit(solution)/shard_map/ppermute | solution.py:262
  22.6 15.5 %collective-permute-start.7 = (f16[4,1,64,512]{3,2,1,0:T(8,128)(2,1)S(1)}, f16[4,1,64,512]{3,2,1,0:T(8,128)(2,1)S(1)}, u32[]{:S(2)}, u32[]{:S(2)}) collective-permute-start(f16[4,1,64,512]{3,2,1,0:T(8,128)(2,1)S(1)} %get-tuple-element.61), channel_id=1, source_target_pairs={{0,1},{1,0},{2,3},{3,2},{4,5},{5,4},{6,7},{7,6},{8,9},{9,8},{10,11... | collective-permute-start | bytes 786440 | tf_op jit(solution)/shard_map/ppermute | solution.py:273
  23.5 15.4 %collective-permute-start.6 = (f16[4,1,64,512]{3,2,1,0:T(8,128)(2,1)S(1)}, f16[4,1,64,512]{3,2,1,0:T(8,128)(2,1)S(1)}, u32[]{:S(2)}, u32[]{:S(2)}) collective-permute-start(f16[4,1,64,512]{3,2,1,0:T(8,128)(2,1)S(1)} %get-tuple-element.62), channel_id=1, source_target_pairs={{1,2},{2,1},{3,0},{0,3},{5,6},{6,5},{7,4},{4,7},{9,10},{10,9},{11,... | collective-permute-start | bytes 786440 | tf_op jit(solution)/shard_map/ppermute | solution.py:273
  31.4 3.7 %copy-start.12 = (f32[8,1,64,512]{3,2,1,0:T(8,128)S(1)}, f32[8,1,64,512]{3,2,1,0:T(8,128)}, u32[]{:S(2)}) copy-start(f32[8,1,64,512]{3,2,1,0:T(8,128)} %get-tuple-element.35) | copy-start | bytes 3145732
  31.4 7.5 %copy-start.8 = (f32[8,1,64,512]{3,2,1,0:T(8,128)S(1)}, f32[8,1,64,512]{3,2,1,0:T(8,128)}, u32[]{:S(2)}) copy-start(f32[8,1,64,512]{3,2,1,0:T(8,128)} %get-tuple-element.34) | copy-start | bytes 3145732
  31.4 7.5 %copy-start.15 = (bf16[8,1,64,512]{3,2,1,0:T(8,128)(2,1)S(1)}, bf16[8,1,64,512]{3,2,1,0:T(8,128)(2,1)}, u32[]{:S(2)}) copy-start(bf16[8,1,64,512]{3,2,1,0:T(8,128)(2,1)} %copy-done.14) | copy-start | bytes 1572868
  35.3 7.1 %collective-permute-start.5 = (f16[4,1,64,512]{3,2,1,0:T(8,128)(2,1)S(1)}, f16[4,1,64,512]{3,2,1,0:T(8,128)(2,1)S(1)}, u32[]{:S(2)}, u32[]{:S(2)}) collective-permute-start(f16[4,1,64,512]{3,2,1,0:T(8,128)(2,1)S(1)} %get-tuple-element.59), channel_id=1, source_target_pairs={{0,1},{1,0},{2,3},{3,2},{4,5},{5,4},{6,7},{7,6},{8,9},{9,8},{10,11... | collective-permute-start | bytes 786440 | tf_op jit(solution)/shard_map/ppermute | solution.py:273
  35.8 8.3 %copy-start.7 = (f32[8,1,64,512]{3,2,1,0:T(8,128)S(1)}, f32[8,1,64,512]{3,2,1,0:T(8,128)}, u32[]{:S(2)}) copy-start(f32[8,1,64,512]{3,2,1,0:T(8,128)} %get-tuple-element.28) | copy-start | bytes 3145732
  35.8 8.3 %collective-permute-start.4 = (f16[4,1,64,512]{3,2,1,0:T(8,128)(2,1)S(1)}, f16[4,1,64,512]{3,2,1,0:T(8,128)(2,1)S(1)}, u32[]{:S(2)}, u32[]{:S(2)}) collective-permute-start(f16[4,1,64,512]{3,2,1,0:T(8,128)(2,1)S(1)} %get-tuple-element.60), channel_id=1, source_target_pairs={{1,2},{2,1},{3,0},{0,3},{5,6},{6,5},{7,4},{4,7},{9,10},{10,9},{11,... | collective-permute-start | bytes 786440 | tf_op jit(solution)/shard_map/ppermute | solution.py:273
  37.3 21.9 %collective-permute-start.8 = (f16[8,1,64,512]{3,2,1,0:T(8,128)(2,1)}, f16[8,1,64,512]{3,2,1,0:T(8,128)(2,1)}, u32[]{:S(2)}, u32[]{:S(2)}) collective-permute-start(f16[8,1,64,512]{3,2,1,0:T(8,128)(2,1)} %convert_element_type.119), channel_id=1, source_target_pairs={{0,1},{1,0},{2,3},{3,2},{4,5},{5,4},{6,7},{7,6},{8,9},{9,8},{10,11... | collective-permute-start | bytes 1572872 | tf_op jit(solution)/shard_map/ppermute | solution.py:262
  38.1 21.2 %collective-permute-start.10 = (f16[8,1,64,512]{3,2,1,0:T(8,128)(2,1)S(1)}, f16[8,1,64,512]{3,2,1,0:T(8,128)(2,1)}, u32[]{:S(2)}, u32[]{:S(2)}) collective-permute-start(f16[8,1,64,512]{3,2,1,0:T(8,128)(2,1)S(1)} %convert_element_type.120), channel_id=1, source_target_pairs={{1,2},{2,1},{3,0},{0,3},{5,6},{6,5},{7,4},{4,7},{9,10},{10,9},{11,... | collective-permute-start | bytes 1572872 | tf_op jit(solution)/shard_map/ppermute | solution.py:262
  44.4 14.9 %copy-start.11 = (f32[8,1,64,512]{3,2,1,0:T(8,128)S(1)}, f32[8,1,64,512]{3,2,1,0:T(8,128)}, u32[]{:S(2)}) copy-start(f32[8,1,64,512]{3,2,1,0:T(8,128)} %get-tuple-element.43) | copy-start | bytes 3145732
  46.2 23.2 %copy-start.6 = (f32[8,1,64,512]{3,2,1,0:T(8,128)S(1)}, f32[8,1,64,512]{3,2,1,0:T(8,128)}, u32[]{:S(2)}) copy-start(f32[8,1,64,512]{3,2,1,0:T(8,128)} %get-tuple-element.44) | copy-start | bytes 3145732
  46.2 30.3 %all-to-all-start = ((bf16[32,32,512]{2,1,0:T(8,128)(2,1)}), bf16[32,32,512]{2,1,0:T(8,128)(2,1)}, u32[]{:S(2)}, u32[]{:S(2)}) async-start(bf16[32,32,512]{2,1,0:T(8,128)(2,1)} %vertical_filter.4), calls=%async_computation | async-start | bytes 2097152 | tf_op jit(solution)/shard_map/all_to_all | solution.py:284
  60.5 7.8 %collective-permute-start.11 = (f16[4,1,64,512]{3,2,1,0:T(8,128)(2,1)S(1)}, f16[4,1,64,512]{3,2,1,0:T(8,128)(2,1)S(1)}, u32[]{:S(2)}, u32[]{:S(2)}) collective-permute-start(f16[4,1,64,512]{3,2,1,0:T(8,128)(2,1)S(1)} %get-tuple-element.53), channel_id=1, source_target_pairs={{0,1},{1,0},{2,3},{3,2},{4,5},{5,4},{6,7},{7,6},{8,9},{9,8},{10,11... | collective-permute-start | bytes 786440 | tf_op jit(solution)/shard_map/ppermute | solution.py:273
  60.9 8.6 %collective-permute-start.9 = (f16[4,1,64,512]{3,2,1,0:T(8,128)(2,1)S(1)}, f16[4,1,64,512]{3,2,1,0:T(8,128)(2,1)S(1)}, u32[]{:S(2)}, u32[]{:S(2)}) collective-permute-start(f16[4,1,64,512]{3,2,1,0:T(8,128)(2,1)S(1)} %get-tuple-element.54), channel_id=1, source_target_pairs={{1,2},{2,1},{3,0},{0,3},{5,6},{6,5},{7,4},{4,7},{9,10},{10,9},{11,... | collective-permute-start | bytes 786440 | tf_op jit(solution)/shard_map/ppermute | solution.py:273
  69.4 7.0 %copy-start.4 = (bf16[2,3,2,64,128]{4,3,2,1,0:T(8,128)(2,1)S(1)}, bf16[2,3,2,64,128]{4,3,2,1,0:T(8,128)(2,1)}, u32[]{:S(2)}) copy-start(bf16[2,3,2,64,128]{4,3,2,1,0:T(8,128)(2,1)} %constant.41.clone.bands_ref) | copy-start | bytes 589828
  70.8 1.0 copy-start.2
  119.5 1.0 copy-start.3
  120.4 21.3 %all-to-all-start.2 = ((bf16[32,32,512]{2,1,0:T(8,128)(2,1)}), bf16[32,32,512]{2,1,0:T(8,128)(2,1)S(1)}, u32[]{:S(2)}, u32[]{:S(2)}) async-start(bf16[32,32,512]{2,1,0:T(8,128)(2,1)} %copy-done.3), calls=%async_computation.2 | async-start | bytes 2097152 | tf_op jit(solution)/shard_map/all_to_all | solution.py:284

commit v5 on v4

--- a/solution.py
+++ b/solution.py
@@ -303,11 +303,11 @@
     got1 = first_exchange(*after(leave1, got0))
     sends0 = for_second_exchange(stay0[0], *got0)
     (chan,) = after((chan,), sends0)
-    leave2 = [v.astype(jnp.float16) for v in time_filter(noise, chan, 2, True)]
+    leave2 = time_filter(noise, chan, 2, True)
     stay2 = time_filter(noise, chan, 2, False)
     got1 = after(got1, (*leave2, *stay2))
     sends1 = for_second_exchange(stay1[0], *got1)
-    got2 = first_exchange(*after(leave2, sends1))
+    got2 = first_exchange(*[v.astype(jnp.float16) for v in after(leave2, sends1)])
     sends2 = for_second_exchange(stay2[0], *got2)
     sums = [
         summed(stay[1], *got, *second_exchange(*sends))

time: 145 us -> 145 us (level)
  waiting for transfers between devices: 24.8 us -> 26.9 us
  other arithmetic: 9.72 us -> 7.83 us
    convert_element_type x2, other arithmetic: 3.64 us -> 0.99 us  [local(): v.astype(jnp.float16)]
  transfers between devices with their start and end apart: 14 -> 14, of which waited for: 6 -> 8; matrix products, arithmetic and copies ran while one was open for 7% -> 6% of each run, Pallas kernels for 19% -> 19%
where the time goes in v5:
time: 145 us; the launch traced here: 144 us
  blocking collectives  38.6 us (27%)
  Pallas kernels  37.7 us (26%)
  starting transfers between devices  30.3 us (21%)
  waiting for transfers between devices  26.9 us (19%)
  other arithmetic  7.83 us (5%)
  local copies, waits for them, and re-layouts  2.67 us (2%)
    all_to_all x1, blocking collectives, along_span(): lax.all_to_all(values, 'span', split_axis=0, concat_axis=0, tiled=True)  38.6 us
    pallas_call x6, Pallas kernels, time_filter(): pl.pallas_call(time_kernel, grid_spec=pltpu.PrefetchScalarGridSpec(num_sc...  21.3 us
    all_to_all x2, starting transfers between devices, along_span(): lax.all_to_all(values, 'span', split_axis=0, concat_axis=0, tiled=True)  16.9 us
    all_to_all x2, waiting for transfers between devices, along_span(): lax.all_to_all(values, 'span', split_axis=0, concat_axis=0, tiled=True)  16.1 us
    pallas_call x2, Pallas kernels, inlet_tiles(): pl.pallas_call(inlet_kernel, grid=(comps, SPANS // block), in_specs=in_sp...  7.45 us
    ppermute x3, waiting for transfers between devices, second_exchange(): lax.ppermute(for_a, 'chan', PAIR_A)  6.22 us
    ppermute x3, starting transfers between devices, first_exchange(): lax.ppermute(to_b, 'chan', PAIR_B)  5.06 us
    pallas_call x3, Pallas kernels, vertical_filter(): pl.pallas_call(vertical_kernel, grid=(1,), in_specs=in_specs, out_specs=p...  4.63 us
  transfers between devices with their start and end apart: 14, of which 8 were waited for; matrix products, arithmetic and copies ran while one was open for 6% of the time, Pallas kernels for 19%

profile of v5, /device:TPU:1, one launch (start us, length us, event | category | flops | bytes accessed | tf_op | source)
XLA Modules:
  0.0 144.2 jit_solution(3837097328589961828)
XLA Ops:
  0.0 3.4 %time_filter.8 = (bf16[8,1,64,512]{3,2,1,0:T(8,128)(2,1)}, bf16[8,1,64,512]{3,2,1,0:T(8,128)(2,1)}) custom-call(s32[1]{0:T(128)} %bitcast.2.chan_ref, bf16[4,512,640]{2,1,0:T(8,128)(2,1)} %constant.40.clone.taps_ref, bf16[3,40,64,512]{3,2,1,0:T(8,128)(2,1)} %noise_ref.11), custom_call_target="tpu_custom_call" | custom-call | tf_op jit(solution)/shard_map/time_filter/pallas_call | solution.py:110
  3.4 2.1 %collective-permute-start = (bf16[8,1,64,512]{3,2,1,0:T(8,128)(2,1)}, bf16[8,1,64,512]{3,2,1,0:T(8,128)(2,1)S(1)}, u32[]{:S(2)}, u32[]{:S(2)}) collective-permute-start(bf16[8,1,64,512]{3,2,1,0:T(8,128)(2,1)} %get-tuple-element.31), channel_id=1, source_target_pairs={{0,1},{1,0},{2,3},{3,2},{4,5},{5,4},{6,7},{7,6},{8,9},{9,8},{10,11... | collective-permute-start | bytes 1572872 | tf_op jit(solution)/shard_map/ppermute | solution.py:262
  5.5 1.9 %collective-permute-start.1 = (bf16[8,1,64,512]{3,2,1,0:T(8,128)(2,1)}, bf16[8,1,64,512]{3,2,1,0:T(8,128)(2,1)}, u32[]{:S(2)}, u32[]{:S(2)}) collective-permute-start(bf16[8,1,64,512]{3,2,1,0:T(8,128)(2,1)} %get-tuple-element.32), channel_id=1, source_target_pairs={{1,2},{2,1},{3,0},{0,3},{5,6},{6,5},{7,4},{4,7},{9,10},{10,9},{11,... | collective-permute-start | bytes 1572872 | tf_op jit(solution)/shard_map/ppermute | solution.py:262
  7.4 0.0 copy-done.18
  7.4 0.1 fusion.9
  7.5 0.0 copy-done
  7.5 0.1 dynamic-slice_bitcast_fusion
  7.6 3.5 %time_filter.9 = (f32[8,1,64,512]{3,2,1,0:T(8,128)}, f32[8,1,64,512]{3,2,1,0:T(8,128)}) custom-call(s32[1]{0:T(128)} %bitcast.2.chan_ref, bf16[4,512,640]{2,1,0:T(8,128)(2,1)} %constant.40.clone.taps_ref, bf16[3,40,64,512]{3,2,1,0:T(8,128)(2,1)} %noise_ref.11), custom_call_target="tpu_custom_call" | custom-call | tf_op jit(solution)/shard_map/time_filter/pallas_call | solution.py:110
  11.1 3.5 %time_filter.7 = (f32[8,1,64,512]{3,2,1,0:T(8,128)}, f32[8,1,64,512]{3,2,1,0:T(8,128)}) custom-call(s32[1]{0:T(128)} %bitcast.2.chan_ref, bf16[4,512,640]{2,1,0:T(8,128)(2,1)} %constant.40.clone.taps_ref, bf16[3,40,64,512]{3,2,1,0:T(8,128)(2,1)} %noise_ref.11), custom_call_target="tpu_custom_call" | custom-call | tf_op jit(solution)/shard_map/time_filter/pallas_call | solution.py:110
  14.7 3.7 %time_filter.6 = (f32[8,1,64,512]{3,2,1,0:T(8,128)}, f32[8,1,64,512]{3,2,1,0:T(8,128)}) custom-call(s32[1]{0:T(128)} %bitcast.2.chan_ref, bf16[4,512,640]{2,1,0:T(8,128)(2,1)} %constant.40.clone.taps_ref, bf16[3,40,64,512]{3,2,1,0:T(8,128)(2,1)} %noise_ref.11), custom_call_target="tpu_custom_call" | custom-call | tf_op jit(solution)/shard_map/time_filter/pallas_call | solution.py:110
  18.4 0.0 copy-done.12
  18.4 0.1 convert_element_type.113
  18.5 0.0 copy-done.11
  18.5 0.1 convert_element_type.114
  18.6 0.4 copy-done.5
  19.0 0.2 convert_reduce_fusion.slot_ref
  19.2 0.3 fusion
  19.5 0.0 collective-permute-done
  19.5 0.0 collective-permute-done.1
  19.5 0.5 collective-permute-start.2
  20.0 1.4 collective-permute-start.3
  21.4 1.9 %add_convert_fusion.4 = (f16[4,1,64,512]{3,2,1,0:T(8,128)(2,1)}, f16[4,1,64,512]{3,2,1,0:T(8,128)(2,1)}) fusion(f32[8,1,64,512]{3,2,1,0:T(8,128)S(1)} %copy-done.15, bf16[8,1,64,512]{3,2,1,0:T(8,128)(2,1)} %collective-permute-done.1, bf16[8,1,64,512]{3,2,1,0:T(8,128)(2,1)S(1)} %collective-permute-done), kind=kLoop, calls=%fused_computation.22 | loop fusion | flops 786432 | bytes 2097152 | tf_op jit(solution)/shard_map/convert_element_type | solution.py:268
  23.4 0.9 collective-permute-start.7
  24.2 0.9 collective-permute-start.6
  25.1 3.5 %time_filter.11 = (f32[8,1,64,512]{3,2,1,0:T(8,128)}, f32[8,1,64,512]{3,2,1,0:T(8,128)}) custom-call(s32[1]{0:T(128)} %bitcast.2.chan_ref, bf16[4,512,640]{2,1,0:T(8,128)(2,1)} %constant.40.clone.taps_ref, bf16[3,40,64,512]{3,2,1,0:T(8,128)(2,1)} %noise_ref.11), custom_call_target="tpu_custom_call" | custom-call | tf_op jit(solution)/shard_map/time_filter/pallas_call | solution.py:110
  28.6 3.6 %time_filter.10 = (f32[8,1,64,512]{3,2,1,0:T(8,128)}, f32[8,1,64,512]{3,2,1,0:T(8,128)}) custom-call(s32[1]{0:T(128)} %bitcast.2.chan_ref, bf16[4,512,640]{2,1,0:T(8,128)(2,1)} %constant.40.clone.taps_ref, bf16[3,40,64,512]{3,2,1,0:T(8,128)(2,1)} %noise_ref.11), custom_call_target="tpu_custom_call" | custom-call | tf_op jit(solution)/shard_map/time_filter/pallas_call | solution.py:110
  32.3 0.0 collective-permute-done.2
  32.3 0.8 collective-permute-done.3
  33.1 0.2 add_convert_fusion.2
  33.3 0.1 collective-permute-start.5
  33.4 1.1 collective-permute-start.4
  34.5 0.9 convert_element_type.131
  35.4 0.1 convert_element_type.136
  35.5 1.8 %collective-permute-start.10 = (f16[8,1,64,512]{3,2,1,0:T(8,128)(2,1)S(1)}, f16[8,1,64,512]{3,2,1,0:T(8,128)(2,1)}, u32[]{:S(2)}, u32[]{:S(2)}) collective-permute-start(f16[8,1,64,512]{3,2,1,0:T(8,128)(2,1)S(1)} %convert_element_type.136), channel_id=1, source_target_pairs={{1,2},{2,1},{3,0},{0,3},{5,6},{6,5},{7,4},{4,7},{9,10},{10,9},{11,... | collective-permute-start | bytes 1572872 | tf_op jit(solution)/shard_map/ppermute | solution.py:262
  37.2 0.0 collective-permute-done.7
  37.2 0.6 collective-permute-start.8
  37.8 0.9 collective-permute-done.6
  38.7 1.2 convert_add_fusion.2
  39.9 1.8 %vertical_filter.3.refs_0_ = bf16[32,32,512]{2,1,0:T(8,128)(2,1)} custom-call(bf16[512,512]{1,0:T(8,128)(2,1)S(1)} %get-tuple-element.64.high_ref, bf16[512,512]{1,0:T(8,128)(2,1)S(1)} %get-tuple-element.63.low_ref, f32[4,1,64,512]{3,2,1,0:T(8,128)S(1)} %get-tuple-element.56.first_ref, f32[4,1,64,512]{3,2,1,0:T(8,128)S(1)} %get-tuple-element.55.second_ref), custom_call_target="tpu_custom_call" | custom-call | tf_op jit(solution)/shard_map/vertical_filter/pallas_call | solution.py:146
  41.7 0.8 collective-permute-done.5
  42.5 1.7 %collective-permute-done.4 = f16[4,1,64,512]{3,2,1,0:T(8,128)(2,1)S(1)} collective-permute-done((f16[4,1,64,512]{3,2,1,0:T(8,128)(2,1)S(1)}, f16[4,1,64,512]{3,2,1,0:T(8,128)(2,1)S(1)}, u32[]{:S(2)}, u32[]{:S(2)}) %collective-permute-start.4) | collective-permute-done | bytes 262176 | tf_op jit(solution)/shard_map/ppermute | solution.py:273
  44.2 0.2 convert_add_fusion.4
  44.5 1.8 %vertical_filter.4 = bf16[32,32,512]{2,1,0:T(8,128)(2,1)} custom-call(bf16[512,512]{1,0:T(8,128)(2,1)S(1)} %get-tuple-element.64.high_ref, bf16[512,512]{1,0:T(8,128)(2,1)S(1)} %get-tuple-element.63.low_ref, f32[4,1,64,512]{3,2,1,0:T(8,128)S(1)} %get-tuple-element.58.first_ref, ...), custom_call_target="tpu_custom_call", output_to_operand_aliasing={{}: (4, {})} | custom-call | tf_op jit(solution)/shard_map/vertical_filter/pallas_call | solution.py:146
  46.3 12.9 %all-to-all-start = ((bf16[32,32,512]{2,1,0:T(8,128)(2,1)}), bf16[32,32,512]{2,1,0:T(8,128)(2,1)}, u32[]{:S(2)}, u32[]{:S(2)}) async-start(bf16[32,32,512]{2,1,0:T(8,128)(2,1)} %vertical_filter.4), calls=%async_computation | async-start | bytes 2097152 | tf_op jit(solution)/shard_map/all_to_all | solution.py:284
  59.2 0.0 collective-permute-done.10
  59.2 0.0 collective-permute-done.8
  59.2 1.2 add_convert_fusion
  60.4 0.3 collective-permute-start.11
  60.8 1.9 %collective-permute-start.9 = (f16[4,1,64,512]{3,2,1,0:T(8,128)(2,1)S(1)}, f16[4,1,64,512]{3,2,1,0:T(8,128)(2,1)S(1)}, u32[]{:S(2)}, u32[]{:S(2)}) collective-permute-start(f16[4,1,64,512]{3,2,1,0:T(8,128)(2,1)S(1)} %get-tuple-element.54), channel_id=1, source_target_pairs={{1,2},{2,1},{3,0},{0,3},{5,6},{6,5},{7,4},{4,7},{9,10},{10,9},{11,... | collective-permute-start | bytes 786440 | tf_op jit(solution)/shard_map/ppermute | solution.py:273
  62.7 0.1 copy.19.rms_ref
  62.8 5.5 %collective-permute-done.11 = f16[4,1,64,512]{3,2,1,0:T(8,128)(2,1)S(1)} collective-permute-done((f16[4,1,64,512]{3,2,1,0:T(8,128)(2,1)S(1)}, f16[4,1,64,512]{3,2,1,0:T(8,128)(2,1)S(1)}, u32[]{:S(2)}, u32[]{:S(2)}) %collective-permute-start.11) | collective-permute-done | bytes 262176 | tf_op jit(solution)/shard_map/ppermute | solution.py:273
  68.2 1.1 collective-permute-done.9
  69.3 1.3 convert_add_fusion
  70.7 1.0 copy-done.2
  71.7 1.0 vertical_filter.5.refs_0_
  72.7 3.7 %all-to-all-done.x_ref = bf16[32,32,512]{2,1,0:T(8,128)(2,1)} async-done(((bf16[32,32,512]{2,1,0:T(8,128)(2,1)}), bf16[32,32,512]{2,1,0:T(8,128)(2,1)}, u32[]{:S(2)}, u32[]{:S(2)}) %all-to-all-start) | async-done | bytes 1048608 | tf_op jit(solution)/shard_map/all_to_all | solution.py:284
  76.4 2.8 %span_filter.2 = bf16[32,80,512]{2,1,0:T(8,128)(2,1)S(1)} custom-call(s32[32]{0:T(128)S(1)} %bitcast.5, s32[32]{0:T(128)S(1)} %convert_reduce_fusion.slot_ref, bf16[2,3,2,64,128]{4,3,2,1,0:T(8,128)(2,1)S(1)} %copy-done.4, f32[3,16,1]{2,1,0:T(8,128)S(1)} %copy.19.rms_ref, bf16[32,32,512]{2,1,0:T(8,128)(2,1)} %all-to-all-done.x_ref, ...), custom_call_target="tpu_custom_call", output_to_operand_aliasing={{}: (5, {})} | custom-call | tf_op jit(solution)/shard_map/span_filter/pallas_call | solution.py:219
  79.2 38.6 %all_to_all.15.x_ref.refs_0_ = bf16[32,80,512]{2,1,0:T(8,128)(2,1)S(1)} all-to-all(bf16[32,80,512]{2,1,0:T(8,128)(2,1)S(1)} %span_filter.2), channel_id=1, replica_groups=mesh['span'=32,'chan'=4] {'span'}, dimensions={0} | all-to-all | bytes 5242880 | tf_op jit(solution)/shard_map/all_to_all | solution.py:284
  117.8 1.5 %span_filter.3 = (bf16[32,32,512]{2,1,0:T(8,128)(2,1)S(1)}, bf16[32,64,512]{2,1,0:T(8,128)(2,1)S(1)}) custom-call(s32[32]{0:T(128)S(1)} %bitcast.6, s32[32]{0:T(128)S(1)} %convert_reduce_fusion.slot_ref, bf16[2,3,2,64,128]{4,3,2,1,0:T(8,128)(2,1)S(1)} %copy-done.4, f32[3,16,1]{2,1,0:T(8,128)S(1)} %copy.19.rms_ref, ...), custom_call_target="tpu_custom_call" | custom-call | tf_op jit(solution)/shard_map/span_filter/pallas_call | solution.py:219
  119.4 1.0 copy-done.3
  120.3 4.0 %all-to-all-start.2 = ((bf16[32,32,512]{2,1,0:T(8,128)(2,1)}), bf16[32,32,512]{2,1,0:T(8,128)(2,1)S(1)}, u32[]{:S(2)}, u32[]{:S(2)}) async-start(bf16[32,32,512]{2,1,0:T(8,128)(2,1)} %copy-done.3), calls=%async_computation.2 | async-start | bytes 2097152 | tf_op jit(solution)/shard_map/all_to_all | solution.py:284
  124.4 4.9 %inlet_tiles.2.refs_0_ = f32[1,32,2,8,3,16,64]{6,5,4,3,2,1,0:T(8,128)} custom-call(bf16[32,64,512]{2,1,0:T(8,128)(2,1)S(1)} %get-tuple-element.50.x_ref), custom_call_target="tpu_custom_call" | custom-call | tf_op jit(solution)/shard_map/inlet_tiles/pallas_call | solution.py:245
  129.3 12.4 %all-to-all-done.2.x_ref = bf16[32,32,512]{2,1,0:T(8,128)(2,1)S(1)} async-done(((bf16[32,32,512]{2,1,0:T(8,128)(2,1)}), bf16[32,32,512]{2,1,0:T(8,128)(2,1)S(1)}, u32[]{:S(2)}, u32[]{:S(2)}) %all-to-all-start.2) | async-done | bytes 1048608 | tf_op jit(solution)/shard_map/all_to_all | solution.py:284
  141.7 2.6 %inlet_tiles.3 = f32[1,32,2,8,3,16,64]{6,5,4,3,2,1,0:T(8,128)} custom-call(bf16[32,32,512]{2,1,0:T(8,128)(2,1)S(1)} %all-to-all-done.2.x_ref, f32[1,32,2,8,3,16,64]{6,5,4,3,2,1,0:T(8,128)} %inlet_tiles.2.refs_0_), custom_call_target="tpu_custom_call", output_to_operand_aliasing={{}: (1, {})} | custom-call | tf_op jit(solution)/shard_map/inlet_tiles/pallas_call | solution.py:245
  (34 shorter events, 0.1 us)
Async XLA Ops:
  0.0 7.5 %copy-start = (f32[3,512]{1,0:T(4,128)S(1)}, f32[3,512]{1,0:T(4,128)}, u32[]{:S(2)}) copy-start(f32[3,512]{1,0:T(4,128)} %param.14) | copy-start | bytes 18436
  0.0 7.4 %copy-start.18 = (s32[512]{0:T(512)S(1)}, s32[512]{0:T(512)}, u32[]{:S(2)}) copy-start(s32[512]{0:T(512)} %param.13) | copy-start | bytes 6148
  3.4 16.1 %collective-permute-start = (bf16[8,1,64,512]{3,2,1,0:T(8,128)(2,1)}, bf16[8,1,64,512]{3,2,1,0:T(8,128)(2,1)S(1)}, u32[]{:S(2)}, u32[]{:S(2)}) collective-permute-start(bf16[8,1,64,512]{3,2,1,0:T(8,128)(2,1)} %get-tuple-element.31), channel_id=1, source_target_pairs={{0,1},{1,0},{2,3},{3,2},{4,5},{5,4},{6,7},{7,6},{8,9},{9,8},{10,11... | collective-permute-start | bytes 1572872 | tf_op jit(solution)/shard_map/ppermute | solution.py:262
  5.5 14.0 %collective-permute-start.1 = (bf16[8,1,64,512]{3,2,1,0:T(8,128)(2,1)}, bf16[8,1,64,512]{3,2,1,0:T(8,128)(2,1)}, u32[]{:S(2)}, u32[]{:S(2)}) collective-permute-start(bf16[8,1,64,512]{3,2,1,0:T(8,128)(2,1)} %get-tuple-element.32), channel_id=1, source_target_pairs={{1,2},{2,1},{3,0},{0,3},{5,6},{6,5},{7,4},{4,7},{9,10},{10,9},{11,... | collective-permute-start | bytes 1572872 | tf_op jit(solution)/shard_map/ppermute | solution.py:262
  14.7 3.7 %copy-start.12 = (f32[8,1,64,512]{3,2,1,0:T(8,128)S(1)}, f32[8,1,64,512]{3,2,1,0:T(8,128)}, u32[]{:S(2)}) copy-start(f32[8,1,64,512]{3,2,1,0:T(8,128)} %get-tuple-element.29) | copy-start | bytes 3145732
  14.7 3.8 %copy-start.11 = (f32[8,1,64,512]{3,2,1,0:T(8,128)S(1)}, f32[8,1,64,512]{3,2,1,0:T(8,128)}, u32[]{:S(2)}) copy-start(f32[8,1,64,512]{3,2,1,0:T(8,128)} %get-tuple-element.30) | copy-start | bytes 3145732
  18.4 0.7 copy-start.5
  18.4 3.0 %copy-start.15 = (f32[8,1,64,512]{3,2,1,0:T(8,128)S(1)}, f32[8,1,64,512]{3,2,1,0:T(8,128)}, u32[]{:S(2)}) copy-start(f32[8,1,64,512]{3,2,1,0:T(8,128)} %get-tuple-element.33) | copy-start | bytes 3145732
  19.5 25.0 %copy-start.1 = (bf16[512,512]{1,0:T(8,128)(2,1)}, bf16[512,512]{1,0:T(8,128)(2,1)S(1)}, u32[]{:S(2)}) copy-start(bf16[512,512]{1,0:T(8,128)(2,1)S(1)} %get-tuple-element.64.high_ref) | copy-start | bytes 1572868
  19.5 9.1 %copy-start.16 = (bf16[8,1,64,512]{3,2,1,0:T(8,128)(2,1)}, bf16[8,1,64,512]{3,2,1,0:T(8,128)(2,1)S(1)}, u32[]{:S(2)}) copy-start(bf16[8,1,64,512]{3,2,1,0:T(8,128)(2,1)S(1)} %collective-permute-done) | copy-start | bytes 1572868
  19.5 12.7 %collective-permute-start.2 = (f16[8,1,64,512]{3,2,1,0:T(8,128)(2,1)S(1)}, f16[8,1,64,512]{3,2,1,0:T(8,128)(2,1)S(1)}, u32[]{:S(2)}, u32[]{:S(2)}) collective-permute-start(f16[8,1,64,512]{3,2,1,0:T(8,128)(2,1)S(1)} %convert_element_type.113), channel_id=1, source_target_pairs={{0,1},{1,0},{2,3},{3,2},{4,5},{5,4},{6,7},{7,6},{8,9},{9,8},{10,11... | collective-permute-start | bytes 1572872 | tf_op jit(solution)/shard_map/ppermute | solution.py:262
  20.0 13.1 %collective-permute-start.3 = (f16[8,1,64,512]{3,2,1,0:T(8,128)(2,1)S(1)}, f16[8,1,64,512]{3,2,1,0:T(8,128)(2,1)S(1)}, u32[]{:S(2)}, u32[]{:S(2)}) collective-permute-start(f16[8,1,64,512]{3,2,1,0:T(8,128)(2,1)S(1)} %convert_element_type.114), channel_id=1, source_target_pairs={{1,2},{2,1},{3,0},{0,3},{5,6},{6,5},{7,4},{4,7},{9,10},{10,9},{11,... | collective-permute-start | bytes 1572872 | tf_op jit(solution)/shard_map/ppermute | solution.py:262
  23.4 13.9 %collective-permute-start.7 = (f16[4,1,64,512]{3,2,1,0:T(8,128)(2,1)}, f16[4,1,64,512]{3,2,1,0:T(8,128)(2,1)S(1)}, u32[]{:S(2)}, u32[]{:S(2)}) collective-permute-start(f16[4,1,64,512]{3,2,1,0:T(8,128)(2,1)} %get-tuple-element.61), channel_id=1, source_target_pairs={{0,1},{1,0},{2,3},{3,2},{4,5},{5,4},{6,7},{7,6},{8,9},{9,8},{10,11... | collective-permute-start | bytes 786440 | tf_op jit(solution)/shard_map/ppermute | solution.py:273
  24.2 14.5 %collective-permute-start.6 = (f16[4,1,64,512]{3,2,1,0:T(8,128)(2,1)}, f16[4,1,64,512]{3,2,1,0:T(8,128)(2,1)S(1)}, u32[]{:S(2)}, u32[]{:S(2)}) collective-permute-start(f16[4,1,64,512]{3,2,1,0:T(8,128)(2,1)} %get-tuple-element.62), channel_id=1, source_target_pairs={{1,2},{2,1},{3,0},{0,3},{5,6},{6,5},{7,4},{4,7},{9,10},{10,9},{11,... | collective-permute-start | bytes 786440 | tf_op jit(solution)/shard_map/ppermute | solution.py:273
  28.6 4.5 %copy-start.14 = (f32[8,1,64,512]{3,2,1,0:T(8,128)S(1)}, f32[8,1,64,512]{3,2,1,0:T(8,128)}, u32[]{:S(2)}) copy-start(f32[8,1,64,512]{3,2,1,0:T(8,128)} %get-tuple-element.35) | copy-start | bytes 3145732
  32.3 2.2 %copy-start.10 = (f32[8,1,64,512]{3,2,1,0:T(8,128)S(1)}, f32[8,1,64,512]{3,2,1,0:T(8,128)}, u32[]{:S(2)}) copy-start(f32[8,1,64,512]{3,2,1,0:T(8,128)} %get-tuple-element.47) | copy-start | bytes 3145732
  32.3 3.1 %copy-start.9 = (f32[8,1,64,512]{3,2,1,0:T(8,128)S(1)}, f32[8,1,64,512]{3,2,1,0:T(8,128)}, u32[]{:S(2)}) copy-start(f32[8,1,64,512]{3,2,1,0:T(8,128)} %get-tuple-element.48) | copy-start | bytes 3145732
  33.1 5.6 %copy-start.8 = (f32[8,1,64,512]{3,2,1,0:T(8,128)S(1)}, f32[8,1,64,512]{3,2,1,0:T(8,128)}, u32[]{:S(2)}) copy-start(f32[8,1,64,512]{3,2,1,0:T(8,128)} %get-tuple-element.34) | copy-start | bytes 3145732
  33.1 5.6 %copy-start.17 = (bf16[8,1,64,512]{3,2,1,0:T(8,128)(2,1)S(1)}, bf16[8,1,64,512]{3,2,1,0:T(8,128)(2,1)}, u32[]{:S(2)}) copy-start(bf16[8,1,64,512]{3,2,1,0:T(8,128)(2,1)} %copy-done.16) | copy-start | bytes 1572868
  33.3 9.2 %collective-permute-start.5 = (f16[4,1,64,512]{3,2,1,0:T(8,128)(2,1)S(1)}, f16[4,1,64,512]{3,2,1,0:T(8,128)(2,1)S(1)}, u32[]{:S(2)}, u32[]{:S(2)}) collective-permute-start(f16[4,1,64,512]{3,2,1,0:T(8,128)(2,1)S(1)} %get-tuple-element.59), channel_id=1, source_target_pairs={{0,1},{1,0},{2,3},{3,2},{4,5},{5,4},{6,7},{7,6},{8,9},{9,8},{10,11... | collective-permute-start | bytes 786440 | tf_op jit(solution)/shard_map/ppermute | solution.py:273
  33.4 10.8 %collective-permute-start.4 = (f16[4,1,64,512]{3,2,1,0:T(8,128)(2,1)S(1)}, f16[4,1,64,512]{3,2,1,0:T(8,128)(2,1)S(1)}, u32[]{:S(2)}, u32[]{:S(2)}) collective-permute-start(f16[4,1,64,512]{3,2,1,0:T(8,128)(2,1)S(1)} %get-tuple-element.60), channel_id=1, source_target_pairs={{1,2},{2,1},{3,0},{0,3},{5,6},{6,5},{7,4},{4,7},{9,10},{10,9},{11,... | collective-permute-start | bytes 786440 | tf_op jit(solution)/shard_map/ppermute | solution.py:273
  35.5 8.7 %copy-start.7 = (f32[8,1,64,512]{3,2,1,0:T(8,128)S(1)}, f32[8,1,64,512]{3,2,1,0:T(8,128)}, u32[]{:S(2)}) copy-start(f32[8,1,64,512]{3,2,1,0:T(8,128)} %get-tuple-element.28) | copy-start | bytes 3145732
  35.5 23.7 %collective-permute-start.10 = (f16[8,1,64,512]{3,2,1,0:T(8,128)(2,1)S(1)}, f16[8,1,64,512]{3,2,1,0:T(8,128)(2,1)}, u32[]{:S(2)}, u32[]{:S(2)}) collective-permute-start(f16[8,1,64,512]{3,2,1,0:T(8,128)(2,1)S(1)} %convert_element_type.136), channel_id=1, source_target_pairs={{1,2},{2,1},{3,0},{0,3},{5,6},{6,5},{7,4},{4,7},{9,10},{10,9},{11,... | collective-permute-start | bytes 1572872 | tf_op jit(solution)/shard_map/ppermute | solution.py:262
  37.2 21.9 %collective-permute-start.8 = (f16[8,1,64,512]{3,2,1,0:T(8,128)(2,1)}, f16[8,1,64,512]{3,2,1,0:T(8,128)(2,1)}, u32[]{:S(2)}, u32[]{:S(2)}) collective-permute-start(f16[8,1,64,512]{3,2,1,0:T(8,128)(2,1)} %convert_element_type.131), channel_id=1, source_target_pairs={{0,1},{1,0},{2,3},{3,2},{4,5},{5,4},{6,7},{7,6},{8,9},{9,8},{10,11... | collective-permute-start | bytes 1572872 | tf_op jit(solution)/shard_map/ppermute | solution.py:262
  44.5 14.7 %copy-start.13 = (f32[8,1,64,512]{3,2,1,0:T(8,128)S(1)}, f32[8,1,64,512]{3,2,1,0:T(8,128)}, u32[]{:S(2)}) copy-start(f32[8,1,64,512]{3,2,1,0:T(8,128)} %get-tuple-element.43) | copy-start | bytes 3145732
  46.3 23.1 %copy-start.6 = (f32[8,1,64,512]{3,2,1,0:T(8,128)S(1)}, f32[8,1,64,512]{3,2,1,0:T(8,128)}, u32[]{:S(2)}) copy-start(f32[8,1,64,512]{3,2,1,0:T(8,128)} %get-tuple-element.44) | copy-start | bytes 3145732
  46.3 30.1 %all-to-all-start = ((bf16[32,32,512]{2,1,0:T(8,128)(2,1)}), bf16[32,32,512]{2,1,0:T(8,128)(2,1)}, u32[]{:S(2)}, u32[]{:S(2)}) async-start(bf16[32,32,512]{2,1,0:T(8,128)(2,1)} %vertical_filter.4), calls=%async_computation | async-start | bytes 2097152 | tf_op jit(solution)/shard_map/all_to_all | solution.py:284
  60.4 7.8 %collective-permute-start.11 = (f16[4,1,64,512]{3,2,1,0:T(8,128)(2,1)S(1)}, f16[4,1,64,512]{3,2,1,0:T(8,128)(2,1)S(1)}, u32[]{:S(2)}, u32[]{:S(2)}) collective-permute-start(f16[4,1,64,512]{3,2,1,0:T(8,128)(2,1)S(1)} %get-tuple-element.53), channel_id=1, source_target_pairs={{0,1},{1,0},{2,3},{3,2},{4,5},{5,4},{6,7},{7,6},{8,9},{9,8},{10,11... | collective-permute-start | bytes 786440 | tf_op jit(solution)/shard_map/ppermute | solution.py:273
  60.8 8.6 %collective-permute-start.9 = (f16[4,1,64,512]{3,2,1,0:T(8,128)(2,1)S(1)}, f16[4,1,64,512]{3,2,1,0:T(8,128)(2,1)S(1)}, u32[]{:S(2)}, u32[]{:S(2)}) collective-permute-start(f16[4,1,64,512]{3,2,1,0:T(8,128)(2,1)S(1)} %get-tuple-element.54), channel_id=1, source_target_pairs={{1,2},{2,1},{3,0},{0,3},{5,6},{6,5},{7,4},{4,7},{9,10},{10,9},{11,... | collective-permute-start | bytes 786440 | tf_op jit(solution)/shard_map/ppermute | solution.py:273
  69.3 7.1 %copy-start.4 = (bf16[2,3,2,64,128]{4,3,2,1,0:T(8,128)(2,1)S(1)}, bf16[2,3,2,64,128]{4,3,2,1,0:T(8,128)(2,1)}, u32[]{:S(2)}) copy-start(bf16[2,3,2,64,128]{4,3,2,1,0:T(8,128)(2,1)} %constant.41.clone.bands_ref) | copy-start | bytes 589828
  70.7 1.0 copy-start.2
  119.4 1.0 copy-start.3
  120.3 21.3 %all-to-all-start.2 = ((bf16[32,32,512]{2,1,0:T(8,128)(2,1)}), bf16[32,32,512]{2,1,0:T(8,128)(2,1)S(1)}, u32[]{:S(2)}, u32[]{:S(2)}) async-start(bf16[32,32,512]{2,1,0:T(8,128)(2,1)} %copy-done.3), calls=%async_computation.2 | async-start | bytes 2097152 | tf_op jit(solution)/shard_map/all_to_all | solution.py:284
